TPU v7x, 512 devices: a whole 4x8x8 slice. The times are simulated.
512 devices in a mesh: tm: 16 (over y, core), rows: 32 (over z, x).
Axes of the slice: x: 4, y: 8, z: 8, core: 2. Of those that a mesh axis runs over, the one named last changes fastest.
Arguments:
- latent: bfloat16 [32, 128, 16, 384], P('tm', 'rows'), may hold values from -6 to 6
- gain_first: float32 [384], replicated, may hold values from 0.5 to 2
- conv_first: bfloat16 [27, 384, 384], P(None, 'tm'), may hold values from -0.0625 to 0.0625
- bias_first: float32 [384], replicated, may hold values from -0.5 to 0.5
- conv_upper: bfloat16 [9, 384, 192], replicated, may hold values from -0.109375 to 0.109375
- bias_upper: float32 [192], replicated, may hold values from -0.5 to 0.5
Outputs:
- decoded: bfloat16 [32, 256, 6144], P('tm', 'rows')
All inputs are finite; a program needn't handle non-finite values.
Results may differ from a plain program's by a relative error of at most 0.0052.
Values may be sent and summed in bfloat16 or wider, within the bound.
No kernel may reach another device: no remote copies, remote signals or barrier semaphores. Data moves between devices by JAX's collectives and lax.ppermute only.
A program may use at most 64 MiB of HBM per device.

v0:
```python
import jax
import jax.numpy as jnp
from jax import lax
from jax.sharding import PartitionSpec as P


def from_behind(block, axis, distance):
    devices = range(lax.axis_size(axis))
    route = [(i - distance, i) for i in devices if i - distance in devices]
    return lax.ppermute(block, axis, route)


def padded_2(shard, sides, width):
    for axis, dim in sides:
        count, length = (lax.axis_size(axis), shard.shape[dim])
        up = [(i, (i + 1) % count) for i in range(count - 1)]
        down = [(j, i) for i, j in up]
        last = lax.slice_in_dim(shard, length - width, length, axis=dim)
        initial = lax.slice_in_dim(shard, 0, width, axis=dim)
        before = lax.ppermute(last, axis, up)
        after = lax.ppermute(initial, axis, down)
        shard = jnp.concatenate([before, shard, after], axis=dim)
    return shard


def scaled_silu(features, gain):
    values = features.astype(jnp.float32)
    mean_square = jnp.mean(values * values, axis=-1, keepdims=True)
    scaled = values * lax.rsqrt(mean_square + 1e-06) * gain
    return (scaled * jax.nn.sigmoid(scaled)).astype(jnp.bfloat16)


def tap_products(padded, weight_piece, frames, rows_out, width):
    count = weight_piece.shape[1]
    outputs = weight_piece.shape[2]
    cells = frames * rows_out * width
    running = jnp.zeros((cells, outputs), jnp.float32)
    for depth_tap in range(3):
        for row_tap in range(3):
            for col_tap in range(3):
                window = padded[
                    depth_tap : depth_tap + frames,
                    row_tap : row_tap + rows_out,
                    col_tap : col_tap + width,
                ]
                part = window.reshape(cells, count)
                running = running + jnp.dot(
                    part,
                    weight_piece[9 * depth_tap + 3 * row_tap + col_tap],
                    preferred_element_type=jnp.float32,
                )
    return running


def causal_conv(activated, kernel, bias):
    frames = activated.shape[0]
    rows_out = activated.shape[1] - 2
    width = activated.shape[2]
    previous = from_behind(activated, "tm", 1)
    stacked = jnp.concatenate([previous, activated], axis=0)
    padded = jnp.pad(stacked, ((0, 0), (0, 0), (1, 1), (0, 0)))
    outputs = kernel.shape[2]
    summed = tap_products(
        padded, lax.all_gather(kernel, "tm", axis=1, tiled=True), frames, rows_out, width
    )
    return (summed + bias).reshape(frames, rows_out, width, outputs)


def local(latent, gain_first, conv_first, bias_first, conv_upper, bias_upper):
    rows_dev = latent.shape[1]
    bordered = padded_2(latent, (("rows", 1),), 1)
    conv_out = causal_conv(scaled_silu(bordered, gain_first), conv_first, bias_first)
    block_out = (latent.astype(jnp.float32) + conv_out).astype(jnp.bfloat16)
    block_bordered = padded_2(block_out, (("rows", 1),), 1)
    frames = block_bordered.shape[0]
    width = block_bordered.shape[2]
    chans = block_bordered.shape[3]
    outputs = conv_upper.shape[2]
    widened = jnp.pad(block_bordered, ((0, 0), (0, 0), (1, 1), (0, 0)))
    larger = jnp.repeat(jnp.repeat(widened, 2, axis=1), 2, axis=2)
    window = larger[:, 1 : 2 * rows_dev + 3, 1 : 2 * width + 3]
    cells = frames * 2 * rows_dev * 2 * width
    result = jnp.zeros((cells, outputs), jnp.float32)
    for row_tap in range(3):
        for col_tap in range(3):
            piece = window[
                :, row_tap : row_tap + 2 * rows_dev, col_tap : col_tap + 2 * width
            ].reshape(cells, chans)
            result = result + jnp.dot(
                piece, conv_upper[3 * row_tap + col_tap], preferred_element_type=jnp.float32
            )
    result = (result + bias_upper).astype(jnp.bfloat16)
    return result.reshape(frames, 2 * rows_dev, 2 * width * outputs)


def solution(mesh):
    in_specs = (P("tm", "rows", None, None), P(), P(None, "tm", None), P(), P(), P())
    out_specs = P("tm", "rows", None)
    return jax.shard_map(local, mesh=mesh, in_specs=in_specs, out_specs=out_specs, check_vma=False)
```

profile of v0, /device:TPU:198, one launch (start us, length us, event | category | flops | bytes accessed | tf_op | source)
XLA Modules:
  0.0 113.7 jit_solution(2767410848244882762)
XLA Ops:
  6.5 0.7 all-gather.2.cloned.1.call-update
  7.3 0.8 fusion.40
  8.0 5.4 %collective-permute-start = (bf16[2,1,16,384]{3,2,1,0:T(8,128)(2,1)S(1)}, bf16[2,1,16,384]{3,2,1,0:T(8,128)(2,1)S(1)}, u32[]{:S(2)}, u32[]{:S(2)}) collective-permute-start(bf16[2,1,16,384]{3,2,1,0:T(8,128)(2,1)S(1)} %get-tuple-element.43), channel_id=1, source_target_pairs={{0,1},{1,2},{2,3},{3,4},{4,5},{5,6},{6,7},{7,8},{8,9},{9,10},{10,1... | collective-permute-start | bytes 73736 | tf_op jit(solution)/shard_map/ppermute | solution.py:20
  13.4 1.9 %collective-permute-start.1 = (bf16[2,1,16,384]{3,2,1,0:T(8,128)(2,1)S(1)}, bf16[2,1,16,384]{3,2,1,0:T(8,128)(2,1)S(1)}, u32[]{:S(2)}, u32[]{:S(2)}) collective-permute-start(bf16[2,1,16,384]{3,2,1,0:T(8,128)(2,1)S(1)} %get-tuple-element.44), channel_id=1, source_target_pairs={{1,0},{2,1},{3,2},{4,3},{5,4},{6,5},{7,6},{8,7},{9,8},{10,9},{11,1... | collective-permute-start | bytes 73736 | tf_op jit(solution)/shard_map/ppermute | solution.py:21
  15.4 7.1 %collective-permute-done.1 = bf16[2,1,16,384]{3,2,1,0:T(8,128)(2,1)S(1)} collective-permute-done((bf16[2,1,16,384]{3,2,1,0:T(8,128)(2,1)S(1)}, bf16[2,1,16,384]{3,2,1,0:T(8,128)(2,1)S(1)}, u32[]{:S(2)}, u32[]{:S(2)}) %collective-permute-start.1) | collective-permute-done | bytes 24608 | tf_op jit(solution)/shard_map/ppermute | solution.py:21
  22.5 1.0 fusion.5
  23.5 1.1 fusion.12
  24.6 1.3 %collective-permute-start.2 = (bf16[2,6,16,384]{3,2,1,0:T(8,128)(2,1)S(1)}, bf16[2,6,16,384]{3,2,1,0:T(8,128)(2,1)S(1)}, u32[]{:S(2)}, u32[]{:S(2)}) collective-permute-start(bf16[2,6,16,384]{3,2,1,0:T(8,128)(2,1)S(1)} %fusion.12), channel_id=1, source_target_pairs={{0,32},{32,64},{64,96},{96,128},{128,160},{160,192},{192,224},{224... | collective-permute-start | bytes 442376 | tf_op jit(solution)/shard_map/ppermute | solution.py:10
  25.9 1.0 collective-permute-done.2
  27.3 41.3 %all-gather.2.cloned.1.call-done = bf16[27,384,384]{2,1,0:T(8,128)(2,1)} async-done(((bf16[27,24,384]{2,1,0:T(8,128)(2,1)}), bf16[27,384,384]{2,1,0:T(8,128)(2,1)}) %all-gather.2.cloned.1.call-update) | async-done | bytes 7962640 | tf_op jit(solution)/shard_map/all_gather | solution.py:64
  68.6 1.3 %fusion.14 = f32[128,384]{1,0:T(8,128)S(1)} fusion(bf16[128,384]{1,0:T(8,128)(2,1)S(1)} %bitcast.212, bf16[27,384,384]{2,1,0:T(8,128)(2,1)} %all-gather.2.cloned.1.call-done), kind=kOutput, calls=%fused_computation.95 | convolution fusion | flops 37748736 | bytes 589824 | tf_op jit(solution)/shard_map/dot_general | solution.py:47
  69.9 1.5 %fusion.13 = f32[128,384]{1,0:T(8,128)S(1)} fusion(bf16[128,384]{1,0:T(8,128)(2,1)S(1)} %bitcast.211, bf16[27,384,384]{2,1,0:T(8,128)(2,1)} %all-gather.2.cloned.1.call-done), kind=kOutput, calls=%fused_computation.91 | convolution fusion | flops 37748736 | bytes 589824 | tf_op jit(solution)/shard_map/dot_general | solution.py:47
  71.4 1.2 %fusion.15 = f32[128,384]{1,0:T(8,128)S(1)} fusion(bf16[128,384]{1,0:T(8,128)(2,1)S(1)} %bitcast.210, bf16[27,384,384]{2,1,0:T(8,128)(2,1)} %all-gather.2.cloned.1.call-done), kind=kOutput, calls=%fused_computation.101 | convolution fusion | flops 37748736 | bytes 589824 | tf_op jit(solution)/shard_map/dot_general | solution.py:47
  72.6 1.2 %convolution_add_fusion.31 = f32[128,384]{1,0:T(8,128)S(1)} fusion(f32[128,384]{1,0:T(8,128)S(1)} %fusion.15, bf16[128,384]{1,0:T(8,128)(2,1)S(1)} %bitcast.219, bf16[27,384,384]{2,1,0:T(8,128)(2,1)} %all-gather.2.cloned.1.call-done), kind=kOutput, calls=%fused_computation.36 | convolution fusion | flops 37797888 | bytes 786432 | tf_op jit(solution)/shard_map/dot_general | solution.py:47
  73.8 1.2 %convolution_add_fusion.30 = f32[128,384]{1,0:T(8,128)S(1)} fusion(f32[128,384]{1,0:T(8,128)S(1)} %convolution_add_fusion.31, bf16[128,384]{1,0:T(8,128)(2,1)S(1)} %bitcast.209, bf16[27,384,384]{2,1,0:T(8,128)(2,1)} %all-gather.2.cloned.1.call-done), kind=kOutput, calls=%fused_computation.35 | convolution fusion | flops 37797888 | bytes 786432 | tf_op jit(solution)/shard_map/dot_general | solution.py:47
  74.9 1.2 %convolution_add_fusion.29 = f32[128,384]{1,0:T(8,128)S(1)} fusion(f32[128,384]{1,0:T(8,128)S(1)} %convolution_add_fusion.30, bf16[128,384]{1,0:T(8,128)(2,1)S(1)} %bitcast.208, bf16[27,384,384]{2,1,0:T(8,128)(2,1)} %all-gather.2.cloned.1.call-done), kind=kOutput, calls=%fused_computation.34 | convolution fusion | flops 37797888 | bytes 786432 | tf_op jit(solution)/shard_map/dot_general | solution.py:47
  76.1 1.2 %fusion.4 = f32[128,384]{1,0:T(8,128)S(1)} fusion(f32[128,384]{1,0:T(8,128)S(1)} %fusion.14, f32[128,384]{1,0:T(8,128)S(1)} %convolution_add_fusion.29, bf16[128,384]{1,0:T(8,128)(2,1)S(1)} %bitcast.221, bf16[27,384,384]{2,1,0:T(8,128)(2,1)} %all-gather.2.cloned.1.call-done), kind=kOutput, calls=%fused_computation.33 | convolution fusion | flops 37847040 | bytes 983040 | tf_op jit(solution)/shard_map/dot_general | solution.py:47
  77.3 1.2 %convolution_add_fusion.27 = f32[128,384]{1,0:T(8,128)S(1)} fusion(f32[128,384]{1,0:T(8,128)S(1)} %fusion.4, bf16[128,384]{1,0:T(8,128)(2,1)S(1)} %bitcast.207, bf16[27,384,384]{2,1,0:T(8,128)(2,1)} %all-gather.2.cloned.1.call-done), kind=kOutput, calls=%fused_computation.31 | convolution fusion | flops 37797888 | bytes 786432 | tf_op jit(solution)/shard_map/dot_general | solution.py:47
  78.5 1.2 %fusion.3 = f32[128,384]{1,0:T(8,128)S(1)} fusion(f32[128,384]{1,0:T(8,128)S(1)} %fusion.13, f32[128,384]{1,0:T(8,128)S(1)} %convolution_add_fusion.27, bf16[128,384]{1,0:T(8,128)(2,1)S(1)} %bitcast.220, bf16[27,384,384]{2,1,0:T(8,128)(2,1)} %all-gather.2.cloned.1.call-done), kind=kOutput, calls=%fused_computation.30 | convolution fusion | flops 37847040 | bytes 983040 | tf_op jit(solution)/shard_map/dot_general | solution.py:47
  79.7 1.2 %convolution_add_fusion.25 = f32[128,384]{1,0:T(8,128)S(1)} fusion(f32[128,384]{1,0:T(8,128)S(1)} %fusion.3, bf16[128,384]{1,0:T(8,128)(2,1)S(1)} %bitcast.206, bf16[27,384,384]{2,1,0:T(8,128)(2,1)} %all-gather.2.cloned.1.call-done), kind=kOutput, calls=%fused_computation.28 | convolution fusion | flops 37797888 | bytes 786432 | tf_op jit(solution)/shard_map/dot_general | solution.py:47
  80.9 1.2 %convolution_add_fusion.24 = f32[128,384]{1,0:T(8,128)S(1)} fusion(f32[128,384]{1,0:T(8,128)S(1)} %convolution_add_fusion.25, bf16[128,384]{1,0:T(8,128)(2,1)S(1)} %bitcast.218, bf16[27,384,384]{2,1,0:T(8,128)(2,1)} %all-gather.2.cloned.1.call-done), kind=kOutput, calls=%fused_computation.27 | convolution fusion | flops 37797888 | bytes 786432 | tf_op jit(solution)/shard_map/dot_general | solution.py:47
  85.7 4.2 %collective-permute-start.3 = (bf16[2,1,16,384]{3,2,1,0:T(8,128)(2,1)S(1)}, bf16[2,1,16,384]{3,2,1,0:T(8,128)(2,1)S(1)}, u32[]{:S(2)}, u32[]{:S(2)}) collective-permute-start(bf16[2,1,16,384]{3,2,1,0:T(8,128)(2,1)S(1)} %get-tuple-element.41), channel_id=1, source_target_pairs={{0,1},{1,2},{2,3},{3,4},{4,5},{5,6},{6,7},{7,8},{8,9},{9,10},{10,1... | collective-permute-start | bytes 73736 | tf_op jit(solution)/shard_map/ppermute | solution.py:20
  89.9 1.9 %collective-permute-start.4 = (bf16[2,1,16,384]{3,2,1,0:T(8,128)(2,1)S(1)}, bf16[2,1,16,384]{3,2,1,0:T(8,128)(2,1)S(1)}, u32[]{:S(2)}, u32[]{:S(2)}) collective-permute-start(bf16[2,1,16,384]{3,2,1,0:T(8,128)(2,1)S(1)} %get-tuple-element.42), channel_id=1, source_target_pairs={{1,0},{2,1},{3,2},{4,3},{5,4},{6,5},{7,6},{8,7},{9,8},{10,9},{11,1... | collective-permute-start | bytes 73736 | tf_op jit(solution)/shard_map/ppermute | solution.py:21
  91.8 7.1 %collective-permute-done.4 = bf16[2,1,16,384]{3,2,1,0:T(8,128)(2,1)S(1)} collective-permute-done((bf16[2,1,16,384]{3,2,1,0:T(8,128)(2,1)S(1)}, bf16[2,1,16,384]{3,2,1,0:T(8,128)(2,1)S(1)}, u32[]{:S(2)}, u32[]{:S(2)}) %collective-permute-start.4) | collective-permute-done | bytes 24608 | tf_op jit(solution)/shard_map/ppermute | solution.py:21
  99.4 0.3 broadcast_in_dim.5
  99.7 2.8 %fusion.38 = (bf16[2,8,32,384]{3,0,2,1:T(2,128)(2,1)S(1)}, bf16[2,8,32,384]{3,0,2,1:T(2,128)(2,1)S(1)}, bf16[2,8,32,384]{3,0,2,1:T(2,128)(2,1)S(1)}, bf16[2,8,32...) fusion(bf16[2,12,36,384]{3,0,2,1:T(2,128)(2,1)S(1)} %bitcast.183), kind=kLoop, calls=%fused_computation.128 | loop fusion | bytes 7077888 | tf_op jit(solution)/shard_map/slice | solution.py:86
  103.4 0.3 convolution_add_fusion.7
  104.0 0.3 convolution_add_fusion.5
  104.9 0.3 convolution_add_fusion.2
  105.2 0.3 convolution_add_fusion.1
  105.5 0.3 fusion.1
  106.0 0.9 reshape.170
  (53 shorter events, 6.0 us)
Async XLA Ops:
  6.5 62.1 %all-gather.2.cloned.1.call-start = ((), (), s32[]{:S(2)}) async-start(), calls=%async_computation | async-start | bytes 8460288 | tf_op jit(solution)/shard_map/all_gather | solution.py:64
  8.0 7.3 %collective-permute-start = (bf16[2,1,16,384]{3,2,1,0:T(8,128)(2,1)S(1)}, bf16[2,1,16,384]{3,2,1,0:T(8,128)(2,1)S(1)}, u32[]{:S(2)}, u32[]{:S(2)}) collective-permute-start(bf16[2,1,16,384]{3,2,1,0:T(8,128)(2,1)S(1)} %get-tuple-element.43), channel_id=1, source_target_pairs={{0,1},{1,2},{2,3},{3,4},{4,5},{5,6},{6,7},{7,8},{8,9},{9,10},{10,1... | collective-permute-start | bytes 73736 | tf_op jit(solution)/shard_map/ppermute | solution.py:20
  13.4 9.0 %collective-permute-start.1 = (bf16[2,1,16,384]{3,2,1,0:T(8,128)(2,1)S(1)}, bf16[2,1,16,384]{3,2,1,0:T(8,128)(2,1)S(1)}, u32[]{:S(2)}, u32[]{:S(2)}) collective-permute-start(bf16[2,1,16,384]{3,2,1,0:T(8,128)(2,1)S(1)} %get-tuple-element.44), channel_id=1, source_target_pairs={{1,0},{2,1},{3,2},{4,3},{5,4},{6,5},{7,6},{8,7},{9,8},{10,9},{11,1... | collective-permute-start | bytes 73736 | tf_op jit(solution)/shard_map/ppermute | solution.py:21
  24.6 2.3 %collective-permute-start.2 = (bf16[2,6,16,384]{3,2,1,0:T(8,128)(2,1)S(1)}, bf16[2,6,16,384]{3,2,1,0:T(8,128)(2,1)S(1)}, u32[]{:S(2)}, u32[]{:S(2)}) collective-permute-start(bf16[2,6,16,384]{3,2,1,0:T(8,128)(2,1)S(1)} %fusion.12), channel_id=1, source_target_pairs={{0,32},{32,64},{64,96},{96,128},{128,160},{160,192},{192,224},{224... | collective-permute-start | bytes 442376 | tf_op jit(solution)/shard_map/ppermute | solution.py:10
  68.6 13.5 %copy-start = (bf16[27,384,384]{2,1,0:T(8,128)(2,1)S(1)}, bf16[27,384,384]{2,1,0:T(8,128)(2,1)}, u32[]{:S(2)}) copy-start(bf16[27,384,384]{2,1,0:T(8,128)(2,1)} %all-gather.2.cloned.1.call-done) | copy-start | bytes 23887876
  76.1 9.3 %copy-start.3 = (f32[384]{0:T(512)S(1)}, f32[384]{0:T(512)}, u32[]{:S(2)}) copy-start(f32[384]{0:T(512)} %param.9) | copy-start | bytes 4612
  77.3 8.3 %copy-start.2 = (bf16[2,4,16,384]{3,2,1,0:T(8,128)(2,1)S(1)}, bf16[2,4,16,384]{3,2,1,0:T(8,128)(2,1)}, u32[]{:S(2)}) copy-start(bf16[2,4,16,384]{3,2,1,0:T(8,128)(2,1)} %param.6) | copy-start | bytes 294916
  85.7 6.2 %collective-permute-start.3 = (bf16[2,1,16,384]{3,2,1,0:T(8,128)(2,1)S(1)}, bf16[2,1,16,384]{3,2,1,0:T(8,128)(2,1)S(1)}, u32[]{:S(2)}, u32[]{:S(2)}) collective-permute-start(bf16[2,1,16,384]{3,2,1,0:T(8,128)(2,1)S(1)} %get-tuple-element.41), channel_id=1, source_target_pairs={{0,1},{1,2},{2,3},{3,4},{4,5},{5,6},{6,7},{7,8},{8,9},{9,10},{10,1... | collective-permute-start | bytes 73736 | tf_op jit(solution)/shard_map/ppermute | solution.py:20
  89.9 9.0 %collective-permute-start.4 = (bf16[2,1,16,384]{3,2,1,0:T(8,128)(2,1)S(1)}, bf16[2,1,16,384]{3,2,1,0:T(8,128)(2,1)S(1)}, u32[]{:S(2)}, u32[]{:S(2)}) collective-permute-start(bf16[2,1,16,384]{3,2,1,0:T(8,128)(2,1)S(1)} %get-tuple-element.42), channel_id=1, source_target_pairs={{1,0},{2,1},{3,2},{4,3},{5,4},{6,5},{7,6},{8,7},{9,8},{10,9},{11,1... | collective-permute-start | bytes 73736 | tf_op jit(solution)/shard_map/ppermute | solution.py:21
  99.1 4.0 %copy-start.1 = (bf16[9,384,192]{1,2,0:T(8,128)(2,1)S(1)}, bf16[9,384,192]{1,2,0:T(8,128)(2,1)}, u32[]{:S(2)}) copy-start(bf16[9,384,192]{1,2,0:T(8,128)(2,1)} %param.10) | copy-start | bytes 3981316
  102.7 2.8 %copy-start.4 = (f32[192]{0:T(256)S(1)}, f32[192]{0:T(256)}, u32[]{:S(2)}) copy-start(f32[192]{0:T(256)} %param.11) | copy-start | bytes 2308
Sparse Core Ops, SparseCore 0:
  9.4 59.1 all-gather.1
where the time goes:
time: 114 us
  waiting for transfers between devices  57.2 us (50%)
  matrix products  19.4 us (17%)
  starting transfers between devices  14.8 us (13%)
  between operations  14 us (12%)
  local copies, waits for them, and re-layouts  6.13 us (5%)
  other arithmetic  2.24 us (2%)
    all_gather x1, waiting for transfers between devices, causal_conv(): lax.all_gather(kernel, 'tm', axis=1, tiled=True)  41.3 us
    dot_general x27, matrix products, tap_products(): jnp.dot(part, weight_piece[9 * depth_tap + 3 * row_tap + col_tap], prefer...  16.7 us
    ppermute x2, waiting for transfers between devices, padded_2(): after = lax.ppermute(initial, axis, down)  14.2 us
    ppermute x2, starting transfers between devices, padded_2(): before = lax.ppermute(last, axis, up)  9.61 us
    ppermute x2, starting transfers between devices, padded_2(): after = lax.ppermute(initial, axis, down)  3.84 us
    slice x10, local copies, waits for them, and re-layouts, local(): window[:, row_tap:row_tap + 2 * rows_dev, col_tap:col_tap + 2 * width]  3.22 us
    dot_general x9, matrix products, local(): jnp.dot(piece, conv_upper[3 * row_tap + col_tap], preferred_element_type=...  2.67 us
  transfers between devices with their start and end apart: 6, of which 4 were waited for; matrix products, arithmetic and copies ran while one was open for 3% of the time, Pallas kernels for 0%

commit v1 on v0

v1 whole, which is shorter than its diff:
```python
import jax
import jax.numpy as jnp
import numpy as np
from jax import lax
from jax.experimental import pallas as pl
from jax.experimental.pallas import tpu as pltpu
from jax.sharding import Mesh
from jax.sharding import PartitionSpec as P

F32 = jnp.float32
BF16 = jnp.bfloat16
FRAMES, ROWS, COLS, CHANS, OUTS = 2, 4, 16, 384, 192
LINE = 8
PART = CHANS // LINE
CELLS = FRAMES * ROWS * COLS
BORDERED = FRAMES * (ROWS + 2) * COLS
NT_DIMS = (((1,), (1,)), ((), ()))
TN_DIMS = (((0,), (0,)), ((), ()))
PARAMS = pltpu.CompilerParams(vmem_limit_bytes=40 * 1024 * 1024)


def window_picks():
    picks = np.zeros((3, BORDERED, 9, FRAMES, ROWS, COLS), np.float32)
    for dy in range(3):
        for dx in range(3):
            for r in range(ROWS):
                for c in range(COLS):
                    col = c + dx - 1
                    if 0 <= col < COLS:
                        for f in range(FRAMES):
                            cell = f * (ROWS + 2) * COLS + (r + dy) * COLS + col
                            picks[0, cell, 3 * dy + dx, f, r, c] = 1
                            picks[1 if f == 0 else 2, cell, 3 * dy + dx, 1 - f, r, c] = 1
    return picks.reshape(3, BORDERED, 9 * CELLS)


def row_picks():
    picks = np.zeros((3, COLS, FRAMES, 2 * ROWS, FRAMES, ROWS + 2, COLS), np.float32)
    for dy in range(3):
        for i in range(2 * ROWS):
            row = (i + dy - 1) // 2 + 1
            for f in range(FRAMES):
                for c in range(COLS):
                    picks[dy, c, f, i, f, row, c] = 1
    return picks.reshape(3 * COLS * FRAMES * 2 * ROWS, BORDERED)


def act_kernel(up_ref, lat_ref, down_ref, gain_ref, out_ref):
    pieces = []
    for f in range(FRAMES):
        pieces += [up_ref[f], lat_ref[f].reshape(ROWS * COLS, CHANS), down_ref[f]]
    values = jnp.concatenate(pieces, axis=0).astype(F32)
    mean_square = jnp.mean(values * values, axis=-1, keepdims=True)
    scaled = values * lax.rsqrt(mean_square + 1e-06) * gain_ref[...]
    act = (scaled / (1.0 + jnp.exp(-scaled))).astype(BF16)
    row = lax.broadcasted_iota(jnp.int32, (CHANS, CHANS), 0)
    col = lax.broadcasted_iota(jnp.int32, (CHANS, CHANS), 1)
    eye = jnp.where(row == col, 1.0, 0.0).astype(BF16)
    flipped = lax.dot_general(eye, act, NT_DIMS, preferred_element_type=F32)
    out_ref[...] = flipped.astype(BF16).reshape(LINE, PART, BORDERED)


def conv_kernel(core_ref, act_ref, weight_ref, pick_ref, out_ref, before, windows):
    core = core_ref[0]

    @pl.when(core == 1)
    def _():
        before[...] = act_ref[0]

    @pl.when(core == 0)
    def _():
        before[0] = jnp.zeros_like(before[0])
        before[1:] = act_ref[1, : LINE - 1]

    here = act_ref[core].reshape(LINE * PART, BORDERED)
    prior = before[...].reshape(LINE * PART, BORDERED)

    def picked(block, which):
        return jnp.dot(block, pick_ref[which], preferred_element_type=F32)

    for dt in range(3):
        if dt == 0:
            taken = picked(prior, 0)
        elif dt == 1:
            taken = picked(here, 1) + picked(prior, 2)
        else:
            taken = picked(here, 0)
        taken = taken.astype(BF16)
        for tap in range(9):
            for y in range(LINE):
                windows[
                    (9 * dt + tap) * PART : (9 * dt + tap + 1) * PART, y * CELLS : (y + 1) * CELLS
                ] = taken[y * PART : (y + 1) * PART, tap * CELLS : (tap + 1) * CELLS]
    weight = weight_ref[...].reshape(27 * PART, CHANS)
    sums = lax.dot_general(weight, windows[...], TN_DIMS, preferred_element_type=F32)
    for y in range(LINE):
        out_ref[y] = sums[:, y * CELLS : (y + 1) * CELLS].astype(BF16)


def block_kernel(part_ref, lat_ref, bias_ref, out_ref):
    total = part_ref[0].astype(F32)
    for y in range(1, LINE):
        total = total + part_ref[y].astype(F32)
    conv_out = total.T + bias_ref[...]
    block = (lat_ref[...].reshape(CELLS, CHANS).astype(F32) + conv_out).astype(BF16)
    out_ref[...] = block.reshape(FRAMES, ROWS, COLS, CHANS)


def upper_kernel(up_ref, block_ref, down_ref, weight_ref, bias_ref, pick_ref, out_ref):
    pieces = []
    for f in range(FRAMES):
        pieces += [up_ref[f], block_ref[f].reshape(ROWS * COLS, CHANS), down_ref[f]]
    bordered = jnp.concatenate(pieces, axis=0)
    rows = jnp.dot(pick_ref[...], bordered, preferred_element_type=F32).astype(BF16)
    cells = COLS * FRAMES * 2 * ROWS
    total = jnp.zeros((cells, 6 * OUTS), F32)
    for dy in range(3):
        weight = weight_ref[3 * dy : 3 * dy + 3].reshape(6 * OUTS, CHANS)
        total = total + lax.dot_general(
            rows[dy * cells : (dy + 1) * cells], weight, NT_DIMS, preferred_element_type=F32
        )
    wide = 2 * OUTS
    lines = FRAMES * 2 * ROWS
    total = total.reshape(COLS, lines, 3 * wide)
    left = lax.broadcasted_iota(jnp.int32, (lines, wide), 1) < OUTS
    zero = jnp.zeros((lines, wide), F32)
    for c in range(COLS):
        first = total[c, :, :wide]
        first_before = total[c - 1, :, :wide] if c else zero
        last = total[c, :, 2 * wide :]
        last_after = total[c + 1, :, 2 * wide :] if c < COLS - 1 else zero
        value = (
            jnp.where(left, first_before, first)
            + total[c, :, wide : 2 * wide]
            + jnp.where(left, last, last_after)
            + bias_ref[...]
        )
        out_ref[:, c * wide : (c + 1) * wide] = value.astype(BF16)


def row_neighbours(block):
    axes = ("z", "x")
    count = lax.axis_size(axes)
    down = [(i, i + 1) for i in range(count - 1)]
    up = [(i + 1, i) for i in range(count - 1)]
    above = lax.ppermute(block[:, ROWS - 1], axes, down)
    below = lax.ppermute(block[:, 0], axes, up)
    return above, below


def call(kernel, shape, **kwargs):
    return pl.pallas_call(
        kernel, out_shape=jax.ShapeDtypeStruct(shape, BF16), compiler_params=PARAMS, **kwargs
    )


def local(latent, gain_first, conv_first, bias_first, conv_upper, bias_upper):
    above, below = row_neighbours(latent)
    weight = lax.all_gather(conv_first, "core", axis=1, tiled=True)
    upper = jnp.swapaxes(conv_upper, 1, 2)
    upper = jnp.concatenate([upper, upper], axis=1)
    upper_bias = jnp.tile(bias_upper, 2)[None]
    acts = call(act_kernel, (LINE, PART, BORDERED))(above, latent, below, gain_first[None])
    acts = lax.all_to_all(acts, "y", 0, 0, tiled=True)
    acts = lax.all_gather(acts, "core", axis=0, tiled=False)
    core = lax.axis_index("core").astype(jnp.int32)[None]
    vmem = pl.BlockSpec(memory_space=pltpu.VMEM)
    parts = call(
        conv_kernel,
        (LINE, CHANS, CELLS),
        in_specs=[pl.BlockSpec(memory_space=pltpu.SMEM), vmem, vmem, vmem],
        out_specs=vmem,
        scratch_shapes=[
            pltpu.VMEM((LINE, PART, BORDERED), BF16),
            pltpu.VMEM((27 * PART, LINE * CELLS), BF16),
        ],
    )(core, acts, weight, jnp.asarray(window_picks(), BF16))
    parts = lax.all_to_all(parts, "y", 0, 0, tiled=True)
    block = call(block_kernel, (FRAMES, ROWS, COLS, CHANS))(parts, latent, bias_first[None])
    above, below = row_neighbours(block)
    out = call(upper_kernel, (FRAMES * 2 * ROWS, 2 * COLS * OUTS))(
        above, block, below, upper, upper_bias, jnp.asarray(row_picks(), BF16)
    )
    return out.reshape(FRAMES, 2 * ROWS, 2 * COLS * OUTS)


def solution(mesh):
    fine = Mesh(mesh.devices.reshape(8, 2, 8, 4), ("y", "core", "z", "x"))
    tm, rows = ("y", "core"), ("z", "x")
    in_specs = (P(tm, rows, None, None), P(), P(None, tm, None), P(), P(), P())
    return jax.shard_map(
        local, mesh=fine, in_specs=in_specs, out_specs=P(tm, rows, None), check_vma=False
    )
```

time: 114 us -> 79 us (0.69)
  the two profiles are of different devices: /device:TPU:198 before, /device:TPU:256 now
where the time goes in v1:
time: 79 us; the launch traced here: 78.5 us
  waiting for transfers between devices  39.9 us (51%)
  starting transfers between devices  22.3 us (28%)
  Pallas kernels  6.81 us (9%)
  blocking collectives  4.79 us (6%)
  local copies, waits for them, and re-layouts  2.56 us (3%)
  other arithmetic  2.07 us (3%)
    all_to_all x1, waiting for transfers between devices, local(): parts = lax.all_to_all(parts, 'y', 0, 0, tiled=True)  23.6 us
    ppermute x2, waiting for transfers between devices, row_neighbours(): above = lax.ppermute(block[:, ROWS - 1], axes, down)  9.18 us
    all_to_all x1, starting transfers between devices, local(): acts = lax.all_to_all(acts, 'y', 0, 0, tiled=True)  7.1 us
    all_to_all x1, waiting for transfers between devices, local(): acts = lax.all_to_all(acts, 'y', 0, 0, tiled=True)  7.06 us
    ppermute x2, starting transfers between devices, row_neighbours(): above = lax.ppermute(block[:, ROWS - 1], axes, down)  6.01 us
    ppermute x2, starting transfers between devices, row_neighbours(): below = lax.ppermute(block[:, 0], axes, up)  5.67 us
    all_to_all x1, starting transfers between devices, local(): parts = lax.all_to_all(parts, 'y', 0, 0, tiled=True)  3.55 us
    pallas_call x1, Pallas kernels, local(): call(conv_kernel, (LINE, CHANS, CELLS), in_specs=[pl.BlockSpec(memory_spa...  3.47 us
  transfers between devices with their start and end apart: 6, of which 4 were waited for; matrix products, arithmetic and copies ran while one was open for 4% of the time, Pallas kernels for 0%

profile of v1, /device:TPU:256, one launch (start us, length us, event | category | flops | bytes accessed | tf_op | source)
XLA Modules:
  0.0 78.5 jit_solution(4909541626668497840)
XLA Ops:
  0.0 0.0 copy-start
  0.0 0.9 %slice_bitcast_fusion.2 = (bf16[2,16,384]{2,1,0:T(8,128)(2,1)S(1)}, bf16[2,16,384]{2,1,0:T(8,128)(2,1)S(1)}) fusion(bf16[2,4,16,384]{3,2,1,0:T(8,128)(2,1)} %lat_ref.3), kind=kLoop, calls=%fused_computation.3 | loop fusion | bytes 98304 | tf_op jit(solution)/shard_map/squeeze | solution.py:147
  0.9 3.7 %collective-permute-start.1 = (bf16[2,16,384]{2,1,0:T(8,128)(2,1)S(1)}, bf16[2,16,384]{2,1,0:T(8,128)(2,1)S(1)}, u32[]{:S(2)}, u32[]{:S(2)}) collective-permute-start(bf16[2,16,384]{2,1,0:T(8,128)(2,1)S(1)} %get-tuple-element.7), channel_id=1, source_target_pairs={{1,0},{2,1},{3,2},{4,3},{5,4},{6,5},{7,6},{8,7},{9,8},{10,9},{11,1... | collective-permute-start | bytes 73736 | tf_op jit(solution)/shard_map/ppermute | solution.py:147
  4.6 2.1 %collective-permute-start = (bf16[2,16,384]{2,1,0:T(8,128)(2,1)S(1)}, bf16[2,16,384]{2,1,0:T(8,128)(2,1)S(1)}, u32[]{:S(2)}, u32[]{:S(2)}) collective-permute-start(bf16[2,16,384]{2,1,0:T(8,128)(2,1)S(1)} %get-tuple-element.8), channel_id=1, source_target_pairs={{0,1},{1,2},{2,3},{3,4},{4,5},{5,6},{6,7},{7,8},{8,9},{9,10},{10,1... | collective-permute-start | bytes 73736 | tf_op jit(solution)/shard_map/ppermute | solution.py:146
  6.7 0.7 broadcast_in_dim.10.gain_ref
  7.4 0.0 collective-permute-done.1.down_ref
  7.4 6.3 %collective-permute-done.up_ref = bf16[2,16,384]{2,1,0:T(8,128)(2,1)S(1)} collective-permute-done((bf16[2,16,384]{2,1,0:T(8,128)(2,1)S(1)}, bf16[2,16,384]{2,1,0:T(8,128)(2,1)S(1)}, u32[]{:S(2)}, u32[]{:S(2)}) %collective-permute-start) | collective-permute-done | bytes 24608 | tf_op jit(solution)/shard_map/ppermute | solution.py:146
  13.7 0.0 copy-start.1
  13.7 0.9 %copy-done.1 = bf16[2,4,16,384]{3,2,1,0:T(8,128)(2,1)S(1)} copy-done((bf16[2,4,16,384]{3,2,1,0:T(8,128)(2,1)S(1)}, bf16[2,4,16,384]{3,2,1,0:T(8,128)(2,1)}, u32[]{:S(2)}) %copy-start.1) | copy-done | bytes 98328
  14.6 1.1 %shard_map.82 = bf16[8,48,192]{2,1,0:T(8,128)(2,1)} custom-call(bf16[2,16,384]{2,1,0:T(8,128)(2,1)S(1)} %collective-permute-done.up_ref, bf16[2,4,16,384]{3,2,1,0:T(8,128)(2,1)S(1)} %copy-done.1, bf16[2,16,384]{2,1,0:T(8,128)(2,1)S(1)} %collective-permute-done.1.down_ref, f32[1,384]{1,0:T(1,128)S(1)} %broadcast_in_dim.10.gain_ref), custom_call_target="tpu_custom_call" | custom-call | tf_op jit(solution)/shard_map/pallas_call | solution.py:163
  15.7 7.1 %all-to-all-start = ((bf16[8,48,192]{2,1,0:T(8,128)(2,1)}), bf16[8,48,192]{2,1,0:T(8,128)(2,1)S(1)}, u32[]{:S(2)}, u32[]{:S(2)}) async-start(bf16[8,48,192]{2,1,0:T(8,128)(2,1)} %shard_map.82), calls=%async_computation | async-start | bytes 393216 | tf_op jit(solution)/shard_map/all_to_all | solution.py:164
  22.8 2.7 %all_gather.11.weight_ref = bf16[27,48,384]{2,1,0:T(8,128)(2,1)S(1)} all-gather(bf16[27,24,384]{2,1,0:T(8,128)(2,1)} %param.10), channel_id=1, replica_groups=mesh['y'=8,'core'=2,'z'=8,'x'=4] {'core'}, dimensions={1}, use_global_device_ids=true | all-gather | bytes 1492992 | tf_op jit(solution)/shard_map/all_gather | solution.py:159
  25.5 7.1 %all-to-all-done = bf16[8,48,192]{2,1,0:T(8,128)(2,1)S(1)} async-done(((bf16[8,48,192]{2,1,0:T(8,128)(2,1)}), bf16[8,48,192]{2,1,0:T(8,128)(2,1)S(1)}, u32[]{:S(2)}, u32[]{:S(2)}) %all-to-all-start) | async-done | bytes 147488 | tf_op jit(solution)/shard_map/all_to_all | solution.py:164
  32.5 2.1 %all-gather = bf16[16,48,192]{2,1,0:T(8,128)(2,1)S(1)} all-gather(bf16[8,48,192]{2,1,0:T(8,128)(2,1)S(1)} %all-to-all-done), channel_id=2, replica_groups=mesh['y'=8,'core'=2,'z'=8,'x'=4] {'core'}, dimensions={0}, use_global_device_ids=true | all-gather | bytes 442368 | tf_op jit(solution)/shard_map/all_gather | solution.py:165
  34.6 0.0 copy-done
  34.6 3.5 %shard_map.83 = bf16[8,384,128]{2,1,0:T(8,128)(2,1)} custom-call(s32[1]{0:T(128)} %bitcast.core_ref, bf16[2,8,48,192]{3,2,1,0:T(8,128)(2,1)S(1)} %bitcast.20, bf16[27,48,384]{2,1,0:T(8,128)(2,1)S(1)} %all_gather.11.weight_ref, bf16[3,192,1152]{2,1,0:T(8,128)(2,1)S(1)} %copy-done), custom_call_target="tpu_custom_call" | custom-call | tf_op jit(solution)/shard_map/pallas_call | solution.py:168
  38.1 3.5 %all-to-all-start.1 = ((bf16[8,384,128]{2,1,0:T(8,128)(2,1)}), bf16[8,384,128]{2,1,0:T(8,128)(2,1)S(1)}, u32[]{:S(2)}, u32[]{:S(2)}) async-start(bf16[8,384,128]{2,1,0:T(8,128)(2,1)} %shard_map.83), calls=%async_computation.1 | async-start | bytes 1572864 | tf_op jit(solution)/shard_map/all_to_all | solution.py:178
  41.6 0.0 copy-done.4
  41.7 0.0 copy-start.5
  41.7 0.0 copy-start.3
  41.7 23.6 %all-to-all-done.1.part_ref = bf16[8,384,128]{2,1,0:T(8,128)(2,1)S(1)} async-done(((bf16[8,384,128]{2,1,0:T(8,128)(2,1)}), bf16[8,384,128]{2,1,0:T(8,128)(2,1)S(1)}, u32[]{:S(2)}, u32[]{:S(2)}) %all-to-all-start.1) | async-done | bytes 786464 | tf_op jit(solution)/shard_map/all_to_all | solution.py:178
  65.3 0.0 copy-done.2
  65.3 0.2 shard_map.84.block_ref
  65.5 1.9 %collective-permute-start.3 = (bf16[2,16,384]{2,1,0:T(8,128)(2,1)S(1)}, bf16[2,16,384]{2,1,0:T(8,128)(2,1)S(1)}, u32[]{:S(2)}, u32[]{:S(2)}) collective-permute-start(bf16[2,16,384]{2,1,0:T(8,128)(2,1)S(1)} %get-tuple-element.5), channel_id=1, source_target_pairs={{1,0},{2,1},{3,2},{4,3},{5,4},{6,5},{7,6},{8,7},{9,8},{10,9},{11,1... | collective-permute-start | bytes 73736 | tf_op jit(solution)/shard_map/ppermute | solution.py:147
  67.4 3.9 %collective-permute-start.2 = (bf16[2,16,384]{2,1,0:T(8,128)(2,1)S(1)}, bf16[2,16,384]{2,1,0:T(8,128)(2,1)S(1)}, u32[]{:S(2)}, u32[]{:S(2)}) collective-permute-start(bf16[2,16,384]{2,1,0:T(8,128)(2,1)S(1)} %get-tuple-element.6), channel_id=1, source_target_pairs={{0,1},{1,2},{2,3},{3,4},{4,5},{5,6},{6,7},{7,8},{8,9},{9,10},{10,1... | collective-permute-start | bytes 73736 | tf_op jit(solution)/shard_map/ppermute | solution.py:146
  71.4 2.1 %pad_maximum_fusion.weight_ref = bf16[9,384,384]{2,1,0:T(8,128)(2,1)S(1)} fusion(bf16[9,192,384]{2,1,0:T(8,128)(2,1)} %bitcast.21), kind=kLoop, calls=%fused_computation | loop fusion | flops 5308416 | bytes 3981312 | tf_op jit(solution)/shard_map/concatenate | solution.py:161
  73.4 0.0 copy-done.5
  73.5 0.1 broadcast_in_dim_tile.3.bias_ref
  73.5 0.0 collective-permute-done.3.down_ref
  73.5 2.9 %collective-permute-done.2.up_ref = bf16[2,16,384]{2,1,0:T(8,128)(2,1)S(1)} collective-permute-done((bf16[2,16,384]{2,1,0:T(8,128)(2,1)S(1)}, bf16[2,16,384]{2,1,0:T(8,128)(2,1)S(1)}, u32[]{:S(2)}, u32[]{:S(2)}) %collective-permute-start.2) | collective-permute-done | bytes 24608 | tf_op jit(solution)/shard_map/ppermute | solution.py:146
  76.5 0.0 copy-done.3
  76.5 2.1 %shard_map.85 = bf16[16,6144]{1,0:T(8,128)(2,1)} custom-call(bf16[2,16,384]{2,1,0:T(8,128)(2,1)S(1)} %collective-permute-done.2.up_ref, bf16[2,4,16,384]{3,2,1,0:T(8,128)(2,1)S(1)} %shard_map.84.block_ref, bf16[2,16,384]{2,1,0:T(8,128)(2,1)S(1)} %collective-permute-done.3.down_ref, bf16[9,384,384]{2,1,0:T(8,128)(2,1)S(1)} %pad_maximum_fusion.weight_ref, ...), custom_call_target="tpu_custom_call" | custom-call | tf_op jit(solution)/shard_map/pallas_call | solution.py:181
  (5 shorter events, 0.0 us)
Async XLA Ops:
  0.0 34.6 %copy-start = (bf16[3,192,1152]{2,1,0:T(8,128)(2,1)S(1)}, bf16[3,192,1152]{2,1,0:T(8,128)(2,1)}, u32[]{:S(2)}) copy-start(bf16[3,192,1152]{2,1,0:T(8,128)(2,1)} %constant.10.clone.pick_ref) | copy-start | bytes 3981316
  0.9 6.5 %collective-permute-start.1 = (bf16[2,16,384]{2,1,0:T(8,128)(2,1)S(1)}, bf16[2,16,384]{2,1,0:T(8,128)(2,1)S(1)}, u32[]{:S(2)}, u32[]{:S(2)}) collective-permute-start(bf16[2,16,384]{2,1,0:T(8,128)(2,1)S(1)} %get-tuple-element.7), channel_id=1, source_target_pairs={{1,0},{2,1},{3,2},{4,3},{5,4},{6,5},{7,6},{8,7},{9,8},{10,9},{11,1... | collective-permute-start | bytes 73736 | tf_op jit(solution)/shard_map/ppermute | solution.py:147
  4.6 9.0 %collective-permute-start = (bf16[2,16,384]{2,1,0:T(8,128)(2,1)S(1)}, bf16[2,16,384]{2,1,0:T(8,128)(2,1)S(1)}, u32[]{:S(2)}, u32[]{:S(2)}) collective-permute-start(bf16[2,16,384]{2,1,0:T(8,128)(2,1)S(1)} %get-tuple-element.8), channel_id=1, source_target_pairs={{0,1},{1,2},{2,3},{3,4},{4,5},{5,6},{6,7},{7,8},{8,9},{9,10},{10,1... | collective-permute-start | bytes 73736 | tf_op jit(solution)/shard_map/ppermute | solution.py:146
  13.7 0.9 %copy-start.1 = (bf16[2,4,16,384]{3,2,1,0:T(8,128)(2,1)S(1)}, bf16[2,4,16,384]{3,2,1,0:T(8,128)(2,1)}, u32[]{:S(2)}) copy-start(bf16[2,4,16,384]{3,2,1,0:T(8,128)(2,1)} %lat_ref.3) | copy-start | bytes 294916
  15.7 16.9 %all-to-all-start = ((bf16[8,48,192]{2,1,0:T(8,128)(2,1)}), bf16[8,48,192]{2,1,0:T(8,128)(2,1)S(1)}, u32[]{:S(2)}, u32[]{:S(2)}) async-start(bf16[8,48,192]{2,1,0:T(8,128)(2,1)} %shard_map.82), calls=%async_computation | async-start | bytes 393216 | tf_op jit(solution)/shard_map/all_to_all | solution.py:164
  34.6 7.0 %copy-start.4 = (f32[384]{0:T(512)S(1)}, f32[384]{0:T(512)}, u32[]{:S(2)}) copy-start(f32[384]{0:T(512)} %param.11) | copy-start | bytes 4612
  34.6 30.7 %copy-start.2 = (bf16[2,4,16,384]{3,2,1,0:T(8,128)(2,1)S(1)}, bf16[2,4,16,384]{3,2,1,0:T(8,128)(2,1)}, u32[]{:S(2)}) copy-start(bf16[2,4,16,384]{3,2,1,0:T(8,128)(2,1)} %lat_ref.3) | copy-start | bytes 294916
  38.1 27.2 %all-to-all-start.1 = ((bf16[8,384,128]{2,1,0:T(8,128)(2,1)}), bf16[8,384,128]{2,1,0:T(8,128)(2,1)S(1)}, u32[]{:S(2)}, u32[]{:S(2)}) async-start(bf16[8,384,128]{2,1,0:T(8,128)(2,1)} %shard_map.83), calls=%async_computation.1 | async-start | bytes 1572864 | tf_op jit(solution)/shard_map/all_to_all | solution.py:178
  41.7 31.8 %copy-start.5 = (f32[192]{0:T(256)S(1)}, f32[192]{0:T(256)}, u32[]{:S(2)}) copy-start(f32[192]{0:T(256)} %param.13) | copy-start | bytes 2308
  41.7 34.8 %copy-start.3 = (bf16[768,192]{1,0:T(8,128)(2,1)S(1)}, bf16[768,192]{1,0:T(8,128)(2,1)}, u32[]{:S(2)}) copy-start(bf16[768,192]{1,0:T(8,128)(2,1)} %constant.11.clone.pick_ref) | copy-start | bytes 884740
  65.5 8.0 %collective-permute-start.3 = (bf16[2,16,384]{2,1,0:T(8,128)(2,1)S(1)}, bf16[2,16,384]{2,1,0:T(8,128)(2,1)S(1)}, u32[]{:S(2)}, u32[]{:S(2)}) collective-permute-start(bf16[2,16,384]{2,1,0:T(8,128)(2,1)S(1)} %get-tuple-element.5), channel_id=1, source_target_pairs={{1,0},{2,1},{3,2},{4,3},{5,4},{6,5},{7,6},{8,7},{9,8},{10,9},{11,1... | collective-permute-start | bytes 73736 | tf_op jit(solution)/shard_map/ppermute | solution.py:147
  67.4 9.0 %collective-permute-start.2 = (bf16[2,16,384]{2,1,0:T(8,128)(2,1)S(1)}, bf16[2,16,384]{2,1,0:T(8,128)(2,1)S(1)}, u32[]{:S(2)}, u32[]{:S(2)}) collective-permute-start(bf16[2,16,384]{2,1,0:T(8,128)(2,1)S(1)} %get-tuple-element.6), channel_id=1, source_target_pairs={{0,1},{1,2},{2,3},{3,4},{4,5},{5,6},{6,7},{7,8},{8,9},{9,10},{10,1... | collective-permute-start | bytes 73736 | tf_op jit(solution)/shard_map/ppermute | solution.py:146

commit v2 on v1

--- a/solution.py
+++ b/solution.py
@@ -12,7 +12,10 @@
 FRAMES, ROWS, COLS, CHANS, OUTS = 2, 4, 16, 384, 192
 LINE = 8
 PART = CHANS // LINE
-CELLS = FRAMES * ROWS * COLS
+PAIRS = LINE // 2
+HALF = ROWS // 2
+CELLS = FRAMES * HALF * COLS
+SENT = FRAMES * (HALF + 2) * COLS
 BORDERED = FRAMES * (ROWS + 2) * COLS
 NT_DIMS = (((1,), (1,)), ((), ()))
 TN_DIMS = (((0,), (0,)), ((), ()))
@@ -20,18 +23,20 @@
 
 
 def window_picks():
-    picks = np.zeros((3, BORDERED, 9, FRAMES, ROWS, COLS), np.float32)
+    picks = np.zeros((3, 2, FRAMES, HALF + 2, COLS, 9, 2, FRAMES, HALF, COLS), np.float32)
     for dy in range(3):
         for dx in range(3):
-            for r in range(ROWS):
+            for r in range(HALF):
                 for c in range(COLS):
                     col = c + dx - 1
                     if 0 <= col < COLS:
-                        for f in range(FRAMES):
-                            cell = f * (ROWS + 2) * COLS + (r + dy) * COLS + col
-                            picks[0, cell, 3 * dy + dx, f, r, c] = 1
-                            picks[1 if f == 0 else 2, cell, 3 * dy + dx, 1 - f, r, c] = 1
-    return picks.reshape(3, BORDERED, 9 * CELLS)
+                        for p in range(2):
+                            for f in range(FRAMES):
+                                tap = 3 * dy + dx
+                                picks[0, p, f, r + dy, col, tap, p, f, r, c] = 1
+                                which = 1 if f == 0 else 2
+                                picks[which, p, f, r + dy, col, tap, p, 1 - f, r, c] = 1
+    return picks.reshape(3, 2 * SENT, 9 * 2 * CELLS)
 
 
 def row_picks():
@@ -51,59 +56,92 @@
         pieces += [up_ref[f], lat_ref[f].reshape(ROWS * COLS, CHANS), down_ref[f]]
     values = jnp.concatenate(pieces, axis=0).astype(F32)
     mean_square = jnp.mean(values * values, axis=-1, keepdims=True)
-    scaled = values * lax.rsqrt(mean_square + 1e-06) * gain_ref[...]
+    scaled = values * lax.rsqrt(mean_square + 1e-06) * gain_ref[...].reshape(1, CHANS)
     act = (scaled / (1.0 + jnp.exp(-scaled))).astype(BF16)
     row = lax.broadcasted_iota(jnp.int32, (CHANS, CHANS), 0)
     col = lax.broadcasted_iota(jnp.int32, (CHANS, CHANS), 1)
     eye = jnp.where(row == col, 1.0, 0.0).astype(BF16)
-    flipped = lax.dot_general(eye, act, NT_DIMS, preferred_element_type=F32)
-    out_ref[...] = flipped.astype(BF16).reshape(LINE, PART, BORDERED)
-
-
-def conv_kernel(core_ref, act_ref, weight_ref, pick_ref, out_ref, before, windows):
-    core = core_ref[0]
-
-    @pl.when(core == 1)
-    def _():
-        before[...] = act_ref[0]
-
-    @pl.when(core == 0)
-    def _():
-        before[0] = jnp.zeros_like(before[0])
-        before[1:] = act_ref[1, : LINE - 1]
-
-    here = act_ref[core].reshape(LINE * PART, BORDERED)
-    prior = before[...].reshape(LINE * PART, BORDERED)
+    for half in range(2):
+        cells = []
+        for f in range(FRAMES):
+            start = (f * (ROWS + 2) + half * HALF) * COLS
+            cells.append(act[start : start + (HALF + 2) * COLS])
+        flipped = lax.dot_general(
+            eye, jnp.concatenate(cells, axis=0), NT_DIMS, preferred_element_type=F32
+        )
+        flipped = flipped.astype(BF16).reshape(PAIRS, 2 * PART, SENT)
+        for pair in range(PAIRS):
+            out_ref[2 * pair + half] = flipped[pair]
+
+
+def conv_kernel(
+    place_ref, act_ref, own_ref, other_ref, pick_ref, out_ref, here, before, windows
+):
+    core, half = place_ref[0], place_ref[1]
+    for y in range(LINE):
+        where = (y // 2, slice(None), slice((y % 2) * SENT, (y % 2 + 1) * SENT))
+        here[where] = act_ref[core, y]
+
+        @pl.when(core == 1)
+        def _():
+            before[where] = act_ref[0, y]
+
+        @pl.when(core == 0)
+        def _():
+            before[where] = act_ref[1, y - 1] if y else jnp.zeros_like(act_ref[1, 0])
+
+    now = here[...].reshape(PAIRS * 2 * PART, 2 * SENT)
+    prior = before[...].reshape(PAIRS * 2 * PART, 2 * SENT)
 
     def picked(block, which):
         return jnp.dot(block, pick_ref[which], preferred_element_type=F32)
 
+    lanes = 2 * CELLS
     for dt in range(3):
         if dt == 0:
             taken = picked(prior, 0)
         elif dt == 1:
-            taken = picked(here, 1) + picked(prior, 2)
+            taken = picked(now, 1) + picked(prior, 2)
         else:
-            taken = picked(here, 0)
+            taken = picked(now, 0)
         taken = taken.astype(BF16)
         for tap in range(9):
-            for y in range(LINE):
-                windows[
-                    (9 * dt + tap) * PART : (9 * dt + tap + 1) * PART, y * CELLS : (y + 1) * CELLS
-                ] = taken[y * PART : (y + 1) * PART, tap * CELLS : (tap + 1) * CELLS]
-    weight = weight_ref[...].reshape(27 * PART, CHANS)
-    sums = lax.dot_general(weight, windows[...], TN_DIMS, preferred_element_type=F32)
-    for y in range(LINE):
-        out_ref[y] = sums[:, y * CELLS : (y + 1) * CELLS].astype(BF16)
+            for pair in range(PAIRS):
+                for part in range(2):
+                    row = (2 * pair + part) * PART
+                    windows[
+                        part,
+                        (9 * dt + tap) * PART : (9 * dt + tap + 1) * PART,
+                        pair * lanes : (pair + 1) * lanes,
+                    ] = taken[row : row + PART, tap * lanes : (tap + 1) * lanes]
+    sums = lax.dot_general(
+        windows[half],
+        own_ref[...].reshape(27 * PART, CHANS),
+        TN_DIMS,
+        preferred_element_type=F32,
+    )
+    sums = sums + lax.dot_general(
+        windows[1 - half],
+        other_ref[...].reshape(27 * PART, CHANS),
+        TN_DIMS,
+        preferred_element_type=F32,
+    )
+    out_ref[...] = sums.astype(BF16).reshape(LINE, CELLS, CHANS)
 
 
 def block_kernel(part_ref, lat_ref, bias_ref, out_ref):
-    total = part_ref[0].astype(F32)
-    for y in range(1, LINE):
-        total = total + part_ref[y].astype(F32)
-    conv_out = total.T + bias_ref[...]
-    block = (lat_ref[...].reshape(CELLS, CHANS).astype(F32) + conv_out).astype(BF16)
-    out_ref[...] = block.reshape(FRAMES, ROWS, COLS, CHANS)
+    bias = bias_ref[...].reshape(1, CHANS)
+    for half in range(2):
+        total = part_ref[half].astype(F32)
+        for y in range(half + 2, LINE, 2):
+            total = total + part_ref[y].astype(F32)
+        total = total + bias
+        size = HALF * COLS
+        for f in range(FRAMES):
+            rows = slice(half * HALF, (half + 1) * HALF)
+            skip = lat_ref[f, rows].reshape(size, CHANS).astype(F32)
+            value = (skip + total[f * size : (f + 1) * size]).astype(BF16)
+            out_ref[f, rows] = value.reshape(HALF, COLS, CHANS)
 
 
 def upper_kernel(up_ref, block_ref, down_ref, weight_ref, bias_ref, pick_ref, out_ref):
@@ -155,28 +193,34 @@
 
 
 def local(latent, gain_first, conv_first, bias_first, conv_upper, bias_upper):
+    other = lax.ppermute(conv_first, "y", [(i, i ^ 1) for i in range(LINE)])
     above, below = row_neighbours(latent)
-    weight = lax.all_gather(conv_first, "core", axis=1, tiled=True)
+    own = lax.all_gather(conv_first, "core", axis=1, tiled=True)
+    other = lax.all_gather(other, "core", axis=1, tiled=True)
     upper = jnp.swapaxes(conv_upper, 1, 2)
     upper = jnp.concatenate([upper, upper], axis=1)
     upper_bias = jnp.tile(bias_upper, 2)[None]
-    acts = call(act_kernel, (LINE, PART, BORDERED))(above, latent, below, gain_first[None])
+    acts = call(act_kernel, (LINE, 2 * PART, SENT))(above, latent, below, gain_first)
     acts = lax.all_to_all(acts, "y", 0, 0, tiled=True)
+    acts, own, other, upper, upper_bias = lax.optimization_barrier(
+        (acts, own, other, upper, upper_bias)
+    )
     acts = lax.all_gather(acts, "core", axis=0, tiled=False)
-    core = lax.axis_index("core").astype(jnp.int32)[None]
+    place = jnp.stack([lax.axis_index("core"), lax.axis_index("y") % 2]).astype(jnp.int32)
     vmem = pl.BlockSpec(memory_space=pltpu.VMEM)
     parts = call(
         conv_kernel,
-        (LINE, CHANS, CELLS),
-        in_specs=[pl.BlockSpec(memory_space=pltpu.SMEM), vmem, vmem, vmem],
+        (LINE, CELLS, CHANS),
+        in_specs=[pl.BlockSpec(memory_space=pltpu.SMEM), vmem, vmem, vmem, vmem],
         out_specs=vmem,
         scratch_shapes=[
-            pltpu.VMEM((LINE, PART, BORDERED), BF16),
-            pltpu.VMEM((27 * PART, LINE * CELLS), BF16),
+            pltpu.VMEM((PAIRS, 2 * PART, 2 * SENT), BF16),
+            pltpu.VMEM((PAIRS, 2 * PART, 2 * SENT), BF16),
+            pltpu.VMEM((2, 27 * PART, LINE * CELLS), BF16),
         ],
-    )(core, acts, weight, jnp.asarray(window_picks(), BF16))
+    )(place, acts, own, other, jnp.asarray(window_picks(), BF16))
     parts = lax.all_to_all(parts, "y", 0, 0, tiled=True)
-    block = call(block_kernel, (FRAMES, ROWS, COLS, CHANS))(parts, latent, bias_first[None])
+    block = call(block_kernel, (FRAMES, ROWS, COLS, CHANS))(parts, latent, bias_first)
     above, below = row_neighbours(block)
     out = call(upper_kernel, (FRAMES * 2 * ROWS, 2 * COLS * OUTS))(
         above, block, below, upper, upper_bias, jnp.asarray(row_picks(), BF16)

time: 79 us -> 82.5 us (1.044)
  waiting for transfers between devices: 39.9 us -> 15.4 us
  blocking collectives: 4.79 us -> 27.6 us
  starting transfers between devices: 22.3 us -> 24.7 us
  local copies, waits for them, and re-layouts: 2.56 us -> 4.77 us
    all_to_all x1 -> x0, waiting for transfers between devices: 23.6 us -> none  [local(): parts = lax.all_to_all(parts, 'y', 0, 0, tiled=True)]
    all_to_all x0 -> x1, blocking collectives: none -> 17.7 us  [local(): parts = lax.all_to_all(parts, 'y', 0, 0, tiled=True)]
    ppermute x2, starting transfers between devices: 5.67 us -> 10.8 us  [row_neighbours(): below = lax.ppermute(block[:, 0], axes, up)]
    all_gather x1 -> x2, blocking collectives: 2.72 us -> 7.85 us  [the longest x1 5.21 us: local(): own = lax.all_gather(conv_first, 'core', axis=1, tiled=True)]
    all_to_all x1 -> x0, starting transfers between devices: 3.55 us -> none  [local(): parts = lax.all_to_all(parts, 'y', 0, 0, tiled=True)]
    ppermute x0 -> x1, starting transfers between devices: none -> 3.49 us  [local(): other = lax.ppermute(conv_first, 'y', [(i, i ^ 1) for i in range(LINE)])]
    unnamed x12 -> x16, local copies, waits for them, and re-layouts: 0.92 us -> 3.91 us
    ppermute x2, waiting for transfers between devices: 9.18 us -> 7.1 us  [row_neighbours(): above = lax.ppermute(block[:, ROWS - 1], axes, down)]
  transfers between devices with their start and end apart: 6 -> 6, of which waited for: 4 -> 2; matrix products, arithmetic and copies ran while one was open for 4% -> 3% of each run, Pallas kernels for 0% -> 1%
where the time goes in v2:
time: 82.5 us; the launch traced here: 81.8 us
  blocking collectives  27.6 us (33%)
  starting transfers between devices  24.7 us (30%)
  waiting for transfers between devices  15.4 us (19%)
  Pallas kernels  7.03 us (9%)
  local copies, waits for them, and re-layouts  4.77 us (6%)
  other arithmetic  2.24 us (3%)
    all_to_all x1, blocking collectives, local(): parts = lax.all_to_all(parts, 'y', 0, 0, tiled=True)  17.7 us
    ppermute x2, starting transfers between devices, row_neighbours(): below = lax.ppermute(block[:, 0], axes, up)  10.8 us
    all_to_all x1, waiting for transfers between devices, local(): acts = lax.all_to_all(acts, 'y', 0, 0, tiled=True)  8.28 us
    ppermute x2, waiting for transfers between devices, row_neighbours(): above = lax.ppermute(block[:, ROWS - 1], axes, down)  7.1 us
    all_to_all x1, starting transfers between devices, local(): acts = lax.all_to_all(acts, 'y', 0, 0, tiled=True)  6.22 us
    all_gather x1, blocking collectives, local(): own = lax.all_gather(conv_first, 'core', axis=1, tiled=True)  5.21 us
    ppermute x2, starting transfers between devices, row_neighbours(): above = lax.ppermute(block[:, ROWS - 1], axes, down)  4.14 us
    unnamed x16, local copies, waits for them, and re-layouts  3.91 us
  transfers between devices with their start and end apart: 6, of which 2 were waited for; matrix products, arithmetic and copies ran while one was open for 3% of the time, Pallas kernels for 1%

profile of v2, /device:TPU:256, one launch (start us, length us, event | category | flops | bytes accessed | tf_op | source)
XLA Modules:
  0.0 81.8 jit_solution(18079247229488100662)
XLA Ops:
  0.0 0.8 slice_bitcast_fusion.2
  0.8 3.7 %collective-permute-start.1 = (bf16[2,16,384]{2,1,0:T(8,128)(2,1)S(1)}, bf16[2,16,384]{2,1,0:T(8,128)(2,1)S(1)}, u32[]{:S(2)}, u32[]{:S(2)}) collective-permute-start(bf16[2,16,384]{2,1,0:T(8,128)(2,1)S(1)} %get-tuple-element.17), channel_id=1, source_target_pairs={{1,0},{2,1},{3,2},{4,3},{5,4},{6,5},{7,6},{8,7},{9,8},{10,9},{11,1... | collective-permute-start | bytes 73736 | tf_op jit(solution)/shard_map/ppermute | solution.py:185
  4.5 0.0 copy-start.7
  4.5 0.0 copy-start.3
  4.5 0.0 copy-start.5
  4.6 2.2 %collective-permute-start = (bf16[2,16,384]{2,1,0:T(8,128)(2,1)S(1)}, bf16[2,16,384]{2,1,0:T(8,128)(2,1)S(1)}, u32[]{:S(2)}, u32[]{:S(2)}) collective-permute-start(bf16[2,16,384]{2,1,0:T(8,128)(2,1)S(1)} %get-tuple-element.18), channel_id=1, source_target_pairs={{0,1},{1,2},{2,3},{3,4},{4,5},{5,6},{6,7},{7,8},{8,9},{9,10},{10,1... | collective-permute-start | bytes 73736 | tf_op jit(solution)/shard_map/ppermute | solution.py:184
  6.8 3.5 %collective-permute-start.2 = (bf16[27,24,384]{2,1,0:T(8,128)(2,1)}, bf16[27,24,384]{2,1,0:T(8,128)(2,1)S(1)}, u32[]{:S(2)}, u32[]{:S(2)}) collective-permute-start(bf16[27,24,384]{2,1,0:T(8,128)(2,1)} %param.10), channel_id=1, source_target_pairs={{0,64},{64,0},{128,192},{192,128},{256,320},{320,256},{384,448},{4... | collective-permute-start | bytes 1493000 | tf_op jit(solution)/shard_map/ppermute | solution.py:196
  10.3 5.2 %all_gather.12.own_ref = bf16[27,48,384]{2,1,0:T(8,128)(2,1)} all-gather(bf16[27,24,384]{2,1,0:T(8,128)(2,1)} %param.10), channel_id=1, replica_groups=mesh['y'=8,'core'=2,'z'=8,'x'=4] {'core'}, dimensions={1}, use_global_device_ids=true | all-gather | bytes 1492992 | tf_op jit(solution)/shard_map/all_gather | solution.py:198
  15.5 2.2 %pad_maximum_fusion.weight_ref = bf16[9,384,384]{2,1,0:T(8,128)(2,1)S(1)} fusion(bf16[9,192,384]{2,1,0:T(8,128)(2,1)} %bitcast.22), kind=kLoop, calls=%fused_computation | loop fusion | flops 5308416 | bytes 3981312 | tf_op jit(solution)/shard_map/concatenate | solution.py:201
  17.7 0.0 copy-done.7
  17.7 0.1 broadcast_in_dim_tile.3.bias_ref
  17.8 0.0 collective-permute-done.1.down_ref
  17.8 0.0 collective-permute-done.up_ref
  17.8 0.0 copy-done.3
  17.8 1.1 %shard_map.82 = bf16[8,96,128]{2,1,0:T(8,128)(2,1)} custom-call(bf16[2,16,384]{2,1,0:T(8,128)(2,1)S(1)} %collective-permute-done.up_ref, bf16[2,4,16,384]{3,2,1,0:T(8,128)(2,1)S(1)} %copy-done.3, bf16[2,16,384]{2,1,0:T(8,128)(2,1)S(1)} %collective-permute-done.1.down_ref, f32[384]{0:T(512)S(1)} %copy-done.5), custom_call_target="tpu_custom_call" | custom-call | tf_op jit(solution)/shard_map/pallas_call | solution.py:203
  18.9 6.2 %all-to-all-start = ((bf16[8,96,128]{2,1,0:T(8,128)(2,1)}), bf16[8,96,128]{2,1,0:T(8,128)(2,1)S(1)}, u32[]{:S(2)}, u32[]{:S(2)}) async-start(bf16[8,96,128]{2,1,0:T(8,128)(2,1)} %shard_map.82), calls=%async_computation | async-start | bytes 393216 | tf_op jit(solution)/shard_map/all_to_all | solution.py:204
  25.2 0.1 pad_add_fusion.place_ref
  25.2 0.0 collective-permute-done.2
  25.2 2.6 %all_gather.13.other_ref = bf16[27,48,384]{2,1,0:T(8,128)(2,1)} all-gather(bf16[27,24,384]{2,1,0:T(8,128)(2,1)S(1)} %collective-permute-done.2), channel_id=1, replica_groups=mesh['y'=8,'core'=2,'z'=8,'x'=4] {'core'}, dimensions={1}, use_global_device_ids=true | all-gather | bytes 1492992 | tf_op jit(solution)/shard_map/all_gather | solution.py:199
  27.9 8.3 %all-to-all-done = bf16[8,96,128]{2,1,0:T(8,128)(2,1)S(1)} async-done(((bf16[8,96,128]{2,1,0:T(8,128)(2,1)}), bf16[8,96,128]{2,1,0:T(8,128)(2,1)S(1)}, u32[]{:S(2)}, u32[]{:S(2)}) %all-to-all-start) | async-done | bytes 196640 | tf_op jit(solution)/shard_map/all_to_all | solution.py:204
  36.2 2.1 %all-gather = bf16[16,96,128]{2,1,0:T(8,128)(2,1)S(1)} all-gather(bf16[8,96,128]{2,1,0:T(8,128)(2,1)S(1)} %all-to-all-done), channel_id=2, replica_groups=mesh['y'=8,'core'=2,'z'=8,'x'=4] {'core'}, dimensions={0}, use_global_device_ids=true | all-gather | bytes 589824 | tf_op jit(solution)/shard_map/all_gather | solution.py:208
  38.2 1.2 %copy-done = bf16[27,48,384]{2,1,0:T(8,128)(2,1)S(1)} copy-done((bf16[27,48,384]{2,1,0:T(8,128)(2,1)S(1)}, bf16[27,48,384]{2,1,0:T(8,128)(2,1)}, u32[]{:S(2)}) %copy-start) | copy-done | bytes 995352
  39.4 1.2 %copy-done.1 = bf16[27,48,384]{2,1,0:T(8,128)(2,1)S(1)} copy-done((bf16[27,48,384]{2,1,0:T(8,128)(2,1)S(1)}, bf16[27,48,384]{2,1,0:T(8,128)(2,1)}, u32[]{:S(2)}) %copy-start.1) | copy-done | bytes 995352
  40.6 1.5 %copy-done.2 = bf16[3,256,1152]{2,1,0:T(8,128)(2,1)S(1)} copy-done((bf16[3,256,1152]{2,1,0:T(8,128)(2,1)S(1)}, bf16[3,256,1152]{2,1,0:T(8,128)(2,1)}, u32[]{:S(2)}) %copy-start.2) | copy-done | bytes 1769496
  42.1 3.8 %shard_map.83 = bf16[8,64,384]{2,1,0:T(8,128)(2,1)S(1)} custom-call(s32[2]{0:T(128)S(1)} %pad_add_fusion.place_ref, bf16[2,8,96,128]{3,2,1,0:T(8,128)(2,1)S(1)} %bitcast.21, bf16[27,48,384]{2,1,0:T(8,128)(2,1)S(1)} %copy-done, bf16[27,48,384]{2,1,0:T(8,128)(2,1)S(1)} %copy-done.1, bf16[3,256,1152]{2,1,0:T(8,128)(2,1)S(1)} %copy-done.2), custom_call_target="tpu_custom_call" | custom-call | tf_op jit(solution)/shard_map/pallas_call | solution.py:211
  45.9 17.7 %all_to_all.10.part_ref = bf16[8,64,384]{2,1,0:T(8,128)(2,1)S(1)} all-to-all(bf16[8,64,384]{2,1,0:T(8,128)(2,1)S(1)} %shard_map.83), channel_id=1, replica_groups=mesh['y'=8,'core'=2,'z'=8,'x'=4] {'y'}, dimensions={0} | all-to-all | bytes 786432 | tf_op jit(solution)/shard_map/all_to_all | solution.py:222
  63.5 0.1 shard_map.84.block_ref
  63.6 7.1 %collective-permute-start.4 = (bf16[2,16,384]{2,1,0:T(8,128)(2,1)S(1)}, bf16[2,16,384]{2,1,0:T(8,128)(2,1)S(1)}, u32[]{:S(2)}, u32[]{:S(2)}) collective-permute-start(bf16[2,16,384]{2,1,0:T(8,128)(2,1)S(1)} %get-tuple-element.15), channel_id=1, source_target_pairs={{1,0},{2,1},{3,2},{4,3},{5,4},{6,5},{7,6},{8,7},{9,8},{10,9},{11,1... | collective-permute-start | bytes 73736 | tf_op jit(solution)/shard_map/ppermute | solution.py:185
  70.7 1.9 %collective-permute-start.3 = (bf16[2,16,384]{2,1,0:T(8,128)(2,1)S(1)}, bf16[2,16,384]{2,1,0:T(8,128)(2,1)S(1)}, u32[]{:S(2)}, u32[]{:S(2)}) collective-permute-start(bf16[2,16,384]{2,1,0:T(8,128)(2,1)S(1)} %get-tuple-element.16), channel_id=1, source_target_pairs={{0,1},{1,2},{2,3},{3,4},{4,5},{5,6},{6,7},{7,8},{8,9},{9,10},{10,1... | collective-permute-start | bytes 73736 | tf_op jit(solution)/shard_map/ppermute | solution.py:184
  72.6 0.0 collective-permute-done.4.down_ref
  72.7 7.1 %collective-permute-done.3.up_ref = bf16[2,16,384]{2,1,0:T(8,128)(2,1)S(1)} collective-permute-done((bf16[2,16,384]{2,1,0:T(8,128)(2,1)S(1)}, bf16[2,16,384]{2,1,0:T(8,128)(2,1)S(1)}, u32[]{:S(2)}, u32[]{:S(2)}) %collective-permute-start.3) | collective-permute-done | bytes 24608 | tf_op jit(solution)/shard_map/ppermute | solution.py:184
  79.8 2.1 %shard_map.85 = bf16[16,6144]{1,0:T(8,128)(2,1)} custom-call(bf16[2,16,384]{2,1,0:T(8,128)(2,1)S(1)} %collective-permute-done.3.up_ref, bf16[2,4,16,384]{3,2,1,0:T(8,128)(2,1)S(1)} %shard_map.84.block_ref, bf16[2,16,384]{2,1,0:T(8,128)(2,1)S(1)} %collective-permute-done.4.down_ref, bf16[9,384,384]{2,1,0:T(8,128)(2,1)S(1)} %pad_maximum_fusion.weight_ref, ...), custom_call_target="tpu_custom_call" | custom-call | tf_op jit(solution)/shard_map/pallas_call | solution.py:225
  (10 shorter events, 0.0 us)
Async XLA Ops:
  0.8 17.0 %collective-permute-start.1 = (bf16[2,16,384]{2,1,0:T(8,128)(2,1)S(1)}, bf16[2,16,384]{2,1,0:T(8,128)(2,1)S(1)}, u32[]{:S(2)}, u32[]{:S(2)}) collective-permute-start(bf16[2,16,384]{2,1,0:T(8,128)(2,1)S(1)} %get-tuple-element.17), channel_id=1, source_target_pairs={{1,0},{2,1},{3,2},{4,3},{5,4},{6,5},{7,6},{8,7},{9,8},{10,9},{11,1... | collective-permute-start | bytes 73736 | tf_op jit(solution)/shard_map/ppermute | solution.py:185
  4.5 13.2 %copy-start.7 = (f32[192]{0:T(256)S(1)}, f32[192]{0:T(256)}, u32[]{:S(2)}) copy-start(f32[192]{0:T(256)} %param.13) | copy-start | bytes 2308
  4.5 13.3 %copy-start.3 = (bf16[2,4,16,384]{3,2,1,0:T(8,128)(2,1)S(1)}, bf16[2,4,16,384]{3,2,1,0:T(8,128)(2,1)}, u32[]{:S(2)}) copy-start(bf16[2,4,16,384]{3,2,1,0:T(8,128)(2,1)} %lat_ref.3) | copy-start | bytes 294916
  4.5 13.2 %copy-start.5 = (f32[384]{0:T(512)S(1)}, f32[384]{0:T(512)}, u32[]{:S(2)}) copy-start(f32[384]{0:T(512)} %gain_ref.1) | copy-start | bytes 4612
  4.6 13.2 %collective-permute-start = (bf16[2,16,384]{2,1,0:T(8,128)(2,1)S(1)}, bf16[2,16,384]{2,1,0:T(8,128)(2,1)S(1)}, u32[]{:S(2)}, u32[]{:S(2)}) collective-permute-start(bf16[2,16,384]{2,1,0:T(8,128)(2,1)S(1)} %get-tuple-element.18), channel_id=1, source_target_pairs={{0,1},{1,2},{2,3},{3,4},{4,5},{5,6},{6,7},{7,8},{8,9},{9,10},{10,1... | collective-permute-start | bytes 73736 | tf_op jit(solution)/shard_map/ppermute | solution.py:184
  6.8 18.5 %collective-permute-start.2 = (bf16[27,24,384]{2,1,0:T(8,128)(2,1)}, bf16[27,24,384]{2,1,0:T(8,128)(2,1)S(1)}, u32[]{:S(2)}, u32[]{:S(2)}) collective-permute-start(bf16[27,24,384]{2,1,0:T(8,128)(2,1)} %param.10), channel_id=1, source_target_pairs={{0,64},{64,0},{128,192},{192,128},{256,320},{320,256},{384,448},{4... | collective-permute-start | bytes 1493000 | tf_op jit(solution)/shard_map/ppermute | solution.py:196
  18.9 17.2 %all-to-all-start = ((bf16[8,96,128]{2,1,0:T(8,128)(2,1)}), bf16[8,96,128]{2,1,0:T(8,128)(2,1)S(1)}, u32[]{:S(2)}, u32[]{:S(2)}) async-start(bf16[8,96,128]{2,1,0:T(8,128)(2,1)} %shard_map.82), calls=%async_computation | async-start | bytes 393216 | tf_op jit(solution)/shard_map/all_to_all | solution.py:204
  38.2 1.2 %copy-start = (bf16[27,48,384]{2,1,0:T(8,128)(2,1)S(1)}, bf16[27,48,384]{2,1,0:T(8,128)(2,1)}, u32[]{:S(2)}) copy-start(bf16[27,48,384]{2,1,0:T(8,128)(2,1)} %all_gather.12.own_ref) | copy-start | bytes 2985988
  39.4 1.2 %copy-start.1 = (bf16[27,48,384]{2,1,0:T(8,128)(2,1)S(1)}, bf16[27,48,384]{2,1,0:T(8,128)(2,1)}, u32[]{:S(2)}) copy-start(bf16[27,48,384]{2,1,0:T(8,128)(2,1)} %all_gather.13.other_ref) | copy-start | bytes 2985988
  40.6 1.5 %copy-start.2 = (bf16[3,256,1152]{2,1,0:T(8,128)(2,1)S(1)}, bf16[3,256,1152]{2,1,0:T(8,128)(2,1)}, u32[]{:S(2)}) copy-start(bf16[3,256,1152]{2,1,0:T(8,128)(2,1)} %constant.29.clone.pick_ref) | copy-start | bytes 5308420
  42.1 21.4 %copy-start.6 = (f32[384]{0:T(512)S(1)}, f32[384]{0:T(512)}, u32[]{:S(2)}) copy-start(f32[384]{0:T(512)} %bias_ref.1) | copy-start | bytes 4612
  42.1 37.6 %copy-start.4 = (bf16[768,192]{1,0:T(8,128)(2,1)S(1)}, bf16[768,192]{1,0:T(8,128)(2,1)}, u32[]{:S(2)}) copy-start(bf16[768,192]{1,0:T(8,128)(2,1)} %constant.30.clone.pick_ref) | copy-start | bytes 884740
  63.6 9.0 %collective-permute-start.4 = (bf16[2,16,384]{2,1,0:T(8,128)(2,1)S(1)}, bf16[2,16,384]{2,1,0:T(8,128)(2,1)S(1)}, u32[]{:S(2)}, u32[]{:S(2)}) collective-permute-start(bf16[2,16,384]{2,1,0:T(8,128)(2,1)S(1)} %get-tuple-element.15), channel_id=1, source_target_pairs={{1,0},{2,1},{3,2},{4,3},{5,4},{6,5},{7,6},{8,7},{9,8},{10,9},{11,1... | collective-permute-start | bytes 73736 | tf_op jit(solution)/shard_map/ppermute | solution.py:185
  70.7 9.0 %collective-permute-start.3 = (bf16[2,16,384]{2,1,0:T(8,128)(2,1)S(1)}, bf16[2,16,384]{2,1,0:T(8,128)(2,1)S(1)}, u32[]{:S(2)}, u32[]{:S(2)}) collective-permute-start(bf16[2,16,384]{2,1,0:T(8,128)(2,1)S(1)} %get-tuple-element.16), channel_id=1, source_target_pairs={{0,1},{1,2},{2,3},{3,4},{4,5},{5,6},{6,7},{7,8},{8,9},{9,10},{10,1... | collective-permute-start | bytes 73736 | tf_op jit(solution)/shard_map/ppermute | solution.py:184

commit v3 on v2

v3 whole, which is shorter than its diff:
```python
import jax
import jax.numpy as jnp
from jax import lax
from jax.experimental import pallas as pl
from jax.experimental.pallas import tpu as pltpu
from jax.sharding import Mesh
from jax.sharding import PartitionSpec as P

F32 = jnp.float32
BF16 = jnp.bfloat16
FRAMES, ROWS, COLS, CHANS, OUTS = 2, 4, 16, 384, 192
LINE = 8
PART = CHANS // LINE
PAIRS = LINE // 2
HALF = ROWS // 2
CELLS = FRAMES * HALF * COLS
SENT = FRAMES * ROWS * COLS
EDGE = LINE * FRAMES * COLS
BORDERED = FRAMES * (ROWS + 2) * COLS
NT_DIMS = (((1,), (1,)), ((), ()))
TN_DIMS = (((0,), (0,)), ((), ()))


def one_hot(wanted, there):
    return jnp.where(wanted == there, 1.0, 0.0).astype(BF16)


def window_picks(half):
    lane = lax.broadcasted_iota(jnp.int32, (1, 18 * CELLS), 1)
    tap, frame, row, col = lane >> 7, (lane >> 5) & 3, (lane >> 4) & 1, lane & 15
    dy = (tap * 11) >> 5
    col = col + tap - 3 * dy - 1
    row = row + dy - 1 + 2 * half
    wanted = (frame << 6) + (row << 4) + col
    inside = (col >= 0) & (col < COLS) & (row >= 0) & (row < ROWS)
    wanted = jnp.where(inside, wanted, -1)
    return one_hot(wanted, lax.broadcasted_iota(jnp.int32, (2 * SENT, 18 * CELLS), 0))


def edge_picks(shift):
    lane = lax.broadcasted_iota(jnp.int32, (1, 3 * EDGE), 1)
    col = (lane & 15) + (lane >> 8) - 1
    wanted = (((lane >> 4) & 15) << 4) + col - shift
    wanted = jnp.where((col >= 0) & (col < COLS), wanted, -1)
    return one_hot(wanted, lax.broadcasted_iota(jnp.int32, (EDGE, 3 * EDGE), 0))


def row_picks():
    shape = (6 * ROWS * COLS * FRAMES, BORDERED)
    place = lax.broadcasted_iota(jnp.int32, (shape[0], 1), 0)
    dy, col, frame, i = place >> 8, (place >> 4) & 15, (place >> 3) & 1, place & 7
    wanted = frame * ((ROWS + 2) * COLS) + (((i + dy + 1) >> 1) << 4) + col
    return one_hot(wanted, lax.broadcasted_iota(jnp.int32, shape, 1))


def scaled_silu(block, gain):
    values = block.astype(F32)
    mean_square = jnp.mean(values * values, axis=-1, keepdims=True)
    scaled = values * lax.rsqrt(mean_square + 1e-06) * gain
    return (scaled / (1.0 + jnp.exp(-scaled))).astype(BF16)


def act_kernel(lat_ref, gain_ref, out_ref, lat, gain, arrived):
    copies = [
        pltpu.make_async_copy(lat_ref, lat, arrived.at[0]),
        pltpu.make_async_copy(gain_ref, gain, arrived.at[1]),
    ]
    for copy in copies:
        copy.start()
    row = lax.broadcasted_iota(jnp.int32, (CHANS, CHANS), 0)
    col = lax.broadcasted_iota(jnp.int32, (CHANS, CHANS), 1)
    eye = one_hot(row, col)
    for copy in copies:
        copy.wait()
    act = scaled_silu(lat[...].reshape(SENT, CHANS), gain[...].reshape(1, CHANS))
    flipped = lax.dot_general(eye, act, NT_DIMS, preferred_element_type=F32).astype(BF16)
    for y in range(LINE):
        start = (y // 2) * 2 * PART
        out_ref[y] = flipped[start : start + 2 * PART]


def pack_kernel(act_ref, out_ref):
    row = (ROWS - 1) * (1 - (lax.axis_index("y") & 1))
    lane = lax.broadcasted_iota(jnp.int32, (1, SENT), 1)
    wanted = ((lane >> 4) << 6) + (row << 4) + (lane & 15)
    picks = one_hot(wanted, lax.broadcasted_iota(jnp.int32, (4 * SENT, SENT), 0))
    for core in range(2):
        for group in range(2):
            block = jnp.concatenate([act_ref[core, 4 * group + k] for k in range(4)], axis=1)
            packed = jnp.dot(block, picks, preferred_element_type=F32)
            out_ref[core, group] = packed.astype(BF16)


def weight_dots(blocks, weights, half):
    total = None
    for i in range(2):
        rows = blocks.shape[1]
        part = lax.dot_general(
            blocks[half if i == 0 else 1 - half],
            weights[i].reshape(rows, CHANS),
            TN_DIMS,
            preferred_element_type=F32,
        )
        total = part if total is None else total + part
    return total


def inner_kernel(act_ref, own_ref, other_ref, out_ref, here, before, windows, weights, arrived):
    core, half = lax.axis_index("core"), lax.axis_index("y") & 1
    copies = [
        pltpu.make_async_copy(ref, weights.at[i], arrived.at[i])
        for i, ref in enumerate((own_ref, other_ref))
    ]
    for copy in copies:
        copy.start()
    for y in range(LINE):
        where = (y // 2, slice(None), slice((y % 2) * SENT, (y % 2 + 1) * SENT))
        here[where] = act_ref[core, y]

        @pl.when(core == 1)
        def _():
            before[where] = act_ref[0, y]

        @pl.when(core == 0)
        def _():
            before[where] = act_ref[1, y - 1] if y else jnp.zeros_like(act_ref[1, 0])

    now = here[...].reshape(PAIRS * 2 * PART, 2 * SENT)
    prior = before[...].reshape(PAIRS * 2 * PART, 2 * SENT)
    picks = window_picks(half)
    earliest = jnp.dot(prior, picks, preferred_element_type=F32)
    latest = jnp.dot(now, picks, preferred_element_type=F32)
    lanes = 2 * CELLS
    step = lanes // 4
    frame = (lax.broadcasted_iota(jnp.int32, (PAIRS * 2 * PART, lanes), 1) >> 5) & 1
    for tap in range(9):
        first = earliest[:, tap * lanes : (tap + 1) * lanes]
        last = latest[:, tap * lanes : (tap + 1) * lanes]
        middle = jnp.where(
            frame == 0, pltpu.roll(first, lanes - step, 1), pltpu.roll(last, step, 1)
        )
        for dt, taken in enumerate((first, middle, last)):
            taken = taken.astype(BF16)
            for pair in range(PAIRS):
                for part in range(2):
                    row = (2 * pair + part) * PART
                    windows[
                        part,
                        (9 * dt + tap) * PART : (9 * dt + tap + 1) * PART,
                        pair * lanes : (pair + 1) * lanes,
                    ] = taken[row : row + PART]
    for copy in copies:
        copy.wait()
    sums = weight_dots(windows, weights, half)
    out_ref[...] = sums.reshape(out_ref.shape)


def edge_kernel(edge_ref, part_ref, own_ref, other_ref, out_ref, windows, weights, arrived):
    core, half = lax.axis_index("core"), lax.axis_index("y") & 1
    copies = []
    for i, ref in enumerate((own_ref, other_ref)):
        for dt in range(3):
            taps = ref.at[pl.ds(9 * dt + 6 * half, 3)]
            copies.append(pltpu.make_async_copy(taps, weights.at[i, dt], arrived.at[i, dt]))
    for copy in copies:
        copy.start()

    def windows_of(which, shift):
        block = jnp.concatenate([edge_ref[which, 0], edge_ref[which, 1]], axis=1)
        return jnp.dot(block, edge_picks(shift), preferred_element_type=F32)

    earliest = windows_of(1 - core, 2 * COLS * (1 - core))
    latest = windows_of(core, 0)
    frame = (lax.broadcasted_iota(jnp.int32, (2 * PART, EDGE), 1) >> 4) & 1
    for dx in range(3):
        first = earliest[:, dx * EDGE : (dx + 1) * EDGE]
        last = latest[:, dx * EDGE : (dx + 1) * EDGE]
        middle = jnp.where(
            frame == 0, pltpu.roll(first, EDGE - COLS, 1), pltpu.roll(last, COLS, 1)
        )
        for dt, taken in enumerate((first, middle, last)):
            taken = taken.astype(BF16)
            for part in range(2):
                row = (3 * dt + dx) * PART
                windows[part, row : row + PART] = taken[part * PART : (part + 1) * PART]
    for copy in copies:
        copy.wait()
    sums = weight_dots(windows, weights, half)
    for y in range(LINE):
        for f in range(FRAMES):
            beside = sums[(2 * y + f) * COLS : (2 * y + f + 1) * COLS]
            for r in range(HALF):
                value = part_ref[y, f, r] + jnp.where(half == r, beside, 0.0)
                row = (f * HALF + r) * COLS
                out_ref[y, row : row + COLS] = value.astype(BF16)


def block_kernel(part_ref, lat_ref, bias_ref, later_ref, out_ref):
    del later_ref
    bias = bias_ref[...].reshape(1, CHANS)
    for half in range(2):
        total = part_ref[half].astype(F32)
        for y in range(half + 2, LINE, 2):
            total = total + part_ref[y].astype(F32)
        total = total + bias
        size = HALF * COLS
        for f in range(FRAMES):
            rows = slice(half * HALF, (half + 1) * HALF)
            skip = lat_ref[f, rows].reshape(size, CHANS).astype(F32)
            value = (skip + total[f * size : (f + 1) * size]).astype(BF16)
            out_ref[f, rows] = value.reshape(HALF, COLS, CHANS)


def upper_kernel(up_ref, block_ref, down_ref, weight_ref, bias_ref, out_ref):
    pieces = []
    for f in range(FRAMES):
        pieces += [up_ref[f], block_ref[f].reshape(ROWS * COLS, CHANS), down_ref[f]]
    bordered = jnp.concatenate(pieces, axis=0)
    rows = jnp.dot(row_picks(), bordered, preferred_element_type=F32).astype(BF16)
    cells = COLS * FRAMES * 2 * ROWS
    total = jnp.zeros((cells, 6 * OUTS), F32)
    for dy in range(3):
        weight = weight_ref[3 * dy : 3 * dy + 3].reshape(6 * OUTS, CHANS)
        total = total + lax.dot_general(
            rows[dy * cells : (dy + 1) * cells], weight, NT_DIMS, preferred_element_type=F32
        )
    wide = 2 * OUTS
    bias = bias_ref[...].reshape(1, OUTS)
    bias = jnp.concatenate([bias, bias], axis=1)
    lines = FRAMES * 2 * ROWS
    total = total.reshape(COLS, lines, 3 * wide)
    left = lax.broadcasted_iota(jnp.int32, (lines, wide), 1) < OUTS
    zero = jnp.zeros((lines, wide), F32)
    for c in range(COLS):
        first = total[c, :, :wide]
        first_before = total[c - 1, :, :wide] if c else zero
        last = total[c, :, 2 * wide :]
        last_after = total[c + 1, :, 2 * wide :] if c < COLS - 1 else zero
        value = (
            jnp.where(left, first_before, first)
            + total[c, :, wide : 2 * wide]
            + jnp.where(left, last, last_after)
            + bias
        )
        out_ref[:, c * wide : (c + 1) * wide] = value.astype(BF16)


def row_neighbours(block):
    axes = ("z", "x")
    count = lax.axis_size(axes)
    down = [(i, i + 1) for i in range(count - 1)]
    up = [(i + 1, i) for i in range(count - 1)]
    above = lax.ppermute(block[:, ROWS - 1], axes, down)
    below = lax.ppermute(block[:, 0], axes, up)
    return above, below


def row_beside(edges):
    axes = ("y", "z", "x")
    count = lax.axis_size(("z", "x"))
    pairs = []
    for y in range(LINE):
        for i in range(count):
            j = i + 1 if y % 2 == 0 else i - 1
            if 0 <= j < count:
                pairs.append((y * count + i, y * count + j))
    return lax.ppermute(edges, axes, pairs)


def call(kernel, shape, inputs, scratch=(), kind=BF16, limit=16):
    spaces = [pltpu.HBM if far else pltpu.VMEM for _, far in inputs]
    return pl.pallas_call(
        kernel,
        out_shape=jax.ShapeDtypeStruct(shape, kind),
        in_specs=[pl.BlockSpec(memory_space=space) for space in spaces],
        out_specs=pl.BlockSpec(memory_space=pltpu.VMEM),
        scratch_shapes=list(scratch),
        compiler_params=pltpu.CompilerParams(vmem_limit_bytes=limit * 1024 * 1024),
    )(*[array for array, _ in inputs])


def local(latent, gain_first, conv_first, bias_first, conv_upper, bias_upper):
    other = lax.ppermute(conv_first, "y", [(i, i ^ 1) for i in range(LINE)])
    acts = call(
        act_kernel,
        (LINE, 2 * PART, SENT),
        [(latent, True), (gain_first, True)],
        [
            pltpu.VMEM(latent.shape, BF16),
            pltpu.VMEM(gain_first.shape, F32),
            pltpu.SemaphoreType.DMA((2,)),
        ],
    )
    acts, conv_first, conv_upper = lax.optimization_barrier((acts, conv_first, conv_upper))
    own = lax.all_gather(conv_first, "core", axis=1, tiled=True)
    other = lax.all_gather(other, "core", axis=1, tiled=True)
    upper = jnp.swapaxes(conv_upper, 1, 2)
    upper = jnp.concatenate([upper, upper], axis=1)
    acts = lax.all_to_all(acts, "y", 0, 0, tiled=True)
    acts, own, other = lax.optimization_barrier((acts, own, other))
    acts = lax.all_gather(acts, "core", axis=0, tiled=False)
    edges = row_beside(call(pack_kernel, (2, 2, 2 * PART, SENT), [(acts, False)]))
    parts = call(
        inner_kernel,
        (LINE, FRAMES, HALF, COLS, CHANS),
        [(acts, False), (own, True), (other, True)],
        [
            pltpu.VMEM((PAIRS, 2 * PART, 2 * SENT), BF16),
            pltpu.VMEM((PAIRS, 2 * PART, 2 * SENT), BF16),
            pltpu.VMEM((2, 27 * PART, LINE * CELLS), BF16),
            pltpu.VMEM((2, 27, PART, CHANS), BF16),
            pltpu.SemaphoreType.DMA((2,)),
        ],
        kind=F32,
        limit=32,
    )
    parts = call(
        edge_kernel,
        (LINE, CELLS, CHANS),
        [(edges, False), (parts, False), (own, True), (other, True)],
        [
            pltpu.VMEM((2, 9 * PART, EDGE), BF16),
            pltpu.VMEM((2, 3, 3, PART, CHANS), BF16),
            pltpu.SemaphoreType.DMA((2, 3)),
        ],
    )
    parts = lax.all_to_all(parts, "y", 0, 0, tiled=True)
    block = call(
        block_kernel,
        (FRAMES, ROWS, COLS, CHANS),
        [(parts, False), (latent, False), (bias_first, False), (upper, True)],
    )
    above, below = row_neighbours(block)
    out = call(
        upper_kernel,
        (FRAMES * 2 * ROWS, 2 * COLS * OUTS),
        [(array, False) for array in (above, block, below, upper, bias_upper)],
    )
    return out.reshape(FRAMES, 2 * ROWS, 2 * COLS * OUTS)


def solution(mesh):
    fine = Mesh(mesh.devices.reshape(8, 2, 8, 4), ("y", "core", "z", "x"))
    tm, rows = ("y", "core"), ("z", "x")
    in_specs = (P(tm, rows, None, None), P(), P(None, tm, None), P(), P(), P())
    return jax.shard_map(
        local, mesh=fine, in_specs=in_specs, out_specs=P(tm, rows, None), check_vma=False
    )
```

time: 82.5 us -> 71.4 us (0.87)
  blocking collectives: 27.6 us -> 7.3 us
  waiting for transfers between devices: 15.4 us -> 27.7 us
  local copies, waits for them, and re-layouts: 4.77 us -> 1.6 us
  Pallas kernels: 7.03 us -> 9.65 us
  starting transfers between devices: 24.7 us -> 22.6 us
    all_to_all x1 -> x0, blocking collectives: 17.7 us -> none  [local(): parts = lax.all_to_all(parts, 'y', 0, 0, tiled=True)]
    all_to_all x0 -> x1, waiting for transfers between devices: none -> 12.2 us  [local(): parts = lax.all_to_all(parts, 'y', 0, 0, tiled=True)]
    ppermute x2 -> x1, starting transfers between devices: 10.8 us -> 3.43 us  [row_neighbours(): below = lax.ppermute(block[:, 0], axes, up)]
    all_to_all x0 -> x1, starting transfers between devices: none -> 3.67 us  [local(): parts = lax.all_to_all(parts, 'y', 0, 0, tiled=True)]
    ppermute x0 -> x1, starting transfers between devices: none -> 3.4 us  [row_beside(): return lax.ppermute(edges, axes, pairs)]
    all_to_all x1, waiting for transfers between devices: 8.28 us -> 4.97 us  [local(): acts = lax.all_to_all(acts, 'y', 0, 0, tiled=True)]
    ppermute x0 -> x1, waiting for transfers between devices: none -> 3.12 us  [row_beside(): return lax.ppermute(edges, axes, pairs)]
    pallas_call x4 -> x6, Pallas kernels: 7.03 us -> 9.65 us  [call(): pl.pallas_call(kernel, out_shape=jax.ShapeDtypeStruct(shape, kind), in_sp...]
  transfers between devices with their start and end apart: 6 -> 6, of which waited for: 2 -> 5; matrix products, arithmetic and copies ran while one was open for 3% -> 3% of each run, Pallas kernels for 1% -> 7%
where the time goes in v3:
time: 71.4 us; the launch traced here: 70.9 us
  waiting for transfers between devices  27.7 us (39%)
  starting transfers between devices  22.6 us (32%)
  Pallas kernels  9.65 us (14%)
  blocking collectives  7.3 us (10%)
  other arithmetic  2.02 us (3%)
  local copies, waits for them, and re-layouts  1.6 us (2%)
    all_to_all x1, waiting for transfers between devices, local(): parts = lax.all_to_all(parts, 'y', 0, 0, tiled=True)  12.2 us
    pallas_call x6, Pallas kernels, call(): pl.pallas_call(kernel, out_shape=jax.ShapeDtypeStruct(shape, kind), in_sp...  9.65 us
    ppermute x1, waiting for transfers between devices, row_neighbours(): above = lax.ppermute(block[:, ROWS - 1], axes, down)  6.61 us
    all_to_all x1, starting transfers between devices, local(): acts = lax.all_to_all(acts, 'y', 0, 0, tiled=True)  6.21 us
    all_to_all x1, waiting for transfers between devices, local(): acts = lax.all_to_all(acts, 'y', 0, 0, tiled=True)  4.97 us
    all_to_all x1, starting transfers between devices, local(): parts = lax.all_to_all(parts, 'y', 0, 0, tiled=True)  3.67 us
    ppermute x1, starting transfers between devices, local(): other = lax.ppermute(conv_first, 'y', [(i, i ^ 1) for i in range(LINE)])  3.47 us
    ppermute x1, starting transfers between devices, row_neighbours(): below = lax.ppermute(block[:, 0], axes, up)  3.43 us
  transfers between devices with their start and end apart: 6, of which 5 were waited for; matrix products, arithmetic and copies ran while one was open for 3% of the time, Pallas kernels for 7%

profile of v3, /device:TPU:256, one launch (start us, length us, event | category | flops | bytes accessed | tf_op | source)
XLA Modules:
  0.0 70.9 jit_solution(11253194581349185946)
XLA Ops:
  0.0 3.5 %collective-permute-start = (bf16[27,24,384]{2,1,0:T(8,128)(2,1)}, bf16[27,24,384]{2,1,0:T(8,128)(2,1)S(1)}, u32[]{:S(2)}, u32[]{:S(2)}) collective-permute-start(bf16[27,24,384]{2,1,0:T(8,128)(2,1)} %param.8), channel_id=1, source_target_pairs={{0,64},{64,0},{128,192},{192,128},{256,320},{320,256},{384,448},{4... | collective-permute-start | bytes 1493000 | tf_op jit(solution)/shard_map/ppermute | solution.py:283
  3.5 0.0 copy-start
  3.5 0.9 %copy-done = bf16[2,4,16,384]{3,2,1,0:T(8,128)(2,1)S(1)} copy-done((bf16[2,4,16,384]{3,2,1,0:T(8,128)(2,1)S(1)}, bf16[2,4,16,384]{3,2,1,0:T(8,128)(2,1)}, u32[]{:S(2)}) %copy-start) | copy-done | bytes 98328
  4.4 0.0 copy-start.2
  4.4 0.7 copy-done.2
  5.1 1.2 %shard_map.64 = bf16[8,96,128]{2,1,0:T(8,128)(2,1)} custom-call(bf16[2,4,16,384]{3,2,1,0:T(8,128)(2,1)S(1)} %copy-done, f32[384]{0:T(512)S(1)} %copy-done.2), custom_call_target="tpu_custom_call" | custom-call | tf_op jit(solution)/shard_map/pallas_call | solution.py:272
  6.3 6.2 %all-to-all-start = ((bf16[8,96,128]{2,1,0:T(8,128)(2,1)}), bf16[8,96,128]{2,1,0:T(8,128)(2,1)S(1)}, u32[]{:S(2)}, u32[]{:S(2)}) async-start(bf16[8,96,128]{2,1,0:T(8,128)(2,1)} %shard_map.64), calls=%async_computation | async-start | bytes 393216 | tf_op jit(solution)/shard_map/all_to_all | solution.py:299
  12.5 2.7 %all_gather.12.own_ref = bf16[27,48,384]{2,1,0:T(8,128)(2,1)S(1)} all-gather(bf16[27,24,384]{2,1,0:T(8,128)(2,1)} %param.8), channel_id=1, replica_groups=mesh['y'=8,'core'=2,'z'=8,'x'=4] {'core'}, dimensions={1}, use_global_device_ids=true | all-gather | bytes 1492992 | tf_op jit(solution)/shard_map/all_gather | solution.py:295
  15.2 0.7 %collective-permute-done = bf16[27,24,384]{2,1,0:T(8,128)(2,1)S(1)} collective-permute-done((bf16[27,24,384]{2,1,0:T(8,128)(2,1)}, bf16[27,24,384]{2,1,0:T(8,128)(2,1)S(1)}, u32[]{:S(2)}, u32[]{:S(2)}) %collective-permute-start) | collective-permute-done | bytes 497696 | tf_op jit(solution)/shard_map/ppermute | solution.py:283
  15.9 2.5 %all_gather.13.other_ref = bf16[27,48,384]{2,1,0:T(8,128)(2,1)S(1)} all-gather(bf16[27,24,384]{2,1,0:T(8,128)(2,1)S(1)} %collective-permute-done), channel_id=1, replica_groups=mesh['y'=8,'core'=2,'z'=8,'x'=4] {'core'}, dimensions={1}, use_global_device_ids=true | all-gather | bytes 1492992 | tf_op jit(solution)/shard_map/all_gather | solution.py:296
  18.4 5.0 %all-to-all-done = bf16[8,96,128]{2,1,0:T(8,128)(2,1)S(1)} async-done(((bf16[8,96,128]{2,1,0:T(8,128)(2,1)}), bf16[8,96,128]{2,1,0:T(8,128)(2,1)S(1)}, u32[]{:S(2)}, u32[]{:S(2)}) %all-to-all-start) | async-done | bytes 196640 | tf_op jit(solution)/shard_map/all_to_all | solution.py:299
  23.4 2.1 %all-gather = bf16[16,96,128]{2,1,0:T(8,128)(2,1)S(1)} all-gather(bf16[8,96,128]{2,1,0:T(8,128)(2,1)S(1)} %all-to-all-done), channel_id=2, replica_groups=mesh['y'=8,'core'=2,'z'=8,'x'=4] {'core'}, dimensions={0}, use_global_device_ids=true | all-gather | bytes 589824 | tf_op jit(solution)/shard_map/all_gather | solution.py:301
  25.5 0.3 shard_map.65
  25.8 3.4 %collective-permute-start.1 = (bf16[2,2,96,128]{3,2,1,0:T(8,128)(2,1)S(1)}, bf16[2,2,96,128]{3,2,1,0:T(8,128)(2,1)S(1)}, u32[]{:S(2)}, u32[]{:S(2)}) collective-permute-start(bf16[2,2,96,128]{3,2,1,0:T(8,128)(2,1)S(1)} %shard_map.65), channel_id=1, source_target_pairs={{0,1},{1,2},{2,3},{3,4},{4,5},{5,6},{6,7},{7,8},{8,9},{9,10},{10,1... | collective-permute-start | bytes 294920 | tf_op jit(solution)/shard_map/ppermute | solution.py:267
  29.2 3.5 %shard_map.66.part_ref = f32[8,2,2,16,384]{4,3,2,1,0:T(8,128)S(1)} custom-call(bf16[2,8,96,128]{3,2,1,0:T(8,128)(2,1)S(1)} %bitcast.12, bf16[27,48,384]{2,1,0:T(8,128)(2,1)S(1)} %all_gather.12.own_ref, bf16[27,48,384]{2,1,0:T(8,128)(2,1)S(1)} %all_gather.13.other_ref), custom_call_target="tpu_custom_call" | custom-call | tf_op jit(solution)/shard_map/pallas_call | solution.py:272
  32.7 3.1 %collective-permute-done.1.edge_ref = bf16[2,2,96,128]{3,2,1,0:T(8,128)(2,1)S(1)} collective-permute-done((bf16[2,2,96,128]{3,2,1,0:T(8,128)(2,1)S(1)}, bf16[2,2,96,128]{3,2,1,0:T(8,128)(2,1)S(1)}, u32[]{:S(2)}, u32[]{:S(2)}) %collective-permute-start.1) | collective-permute-done | bytes 98336 | tf_op jit(solution)/shard_map/ppermute | solution.py:267
  35.8 2.5 %shard_map.67 = bf16[8,64,384]{2,1,0:T(8,128)(2,1)} custom-call(bf16[2,2,96,128]{3,2,1,0:T(8,128)(2,1)S(1)} %collective-permute-done.1.edge_ref, f32[8,2,2,16,384]{4,3,2,1,0:T(8,128)S(1)} %shard_map.66.part_ref, bf16[27,48,384]{2,1,0:T(8,128)(2,1)S(1)} %all_gather.12.own_ref, bf16[27,48,384]{2,1,0:T(8,128)(2,1)S(1)} %all_gather.13.other_ref), custom_call_target="tpu_custom_call" | custom-call | tf_op jit(solution)/shard_map/pallas_call | solution.py:272
  38.3 0.0 copy-start.1
  38.3 0.0 copy-start.3
  38.3 3.7 %all-to-all-start.1 = ((bf16[8,64,384]{2,1,0:T(8,128)(2,1)}), bf16[8,64,384]{2,1,0:T(8,128)(2,1)S(1)}, u32[]{:S(2)}, u32[]{:S(2)}) async-start(bf16[8,64,384]{2,1,0:T(8,128)(2,1)} %shard_map.67), calls=%async_computation.1 | async-start | bytes 786432 | tf_op jit(solution)/shard_map/all_to_all | solution.py:327
  42.0 2.0 %pad_maximum_fusion.later_ref.weight_ref = bf16[9,384,384]{2,1,0:T(8,128)(2,1)S(1)} fusion(bf16[9,192,384]{2,1,0:T(8,128)(2,1)} %bitcast.13), kind=kLoop, calls=%fused_computation | loop fusion | flops 5308416 | bytes 3981312 | tf_op jit(solution)/shard_map/concatenate | solution.py:298
  44.0 0.0 copy-start.4
  44.0 12.2 %all-to-all-done.1.part_ref = bf16[8,64,384]{2,1,0:T(8,128)(2,1)S(1)} async-done(((bf16[8,64,384]{2,1,0:T(8,128)(2,1)}), bf16[8,64,384]{2,1,0:T(8,128)(2,1)S(1)}, u32[]{:S(2)}, u32[]{:S(2)}) %all-to-all-start.1) | async-done | bytes 393248 | tf_op jit(solution)/shard_map/all_to_all | solution.py:327
  56.3 0.0 copy-done.1
  56.3 0.0 copy-done.3
  56.3 0.1 shard_map.68.block_ref
  56.4 3.4 %collective-permute-start.3 = (bf16[2,16,384]{2,1,0:T(8,128)(2,1)S(1)}, bf16[2,16,384]{2,1,0:T(8,128)(2,1)S(1)}, u32[]{:S(2)}, u32[]{:S(2)}) collective-permute-start(bf16[2,16,384]{2,1,0:T(8,128)(2,1)S(1)} %get-tuple-element.17), channel_id=1, source_target_pairs={{1,0},{2,1},{3,2},{4,3},{5,4},{6,5},{7,6},{8,7},{9,8},{10,9},{11,1... | collective-permute-start | bytes 73736 | tf_op jit(solution)/shard_map/ppermute | solution.py:254
  59.8 2.4 %collective-permute-start.2 = (bf16[2,16,384]{2,1,0:T(8,128)(2,1)S(1)}, bf16[2,16,384]{2,1,0:T(8,128)(2,1)S(1)}, u32[]{:S(2)}, u32[]{:S(2)}) collective-permute-start(bf16[2,16,384]{2,1,0:T(8,128)(2,1)S(1)} %get-tuple-element.18), channel_id=1, source_target_pairs={{0,1},{1,2},{2,3},{3,4},{4,5},{5,6},{6,7},{7,8},{8,9},{9,10},{10,1... | collective-permute-start | bytes 73736 | tf_op jit(solution)/shard_map/ppermute | solution.py:253
  62.2 0.0 collective-permute-done.3.down_ref
  62.2 6.6 %collective-permute-done.2.up_ref = bf16[2,16,384]{2,1,0:T(8,128)(2,1)S(1)} collective-permute-done((bf16[2,16,384]{2,1,0:T(8,128)(2,1)S(1)}, bf16[2,16,384]{2,1,0:T(8,128)(2,1)S(1)}, u32[]{:S(2)}, u32[]{:S(2)}) %collective-permute-start.2) | collective-permute-done | bytes 24608 | tf_op jit(solution)/shard_map/ppermute | solution.py:253
  68.8 0.0 copy-done.4
  68.8 2.1 %shard_map.69 = bf16[16,6144]{1,0:T(8,128)(2,1)} custom-call(bf16[2,16,384]{2,1,0:T(8,128)(2,1)S(1)} %collective-permute-done.2.up_ref, bf16[2,4,16,384]{3,2,1,0:T(8,128)(2,1)S(1)} %shard_map.68.block_ref, bf16[2,16,384]{2,1,0:T(8,128)(2,1)S(1)} %collective-permute-done.3.down_ref, bf16[9,384,384]{2,1,0:T(8,128)(2,1)S(1)} %pad_maximum_fusion.later_ref.weight_ref, ...), custom_call_target="tpu_custom_call" | custom-call | tf_op jit(solution)/shard_map/pallas_call | solution.py:272
  (1 shorter events, 0.0 us)
Async XLA Ops:
  0.0 15.9 %collective-permute-start = (bf16[27,24,384]{2,1,0:T(8,128)(2,1)}, bf16[27,24,384]{2,1,0:T(8,128)(2,1)S(1)}, u32[]{:S(2)}, u32[]{:S(2)}) collective-permute-start(bf16[27,24,384]{2,1,0:T(8,128)(2,1)} %param.8), channel_id=1, source_target_pairs={{0,64},{64,0},{128,192},{192,128},{256,320},{320,256},{384,448},{4... | collective-permute-start | bytes 1493000 | tf_op jit(solution)/shard_map/ppermute | solution.py:283
  3.5 0.9 %copy-start = (bf16[2,4,16,384]{3,2,1,0:T(8,128)(2,1)S(1)}, bf16[2,4,16,384]{3,2,1,0:T(8,128)(2,1)}, u32[]{:S(2)}) copy-start(bf16[2,4,16,384]{3,2,1,0:T(8,128)(2,1)} %lat_ref.3) | copy-start | bytes 294916
  4.4 0.7 copy-start.2
  6.3 17.1 %all-to-all-start = ((bf16[8,96,128]{2,1,0:T(8,128)(2,1)}), bf16[8,96,128]{2,1,0:T(8,128)(2,1)S(1)}, u32[]{:S(2)}, u32[]{:S(2)}) async-start(bf16[8,96,128]{2,1,0:T(8,128)(2,1)} %shard_map.64), calls=%async_computation | async-start | bytes 393216 | tf_op jit(solution)/shard_map/all_to_all | solution.py:299
  25.8 10.1 %collective-permute-start.1 = (bf16[2,2,96,128]{3,2,1,0:T(8,128)(2,1)S(1)}, bf16[2,2,96,128]{3,2,1,0:T(8,128)(2,1)S(1)}, u32[]{:S(2)}, u32[]{:S(2)}) collective-permute-start(bf16[2,2,96,128]{3,2,1,0:T(8,128)(2,1)S(1)} %shard_map.65), channel_id=1, source_target_pairs={{0,1},{1,2},{2,3},{3,4},{4,5},{5,6},{6,7},{7,8},{8,9},{9,10},{10,1... | collective-permute-start | bytes 294920 | tf_op jit(solution)/shard_map/ppermute | solution.py:267
  38.3 18.0 %copy-start.1 = (bf16[2,4,16,384]{3,2,1,0:T(8,128)(2,1)S(1)}, bf16[2,4,16,384]{3,2,1,0:T(8,128)(2,1)}, u32[]{:S(2)}) copy-start(bf16[2,4,16,384]{3,2,1,0:T(8,128)(2,1)} %lat_ref.3) | copy-start | bytes 294916
  38.3 18.0 %copy-start.3 = (f32[384]{0:T(512)S(1)}, f32[384]{0:T(512)}, u32[]{:S(2)}) copy-start(f32[384]{0:T(512)} %bias_ref.2) | copy-start | bytes 4612
  38.3 17.9 %all-to-all-start.1 = ((bf16[8,64,384]{2,1,0:T(8,128)(2,1)}), bf16[8,64,384]{2,1,0:T(8,128)(2,1)S(1)}, u32[]{:S(2)}, u32[]{:S(2)}) async-start(bf16[8,64,384]{2,1,0:T(8,128)(2,1)} %shard_map.67), calls=%async_computation.1 | async-start | bytes 786432 | tf_op jit(solution)/shard_map/all_to_all | solution.py:327
  44.0 24.8 %copy-start.4 = (f32[192]{0:T(256)S(1)}, f32[192]{0:T(256)}, u32[]{:S(2)}) copy-start(f32[192]{0:T(256)} %bias_ref.3) | copy-start | bytes 2308
  56.4 5.9 %collective-permute-start.3 = (bf16[2,16,384]{2,1,0:T(8,128)(2,1)S(1)}, bf16[2,16,384]{2,1,0:T(8,128)(2,1)S(1)}, u32[]{:S(2)}, u32[]{:S(2)}) collective-permute-start(bf16[2,16,384]{2,1,0:T(8,128)(2,1)S(1)} %get-tuple-element.17), channel_id=1, source_target_pairs={{1,0},{2,1},{3,2},{4,3},{5,4},{6,5},{7,6},{8,7},{9,8},{10,9},{11,1... | collective-permute-start | bytes 73736 | tf_op jit(solution)/shard_map/ppermute | solution.py:254
  59.8 9.0 %collective-permute-start.2 = (bf16[2,16,384]{2,1,0:T(8,128)(2,1)S(1)}, bf16[2,16,384]{2,1,0:T(8,128)(2,1)S(1)}, u32[]{:S(2)}, u32[]{:S(2)}) collective-permute-start(bf16[2,16,384]{2,1,0:T(8,128)(2,1)S(1)} %get-tuple-element.18), channel_id=1, source_target_pairs={{0,1},{1,2},{2,3},{3,4},{4,5},{5,6},{6,7},{7,8},{8,9},{9,10},{10,1... | collective-permute-start | bytes 73736 | tf_op jit(solution)/shard_map/ppermute | solution.py:253

commit v4 on v3

--- a/solution.py
+++ b/solution.py
@@ -16,7 +16,8 @@
 CELLS = FRAMES * HALF * COLS
 SENT = FRAMES * ROWS * COLS
 EDGE = LINE * FRAMES * COLS
-BORDERED = FRAMES * (ROWS + 2) * COLS
+ORDER = (4, 5, 6, 7, 0, 1, 2, 3)
+SLOT = tuple(ORDER.index(y) for y in range(LINE))
 NT_DIMS = (((1,), (1,)), ((), ()))
 TN_DIMS = (((0,), (0,)), ((), ()))
 
@@ -46,10 +47,12 @@
 
 
 def row_picks():
-    shape = (6 * ROWS * COLS * FRAMES, BORDERED)
+    shape = (6 * ROWS * COLS * FRAMES, SENT)
     place = lax.broadcasted_iota(jnp.int32, (shape[0], 1), 0)
     dy, col, frame, i = place >> 8, (place >> 4) & 15, (place >> 3) & 1, place & 7
-    wanted = frame * ((ROWS + 2) * COLS) + (((i + dy + 1) >> 1) << 4) + col
+    row = ((i + dy + 1) >> 1) - 1
+    wanted = (frame << 6) + (row << 4) + col
+    wanted = jnp.where((row >= 0) & (row < ROWS), wanted, -1)
     return one_hot(wanted, lax.broadcasted_iota(jnp.int32, shape, 1))
 
 
@@ -76,7 +79,7 @@
     flipped = lax.dot_general(eye, act, NT_DIMS, preferred_element_type=F32).astype(BF16)
     for y in range(LINE):
         start = (y // 2) * 2 * PART
-        out_ref[y] = flipped[start : start + 2 * PART]
+        out_ref[SLOT[y]] = flipped[start : start + 2 * PART]
 
 
 def pack_kernel(act_ref, out_ref):
@@ -86,7 +89,7 @@
     picks = one_hot(wanted, lax.broadcasted_iota(jnp.int32, (4 * SENT, SENT), 0))
     for core in range(2):
         for group in range(2):
-            block = jnp.concatenate([act_ref[core, 4 * group + k] for k in range(4)], axis=1)
+            block = jnp.concatenate([act_ref[core, SLOT[4 * group + k]] for k in range(4)], axis=1)
             packed = jnp.dot(block, picks, preferred_element_type=F32)
             out_ref[core, group] = packed.astype(BF16)
 
@@ -115,15 +118,15 @@
         copy.start()
     for y in range(LINE):
         where = (y // 2, slice(None), slice((y % 2) * SENT, (y % 2 + 1) * SENT))
-        here[where] = act_ref[core, y]
+        here[where] = act_ref[core, SLOT[y]]
 
         @pl.when(core == 1)
         def _():
-            before[where] = act_ref[0, y]
+            before[where] = act_ref[0, SLOT[y]]
 
         @pl.when(core == 0)
         def _():
-            before[where] = act_ref[1, y - 1] if y else jnp.zeros_like(act_ref[1, 0])
+            before[where] = act_ref[1, SLOT[y - 1]] if y else jnp.zeros_like(act_ref[1, 0])
 
     now = here[...].reshape(PAIRS * 2 * PART, 2 * SENT)
     prior = before[...].reshape(PAIRS * 2 * PART, 2 * SENT)
@@ -192,16 +195,16 @@
             for r in range(HALF):
                 value = part_ref[y, f, r] + jnp.where(half == r, beside, 0.0)
                 row = (f * HALF + r) * COLS
-                out_ref[y, row : row + COLS] = value.astype(BF16)
+                out_ref[SLOT[y], row : row + COLS] = value.astype(BF16)
 
 
 def block_kernel(part_ref, lat_ref, bias_ref, later_ref, out_ref):
     del later_ref
     bias = bias_ref[...].reshape(1, CHANS)
     for half in range(2):
-        total = part_ref[half].astype(F32)
+        total = part_ref[SLOT[half]].astype(F32)
         for y in range(half + 2, LINE, 2):
-            total = total + part_ref[y].astype(F32)
+            total = total + part_ref[SLOT[y]].astype(F32)
         total = total + bias
         size = HALF * COLS
         for f in range(FRAMES):
@@ -211,35 +214,57 @@
             out_ref[f, rows] = value.reshape(HALF, COLS, CHANS)
 
 
-def upper_kernel(up_ref, block_ref, down_ref, weight_ref, bias_ref, out_ref):
-    pieces = []
-    for f in range(FRAMES):
-        pieces += [up_ref[f], block_ref[f].reshape(ROWS * COLS, CHANS), down_ref[f]]
-    bordered = jnp.concatenate(pieces, axis=0)
-    rows = jnp.dot(row_picks(), bordered, preferred_element_type=F32).astype(BF16)
+def upper_inner_kernel(block_ref, weight_ref, out_ref):
+    rows = jnp.dot(
+        row_picks(), block_ref[...].reshape(SENT, CHANS), preferred_element_type=F32
+    ).astype(BF16)
     cells = COLS * FRAMES * 2 * ROWS
-    total = jnp.zeros((cells, 6 * OUTS), F32)
+    total = None
     for dy in range(3):
-        weight = weight_ref[3 * dy : 3 * dy + 3].reshape(6 * OUTS, CHANS)
-        total = total + lax.dot_general(
-            rows[dy * cells : (dy + 1) * cells], weight, NT_DIMS, preferred_element_type=F32
-        )
+        part = lax.dot_general(
+            rows[dy * cells : (dy + 1) * cells],
+            weight_ref[3 * dy : 3 * dy + 3].reshape(6 * OUTS, CHANS),
+            NT_DIMS,
+            preferred_element_type=F32,
+        )
+        total = part if total is None else total + part
+    out_ref[...] = total.reshape(out_ref.shape)
+
+
+def upper_kernel(up_ref, down_ref, inner_ref, weight_ref, bias_ref, out_ref):
     wide = 2 * OUTS
+    lines = FRAMES * 2 * ROWS
+
+    def taps(ref, dy):
+        return lax.dot_general(
+            ref[...].reshape(FRAMES * COLS, CHANS),
+            weight_ref[3 * dy : 3 * dy + 3].reshape(3 * wide, CHANS),
+            NT_DIMS,
+            preferred_element_type=F32,
+        )
+
+    above, below = taps(up_ref, 0), taps(down_ref, 2)
+    line = lax.broadcasted_iota(jnp.int32, (lines, 3 * wide), 0)
+    totals = []
+    for c in range(COLS):
+        total = inner_ref[c]
+        for f in range(FRAMES):
+            row = f * COLS + c
+            top, bottom = f * 2 * ROWS, (f + 1) * 2 * ROWS - 1
+            total = total + jnp.where(line == top, above[row : row + 1], 0.0)
+            total = total + jnp.where(line == bottom, below[row : row + 1], 0.0)
+        totals.append(total)
     bias = bias_ref[...].reshape(1, OUTS)
     bias = jnp.concatenate([bias, bias], axis=1)
-    lines = FRAMES * 2 * ROWS
-    total = total.reshape(COLS, lines, 3 * wide)
     left = lax.broadcasted_iota(jnp.int32, (lines, wide), 1) < OUTS
     zero = jnp.zeros((lines, wide), F32)
     for c in range(COLS):
-        first = total[c, :, :wide]
-        first_before = total[c - 1, :, :wide] if c else zero
-        last = total[c, :, 2 * wide :]
-        last_after = total[c + 1, :, 2 * wide :] if c < COLS - 1 else zero
+        first_before = totals[c - 1][:, :wide] if c else zero
+        last_after = totals[c + 1][:, 2 * wide :] if c < COLS - 1 else zero
         value = (
-            jnp.where(left, first_before, first)
-            + total[c, :, wide : 2 * wide]
-            + jnp.where(left, last, last_after)
+            jnp.where(left, first_before, totals[c][:, :wide])
+            + totals[c][:, wide : 2 * wide]
+            + jnp.where(left, totals[c][:, 2 * wide :], last_after)
             + bias
         )
         out_ref[:, c * wide : (c + 1) * wide] = value.astype(BF16)
@@ -265,6 +290,10 @@
             if 0 <= j < count:
                 pairs.append((y * count + i, y * count + j))
     return lax.ppermute(edges, axes, pairs)
+
+
+def along_line(blocks):
+    return lax.all_to_all(blocks, "y", 0, 0, tiled=True, axis_index_groups=[list(ORDER)])
 
 
 def call(kernel, shape, inputs, scratch=(), kind=BF16, limit=16):
@@ -290,13 +319,14 @@
             pltpu.VMEM(gain_first.shape, F32),
             pltpu.SemaphoreType.DMA((2,)),
         ],
+        limit=60,
     )
     acts, conv_first, conv_upper = lax.optimization_barrier((acts, conv_first, conv_upper))
     own = lax.all_gather(conv_first, "core", axis=1, tiled=True)
     other = lax.all_gather(other, "core", axis=1, tiled=True)
     upper = jnp.swapaxes(conv_upper, 1, 2)
     upper = jnp.concatenate([upper, upper], axis=1)
-    acts = lax.all_to_all(acts, "y", 0, 0, tiled=True)
+    acts = along_line(acts)
     acts, own, other = lax.optimization_barrier((acts, own, other))
     acts = lax.all_gather(acts, "core", axis=0, tiled=False)
     edges = row_beside(call(pack_kernel, (2, 2, 2 * PART, SENT), [(acts, False)]))
@@ -324,17 +354,23 @@
             pltpu.SemaphoreType.DMA((2, 3)),
         ],
     )
-    parts = lax.all_to_all(parts, "y", 0, 0, tiled=True)
+    parts = along_line(parts)
     block = call(
         block_kernel,
         (FRAMES, ROWS, COLS, CHANS),
         [(parts, False), (latent, False), (bias_first, False), (upper, True)],
     )
     above, below = row_neighbours(block)
+    inner = call(
+        upper_inner_kernel,
+        (COLS, FRAMES * 2 * ROWS, 6 * OUTS),
+        [(block, False), (upper, False)],
+        kind=F32,
+    )
     out = call(
         upper_kernel,
         (FRAMES * 2 * ROWS, 2 * COLS * OUTS),
-        [(array, False) for array in (above, block, below, upper, bias_upper)],
+        [(array, False) for array in (above, below, inner, upper, bias_upper)],
     )
     return out.reshape(FRAMES, 2 * ROWS, 2 * COLS * OUTS)
 

time: 71.4 us -> 69.1 us (0.968)
  waiting for transfers between devices: 27.7 us -> 19.6 us
  starting transfers between devices: 22.6 us -> 28.3 us
  local copies, waits for them, and re-layouts: 1.6 us -> 0.03 us
  Pallas kernels: 9.65 us -> 11.2 us
    all_to_all x2, waiting for transfers between devices: 17.2 us -> 11.2 us  [along_line(): lax.all_to_all(blocks, 'y', 0, 0, tiled=True, axis_index_groups=[list(ORD...]
    all_to_all x2, starting transfers between devices: 9.88 us -> 15.6 us  [along_line(): lax.all_to_all(blocks, 'y', 0, 0, tiled=True, axis_index_groups=[list(ORD...]
    unnamed x10 -> x6, local copies, waits for them, and re-layouts: 1.59 us -> 0.02 us
    pallas_call x6 -> x7, Pallas kernels: 9.65 us -> 11.2 us  [call(): pl.pallas_call(kernel, out_shape=jax.ShapeDtypeStruct(shape, kind), in_sp...]
    ppermute x1, waiting for transfers between devices: 6.61 us -> 5.31 us  [row_neighbours(): above = lax.ppermute(block[:, ROWS - 1], axes, down)]
  transfers between devices with their start and end apart: 6 -> 6, of which waited for: 5 -> 4; matrix products, arithmetic and copies ran while one was open for 3% -> 3% of each run, Pallas kernels for 7% -> 10%
where the time goes in v4:
time: 69.1 us; the launch traced here: 68.7 us
  starting transfers between devices  28.3 us (41%)
  waiting for transfers between devices  19.6 us (28%)
  Pallas kernels  11.2 us (16%)
  blocking collectives  7.3 us (11%)
  other arithmetic  2.02 us (3%)
    all_to_all x2, starting transfers between devices, along_line(): lax.all_to_all(blocks, 'y', 0, 0, tiled=True, axis_index_groups=[list(ORD...  15.6 us
    pallas_call x7, Pallas kernels, call(): pl.pallas_call(kernel, out_shape=jax.ShapeDtypeStruct(shape, kind), in_sp...  11.2 us
    all_to_all x2, waiting for transfers between devices, along_line(): lax.all_to_all(blocks, 'y', 0, 0, tiled=True, axis_index_groups=[list(ORD...  11.2 us
    ppermute x1, waiting for transfers between devices, row_neighbours(): above = lax.ppermute(block[:, ROWS - 1], axes, down)  5.31 us
    ppermute x1, starting transfers between devices, row_neighbours(): below = lax.ppermute(block[:, 0], axes, up)  3.58 us
    ppermute x1, starting transfers between devices, local(): other = lax.ppermute(conv_first, 'y', [(i, i ^ 1) for i in range(LINE)])  3.47 us
    ppermute x1, starting transfers between devices, row_beside(): return lax.ppermute(edges, axes, pairs)  3.4 us
    ppermute x1, waiting for transfers between devices, row_beside(): return lax.ppermute(edges, axes, pairs)  3.12 us
  transfers between devices with their start and end apart: 6, of which 4 were waited for; matrix products, arithmetic and copies ran while one was open for 3% of the time, Pallas kernels for 10%

profile of v4, /device:TPU:256, one launch (start us, length us, event | category | flops | bytes accessed | tf_op | source)
XLA Modules:
  0.0 68.7 jit_solution(9972666664128173963)
XLA Ops:
  0.0 3.5 %collective-permute-start = (bf16[27,24,384]{2,1,0:T(8,128)(2,1)}, bf16[27,24,384]{2,1,0:T(8,128)(2,1)S(1)}, u32[]{:S(2)}, u32[]{:S(2)}) collective-permute-start(bf16[27,24,384]{2,1,0:T(8,128)(2,1)} %param.8), channel_id=1, source_target_pairs={{0,64},{64,0},{128,192},{192,128},{256,320},{320,256},{384,448},{4... | collective-permute-start | bytes 1493000 | tf_op jit(solution)/shard_map/ppermute | solution.py:312
  3.5 2.0 %shard_map.64 = bf16[8,96,128]{2,1,0:T(8,128)(2,1)} custom-call(bf16[2,4,16,384]{3,2,1,0:T(8,128)(2,1)} %lat_ref.3, f32[384]{0:T(512)} %gain_ref.1), custom_call_target="tpu_custom_call" | custom-call | tf_op jit(solution)/shard_map/pallas_call | solution.py:301
  5.5 8.3 %all-to-all-start = ((bf16[8,96,128]{2,1,0:T(8,128)(2,1)}), bf16[8,96,128]{2,1,0:T(8,128)(2,1)S(1)}, u32[]{:S(2)}, u32[]{:S(2)}) async-start(bf16[8,96,128]{2,1,0:T(8,128)(2,1)} %shard_map.64), calls=%async_computation | async-start | bytes 393216 | tf_op jit(solution)/shard_map/all_to_all | solution.py:296
  13.7 2.7 %all_gather.12.own_ref = bf16[27,48,384]{2,1,0:T(8,128)(2,1)S(1)} all-gather(bf16[27,24,384]{2,1,0:T(8,128)(2,1)} %param.8), channel_id=1, replica_groups=mesh['y'=8,'core'=2,'z'=8,'x'=4] {'core'}, dimensions={1}, use_global_device_ids=true | all-gather | bytes 1492992 | tf_op jit(solution)/shard_map/all_gather | solution.py:325
  16.4 0.0 collective-permute-done
  16.4 2.5 %all_gather.13.other_ref = bf16[27,48,384]{2,1,0:T(8,128)(2,1)S(1)} all-gather(bf16[27,24,384]{2,1,0:T(8,128)(2,1)S(1)} %collective-permute-done), channel_id=1, replica_groups=mesh['y'=8,'core'=2,'z'=8,'x'=4] {'core'}, dimensions={1}, use_global_device_ids=true | all-gather | bytes 1492992 | tf_op jit(solution)/shard_map/all_gather | solution.py:326
  19.0 4.4 %all-to-all-done = bf16[8,96,128]{2,1,0:T(8,128)(2,1)S(1)} async-done(((bf16[8,96,128]{2,1,0:T(8,128)(2,1)}), bf16[8,96,128]{2,1,0:T(8,128)(2,1)S(1)}, u32[]{:S(2)}, u32[]{:S(2)}) %all-to-all-start) | async-done | bytes 196640 | tf_op jit(solution)/shard_map/all_to_all | solution.py:296
  23.4 2.1 %all-gather = bf16[16,96,128]{2,1,0:T(8,128)(2,1)S(1)} all-gather(bf16[8,96,128]{2,1,0:T(8,128)(2,1)S(1)} %all-to-all-done), channel_id=2, replica_groups=mesh['y'=8,'core'=2,'z'=8,'x'=4] {'core'}, dimensions={0}, use_global_device_ids=true | all-gather | bytes 589824 | tf_op jit(solution)/shard_map/all_gather | solution.py:331
  25.5 0.3 shard_map.65
  25.8 3.4 %collective-permute-start.1 = (bf16[2,2,96,128]{3,2,1,0:T(8,128)(2,1)S(1)}, bf16[2,2,96,128]{3,2,1,0:T(8,128)(2,1)S(1)}, u32[]{:S(2)}, u32[]{:S(2)}) collective-permute-start(bf16[2,2,96,128]{3,2,1,0:T(8,128)(2,1)S(1)} %shard_map.65), channel_id=1, source_target_pairs={{0,1},{1,2},{2,3},{3,4},{4,5},{5,6},{6,7},{7,8},{8,9},{9,10},{10,1... | collective-permute-start | bytes 294920 | tf_op jit(solution)/shard_map/ppermute | solution.py:292
  29.2 3.5 %shard_map.66.part_ref = f32[8,2,2,16,384]{4,3,2,1,0:T(8,128)S(1)} custom-call(bf16[2,8,96,128]{3,2,1,0:T(8,128)(2,1)S(1)} %bitcast.12, bf16[27,48,384]{2,1,0:T(8,128)(2,1)S(1)} %all_gather.12.own_ref, bf16[27,48,384]{2,1,0:T(8,128)(2,1)S(1)} %all_gather.13.other_ref), custom_call_target="tpu_custom_call" | custom-call | tf_op jit(solution)/shard_map/pallas_call | solution.py:301
  32.7 3.1 %collective-permute-done.1.edge_ref = bf16[2,2,96,128]{3,2,1,0:T(8,128)(2,1)S(1)} collective-permute-done((bf16[2,2,96,128]{3,2,1,0:T(8,128)(2,1)S(1)}, bf16[2,2,96,128]{3,2,1,0:T(8,128)(2,1)S(1)}, u32[]{:S(2)}, u32[]{:S(2)}) %collective-permute-start.1) | collective-permute-done | bytes 98336 | tf_op jit(solution)/shard_map/ppermute | solution.py:292
  35.8 2.5 %shard_map.67 = bf16[8,64,384]{2,1,0:T(8,128)(2,1)} custom-call(bf16[2,2,96,128]{3,2,1,0:T(8,128)(2,1)S(1)} %collective-permute-done.1.edge_ref, f32[8,2,2,16,384]{4,3,2,1,0:T(8,128)S(1)} %shard_map.66.part_ref, bf16[27,48,384]{2,1,0:T(8,128)(2,1)S(1)} %all_gather.12.own_ref, bf16[27,48,384]{2,1,0:T(8,128)(2,1)S(1)} %all_gather.13.other_ref), custom_call_target="tpu_custom_call" | custom-call | tf_op jit(solution)/shard_map/pallas_call | solution.py:301
  38.3 0.0 copy-start
  38.3 0.0 copy-start.1
  38.3 7.3 %all-to-all-start.1 = ((bf16[8,64,384]{2,1,0:T(8,128)(2,1)}), bf16[8,64,384]{2,1,0:T(8,128)(2,1)S(1)}, u32[]{:S(2)}, u32[]{:S(2)}) async-start(bf16[8,64,384]{2,1,0:T(8,128)(2,1)} %shard_map.67), calls=%async_computation.1 | async-start | bytes 786432 | tf_op jit(solution)/shard_map/all_to_all | solution.py:296
  45.7 2.0 %pad_maximum_fusion.later_ref.weight_ref = bf16[9,384,384]{2,1,0:T(8,128)(2,1)S(1)} fusion(bf16[9,192,384]{2,1,0:T(8,128)(2,1)} %bitcast.13), kind=kLoop, calls=%fused_computation | loop fusion | flops 5308416 | bytes 3981312 | tf_op jit(solution)/shard_map/concatenate | solution.py:328
  47.7 6.8 %all-to-all-done.1.part_ref = bf16[8,64,384]{2,1,0:T(8,128)(2,1)S(1)} async-done(((bf16[8,64,384]{2,1,0:T(8,128)(2,1)}), bf16[8,64,384]{2,1,0:T(8,128)(2,1)S(1)}, u32[]{:S(2)}, u32[]{:S(2)}) %all-to-all-start.1) | async-done | bytes 393248 | tf_op jit(solution)/shard_map/all_to_all | solution.py:296
  54.4 0.0 copy-done
  54.4 0.0 copy-done.1
  54.5 0.1 shard_map.68.block_ref
  54.5 0.0 copy-start.2
  54.6 3.6 %collective-permute-start.3 = (bf16[2,16,384]{2,1,0:T(8,128)(2,1)S(1)}, bf16[2,16,384]{2,1,0:T(8,128)(2,1)S(1)}, u32[]{:S(2)}, u32[]{:S(2)}) collective-permute-start(bf16[2,16,384]{2,1,0:T(8,128)(2,1)S(1)} %get-tuple-element.17), channel_id=1, source_target_pairs={{1,0},{2,1},{3,2},{4,3},{5,4},{6,5},{7,6},{8,7},{9,8},{10,9},{11,1... | collective-permute-start | bytes 73736 | tf_op jit(solution)/shard_map/ppermute | solution.py:279
  58.2 2.3 %collective-permute-start.2 = (bf16[2,16,384]{2,1,0:T(8,128)(2,1)S(1)}, bf16[2,16,384]{2,1,0:T(8,128)(2,1)S(1)}, u32[]{:S(2)}, u32[]{:S(2)}) collective-permute-start(bf16[2,16,384]{2,1,0:T(8,128)(2,1)S(1)} %get-tuple-element.18), channel_id=1, source_target_pairs={{0,1},{1,2},{2,3},{3,4},{4,5},{5,6},{6,7},{7,8},{8,9},{9,10},{10,1... | collective-permute-start | bytes 73736 | tf_op jit(solution)/shard_map/ppermute | solution.py:278
  60.4 1.4 %shard_map.69.inner_ref = f32[16,16,1152]{2,1,0:T(8,128)S(1)} custom-call(bf16[2,4,16,384]{3,2,1,0:T(8,128)(2,1)S(1)} %shard_map.68.block_ref, bf16[9,384,384]{2,1,0:T(8,128)(2,1)S(1)} %pad_maximum_fusion.later_ref.weight_ref), custom_call_target="tpu_custom_call" | custom-call | tf_op jit(solution)/shard_map/pallas_call | solution.py:301
  61.9 0.0 collective-permute-done.3.down_ref
  61.9 5.3 %collective-permute-done.2.up_ref = bf16[2,16,384]{2,1,0:T(8,128)(2,1)S(1)} collective-permute-done((bf16[2,16,384]{2,1,0:T(8,128)(2,1)S(1)}, bf16[2,16,384]{2,1,0:T(8,128)(2,1)S(1)}, u32[]{:S(2)}, u32[]{:S(2)}) %collective-permute-start.2) | collective-permute-done | bytes 24608 | tf_op jit(solution)/shard_map/ppermute | solution.py:278
  67.2 0.0 copy-done.2
  67.2 1.5 %shard_map.70 = bf16[16,6144]{1,0:T(8,128)(2,1)} custom-call(bf16[2,16,384]{2,1,0:T(8,128)(2,1)S(1)} %collective-permute-done.2.up_ref, bf16[2,16,384]{2,1,0:T(8,128)(2,1)S(1)} %collective-permute-done.3.down_ref, f32[16,16,1152]{2,1,0:T(8,128)S(1)} %shard_map.69.inner_ref, bf16[9,384,384]{2,1,0:T(8,128)(2,1)S(1)} %pad_maximum_fusion.later_ref.weight_ref, ...), custom_call_target="tpu_custom_call" | custom-call | tf_op jit(solution)/shard_map/pallas_call | solution.py:301
  (1 shorter events, 0.0 us)
Async XLA Ops:
  0.0 16.4 %collective-permute-start = (bf16[27,24,384]{2,1,0:T(8,128)(2,1)}, bf16[27,24,384]{2,1,0:T(8,128)(2,1)S(1)}, u32[]{:S(2)}, u32[]{:S(2)}) collective-permute-start(bf16[27,24,384]{2,1,0:T(8,128)(2,1)} %param.8), channel_id=1, source_target_pairs={{0,64},{64,0},{128,192},{192,128},{256,320},{320,256},{384,448},{4... | collective-permute-start | bytes 1493000 | tf_op jit(solution)/shard_map/ppermute | solution.py:312
  5.5 17.9 %all-to-all-start = ((bf16[8,96,128]{2,1,0:T(8,128)(2,1)}), bf16[8,96,128]{2,1,0:T(8,128)(2,1)S(1)}, u32[]{:S(2)}, u32[]{:S(2)}) async-start(bf16[8,96,128]{2,1,0:T(8,128)(2,1)} %shard_map.64), calls=%async_computation | async-start | bytes 393216 | tf_op jit(solution)/shard_map/all_to_all | solution.py:296
  25.8 10.1 %collective-permute-start.1 = (bf16[2,2,96,128]{3,2,1,0:T(8,128)(2,1)S(1)}, bf16[2,2,96,128]{3,2,1,0:T(8,128)(2,1)S(1)}, u32[]{:S(2)}, u32[]{:S(2)}) collective-permute-start(bf16[2,2,96,128]{3,2,1,0:T(8,128)(2,1)S(1)} %shard_map.65), channel_id=1, source_target_pairs={{0,1},{1,2},{2,3},{3,4},{4,5},{5,6},{6,7},{7,8},{8,9},{9,10},{10,1... | collective-permute-start | bytes 294920 | tf_op jit(solution)/shard_map/ppermute | solution.py:292
  38.3 16.2 %copy-start = (bf16[2,4,16,384]{3,2,1,0:T(8,128)(2,1)S(1)}, bf16[2,4,16,384]{3,2,1,0:T(8,128)(2,1)}, u32[]{:S(2)}) copy-start(bf16[2,4,16,384]{3,2,1,0:T(8,128)(2,1)} %lat_ref.3) | copy-start | bytes 294916
  38.3 16.2 %copy-start.1 = (f32[384]{0:T(512)S(1)}, f32[384]{0:T(512)}, u32[]{:S(2)}) copy-start(f32[384]{0:T(512)} %bias_ref.2) | copy-start | bytes 4612
  38.3 16.1 %all-to-all-start.1 = ((bf16[8,64,384]{2,1,0:T(8,128)(2,1)}), bf16[8,64,384]{2,1,0:T(8,128)(2,1)S(1)}, u32[]{:S(2)}, u32[]{:S(2)}) async-start(bf16[8,64,384]{2,1,0:T(8,128)(2,1)} %shard_map.67), calls=%async_computation.1 | async-start | bytes 786432 | tf_op jit(solution)/shard_map/all_to_all | solution.py:296
  54.5 12.7 %copy-start.2 = (f32[192]{0:T(256)S(1)}, f32[192]{0:T(256)}, u32[]{:S(2)}) copy-start(f32[192]{0:T(256)} %bias_ref.3) | copy-start | bytes 2308
  54.6 7.3 %collective-permute-start.3 = (bf16[2,16,384]{2,1,0:T(8,128)(2,1)S(1)}, bf16[2,16,384]{2,1,0:T(8,128)(2,1)S(1)}, u32[]{:S(2)}, u32[]{:S(2)}) collective-permute-start(bf16[2,16,384]{2,1,0:T(8,128)(2,1)S(1)} %get-tuple-element.17), channel_id=1, source_target_pairs={{1,0},{2,1},{3,2},{4,3},{5,4},{6,5},{7,6},{8,7},{9,8},{10,9},{11,1... | collective-permute-start | bytes 73736 | tf_op jit(solution)/shard_map/ppermute | solution.py:279
  58.2 9.0 %collective-permute-start.2 = (bf16[2,16,384]{2,1,0:T(8,128)(2,1)S(1)}, bf16[2,16,384]{2,1,0:T(8,128)(2,1)S(1)}, u32[]{:S(2)}, u32[]{:S(2)}) collective-permute-start(bf16[2,16,384]{2,1,0:T(8,128)(2,1)S(1)} %get-tuple-element.18), channel_id=1, source_target_pairs={{0,1},{1,2},{2,3},{3,4},{4,5},{5,6},{6,7},{7,8},{8,9},{9,10},{10,1... | collective-permute-start | bytes 73736 | tf_op jit(solution)/shard_map/ppermute | solution.py:278

commit v5 on v4

--- a/solution.py
+++ b/solution.py
@@ -28,7 +28,7 @@
 
 def window_picks(half):
     lane = lax.broadcasted_iota(jnp.int32, (1, 18 * CELLS), 1)
-    tap, frame, row, col = lane >> 7, (lane >> 5) & 3, (lane >> 4) & 1, lane & 15
+    tap, frame, row, col = lane >> 7, (lane >> 5) & 3, ((lane >> 4) & 1) ^ half, lane & 15
     dy = (tap * 11) >> 5
     col = col + tap - 3 * dy - 1
     row = row + dy - 1 + 2 * half
@@ -38,10 +38,10 @@
     return one_hot(wanted, lax.broadcasted_iota(jnp.int32, (2 * SENT, 18 * CELLS), 0))
 
 
-def edge_picks(shift):
+def edge_picks():
     lane = lax.broadcasted_iota(jnp.int32, (1, 3 * EDGE), 1)
     col = (lane & 15) + (lane >> 8) - 1
-    wanted = (((lane >> 4) & 15) << 4) + col - shift
+    wanted = (((lane >> 4) & 15) << 4) + col
     wanted = jnp.where((col >= 0) & (col < COLS), wanted, -1)
     return one_hot(wanted, lax.broadcasted_iota(jnp.int32, (EDGE, 3 * EDGE), 0))
 
@@ -82,8 +82,14 @@
         out_ref[SLOT[y]] = flipped[start : start + 2 * PART]
 
 
+def places():
+    mine = lax.axis_index("y") & 1
+    return lax.axis_index("core"), mine, mine ^ (lax.axis_index("x") & 1)
+
+
 def pack_kernel(act_ref, out_ref):
-    row = (ROWS - 1) * (1 - (lax.axis_index("y") & 1))
+    _, _, half = places()
+    row = (ROWS - 1) * half
     lane = lax.broadcasted_iota(jnp.int32, (1, SENT), 1)
     wanted = ((lane >> 4) << 6) + (row << 4) + (lane & 15)
     picks = one_hot(wanted, lax.broadcasted_iota(jnp.int32, (4 * SENT, SENT), 0))
@@ -94,12 +100,12 @@
             out_ref[core, group] = packed.astype(BF16)
 
 
-def weight_dots(blocks, weights, half):
+def weight_dots(blocks, weights, mine):
     total = None
     for i in range(2):
         rows = blocks.shape[1]
         part = lax.dot_general(
-            blocks[half if i == 0 else 1 - half],
+            blocks[mine if i == 0 else 1 - mine],
             weights[i].reshape(rows, CHANS),
             TN_DIMS,
             preferred_element_type=F32,
@@ -108,8 +114,19 @@
     return total
 
 
-def inner_kernel(act_ref, own_ref, other_ref, out_ref, here, before, windows, weights, arrived):
-    core, half = lax.axis_index("core"), lax.axis_index("y") & 1
+def inner_kernel(
+    act_ref,
+    own_ref,
+    other_ref,
+    out_ref,
+    taps_ref,
+    here,
+    before,
+    windows,
+    weights,
+    arrived,
+):
+    core, mine, half = places()
     copies = [
         pltpu.make_async_copy(ref, weights.at[i], arrived.at[i])
         for i, ref in enumerate((own_ref, other_ref))
@@ -154,64 +171,74 @@
                     ] = taken[row : row + PART]
     for copy in copies:
         copy.wait()
-    sums = weight_dots(windows, weights, half)
+    for i in range(2):
+        for dt in range(3):
+            taps_ref[i, dt] = weights[i, pl.ds(9 * dt + 6 * half, 3)]
+    sums = weight_dots(windows, weights, mine)
     out_ref[...] = sums.reshape(out_ref.shape)
 
 
-def edge_kernel(edge_ref, part_ref, own_ref, other_ref, out_ref, windows, weights, arrived):
-    core, half = lax.axis_index("core"), lax.axis_index("y") & 1
-    copies = []
-    for i, ref in enumerate((own_ref, other_ref)):
-        for dt in range(3):
-            taps = ref.at[pl.ds(9 * dt + 6 * half, 3)]
-            copies.append(pltpu.make_async_copy(taps, weights.at[i, dt], arrived.at[i, dt]))
-    for copy in copies:
-        copy.start()
-
-    def windows_of(which, shift):
-        block = jnp.concatenate([edge_ref[which, 0], edge_ref[which, 1]], axis=1)
-        return jnp.dot(block, edge_picks(shift), preferred_element_type=F32)
-
-    earliest = windows_of(1 - core, 2 * COLS * (1 - core))
-    latest = windows_of(core, 0)
+def edge_kernel(edge_ref, part_ref, taps_ref, out_ref, windows):
+    core, mine, half = places()
+
+    def line_of(which):
+        return jnp.concatenate([edge_ref[which, 0], edge_ref[which, 1]], axis=1)
+
+    chip = 2 * COLS
+    prior = line_of(1 - core).astype(F32)
+    lane = lax.broadcasted_iota(jnp.int32, prior.shape, 1)
+    later = jnp.where(lane < chip, 0.0, pltpu.roll(prior, chip, 1))
+    prior = jnp.where(core == 0, later, prior).astype(BF16)
+    both = jnp.concatenate([prior, line_of(core)], axis=0)
+    taken = jnp.dot(both, edge_picks(), preferred_element_type=F32)
     frame = (lax.broadcasted_iota(jnp.int32, (2 * PART, EDGE), 1) >> 4) & 1
     for dx in range(3):
-        first = earliest[:, dx * EDGE : (dx + 1) * EDGE]
-        last = latest[:, dx * EDGE : (dx + 1) * EDGE]
+        first = taken[: 2 * PART, dx * EDGE : (dx + 1) * EDGE]
+        last = taken[2 * PART :, dx * EDGE : (dx + 1) * EDGE]
         middle = jnp.where(
             frame == 0, pltpu.roll(first, EDGE - COLS, 1), pltpu.roll(last, COLS, 1)
         )
-        for dt, taken in enumerate((first, middle, last)):
-            taken = taken.astype(BF16)
+        for dt, window in enumerate((first, middle, last)):
+            window = window.astype(BF16)
             for part in range(2):
                 row = (3 * dt + dx) * PART
-                windows[part, row : row + PART] = taken[part * PART : (part + 1) * PART]
-    for copy in copies:
-        copy.wait()
-    sums = weight_dots(windows, weights, half)
+                windows[part, row : row + PART] = window[part * PART : (part + 1) * PART]
+    sums = weight_dots(windows, taps_ref, mine)
     for y in range(LINE):
         for f in range(FRAMES):
-            beside = sums[(2 * y + f) * COLS : (2 * y + f + 1) * COLS]
-            for r in range(HALF):
-                value = part_ref[y, f, r] + jnp.where(half == r, beside, 0.0)
-                row = (f * HALF + r) * COLS
-                out_ref[SLOT[y], row : row + COLS] = value.astype(BF16)
-
-
-def block_kernel(part_ref, lat_ref, bias_ref, later_ref, out_ref):
+            start = (2 * y + f) * COLS
+            border = part_ref[y, f, 0] + sums[start : start + COLS]
+            row = f * HALF * COLS
+            out_ref[SLOT[y], row : row + COLS] = border.astype(BF16)
+            out_ref[SLOT[y], row + COLS : row + 2 * COLS] = part_ref[y, f, 1].astype(BF16)
+
+
+def block_kernel(part_ref, lat_ref, bias_ref, later_ref, out_ref, far_ref, near_ref):
     del later_ref
     bias = bias_ref[...].reshape(1, CHANS)
-    for half in range(2):
-        total = part_ref[SLOT[half]].astype(F32)
-        for y in range(half + 2, LINE, 2):
+    odd = lax.axis_index("x") & 1
+    for mine in range(2):
+        total = part_ref[SLOT[mine]].astype(F32)
+        for y in range(mine + 2, LINE, 2):
             total = total + part_ref[SLOT[y]].astype(F32)
         total = total + bias
-        size = HALF * COLS
+        half = mine ^ odd
         for f in range(FRAMES):
-            rows = slice(half * HALF, (half + 1) * HALF)
-            skip = lat_ref[f, rows].reshape(size, CHANS).astype(F32)
-            value = (skip + total[f * size : (f + 1) * size]).astype(BF16)
-            out_ref[f, rows] = value.reshape(HALF, COLS, CHANS)
+            for inside in range(HALF):
+                row = half * HALF + (inside ^ half)
+                start = (f * HALF + inside) * COLS
+                value = lat_ref[f, row].astype(F32) + total[start : start + COLS]
+                out_ref[f, row] = value.astype(BF16)
+
+    @pl.when(odd == 1)
+    def _():
+        far_ref[...] = out_ref[:, ROWS - 1]
+        near_ref[...] = out_ref[:, 0]
+
+    @pl.when(odd == 0)
+    def _():
+        far_ref[...] = out_ref[:, 0]
+        near_ref[...] = out_ref[:, ROWS - 1]
 
 
 def upper_inner_kernel(block_ref, weight_ref, out_ref):
@@ -231,19 +258,24 @@
     out_ref[...] = total.reshape(out_ref.shape)
 
 
-def upper_kernel(up_ref, down_ref, inner_ref, weight_ref, bias_ref, out_ref):
+def upper_kernel(far_ref, near_ref, inner_ref, weight_ref, bias_ref, out_ref):
     wide = 2 * OUTS
     lines = FRAMES * 2 * ROWS
 
-    def taps(ref, dy):
+    far = far_ref[...].reshape(FRAMES * COLS, CHANS).astype(F32)
+    near = near_ref[...].reshape(FRAMES * COLS, CHANS).astype(F32)
+    odd = lax.axis_index("x") & 1
+
+    def taps(row, dy):
         return lax.dot_general(
-            ref[...].reshape(FRAMES * COLS, CHANS),
+            row.astype(BF16),
             weight_ref[3 * dy : 3 * dy + 3].reshape(3 * wide, CHANS),
             NT_DIMS,
             preferred_element_type=F32,
         )
 
-    above, below = taps(up_ref, 0), taps(down_ref, 2)
+    above = taps(jnp.where(odd == 1, near, far), 0)
+    below = taps(jnp.where(odd == 1, far, near), 2)
     line = lax.broadcasted_iota(jnp.int32, (lines, 3 * wide), 0)
     totals = []
     for c in range(COLS):
@@ -270,39 +302,35 @@
         out_ref[:, c * wide : (c + 1) * wide] = value.astype(BF16)
 
 
-def row_neighbours(block):
+def swapped(row, first):
     axes = ("z", "x")
-    count = lax.axis_size(axes)
-    down = [(i, i + 1) for i in range(count - 1)]
-    up = [(i + 1, i) for i in range(count - 1)]
-    above = lax.ppermute(block[:, ROWS - 1], axes, down)
-    below = lax.ppermute(block[:, 0], axes, up)
-    return above, below
+    pairs = []
+    for i in range(first, lax.axis_size(axes) - 1, 2):
+        pairs += [(i, i + 1), (i + 1, i)]
+    return lax.ppermute(row, axes, pairs)
 
 
 def row_beside(edges):
-    axes = ("y", "z", "x")
     count = lax.axis_size(("z", "x"))
     pairs = []
     for y in range(LINE):
-        for i in range(count):
-            j = i + 1 if y % 2 == 0 else i - 1
-            if 0 <= j < count:
-                pairs.append((y * count + i, y * count + j))
-    return lax.ppermute(edges, axes, pairs)
+        for i in range(1 - y % 2, count - 1, 2):
+            here, there = y * count + i, y * count + i + 1
+            pairs += [(here, there), (there, here)]
+    return lax.ppermute(edges, ("y", "z", "x"), pairs)
 
 
 def along_line(blocks):
     return lax.all_to_all(blocks, "y", 0, 0, tiled=True, axis_index_groups=[list(ORDER)])
 
 
-def call(kernel, shape, inputs, scratch=(), kind=BF16, limit=16):
+def call(kernel, outs, inputs, scratch=(), limit=16):
     spaces = [pltpu.HBM if far else pltpu.VMEM for _, far in inputs]
     return pl.pallas_call(
         kernel,
-        out_shape=jax.ShapeDtypeStruct(shape, kind),
+        out_shape=[jax.ShapeDtypeStruct(shape, kind) for shape, kind in outs],
         in_specs=[pl.BlockSpec(memory_space=space) for space in spaces],
-        out_specs=pl.BlockSpec(memory_space=pltpu.VMEM),
+        out_specs=[pl.BlockSpec(memory_space=pltpu.VMEM) for _ in outs],
         scratch_shapes=list(scratch),
         compiler_params=pltpu.CompilerParams(vmem_limit_bytes=limit * 1024 * 1024),
     )(*[array for array, _ in inputs])
@@ -310,9 +338,9 @@
 
 def local(latent, gain_first, conv_first, bias_first, conv_upper, bias_upper):
     other = lax.ppermute(conv_first, "y", [(i, i ^ 1) for i in range(LINE)])
-    acts = call(
+    (acts,) = call(
         act_kernel,
-        (LINE, 2 * PART, SENT),
+        [((LINE, 2 * PART, SENT), BF16)],
         [(latent, True), (gain_first, True)],
         [
             pltpu.VMEM(latent.shape, BF16),
@@ -329,10 +357,11 @@
     acts = along_line(acts)
     acts, own, other = lax.optimization_barrier((acts, own, other))
     acts = lax.all_gather(acts, "core", axis=0, tiled=False)
-    edges = row_beside(call(pack_kernel, (2, 2, 2 * PART, SENT), [(acts, False)]))
-    parts = call(
+    (edges,) = call(pack_kernel, [((2, 2, 2 * PART, SENT), BF16)], [(acts, False)])
+    edges = row_beside(edges)
+    parts, taps = call(
         inner_kernel,
-        (LINE, FRAMES, HALF, COLS, CHANS),
+        [((LINE, FRAMES, HALF, COLS, CHANS), F32), ((2, 3, 3, PART, CHANS), BF16)],
         [(acts, False), (own, True), (other, True)],
         [
             pltpu.VMEM((PAIRS, 2 * PART, 2 * SENT), BF16),
@@ -341,36 +370,31 @@
             pltpu.VMEM((2, 27, PART, CHANS), BF16),
             pltpu.SemaphoreType.DMA((2,)),
         ],
-        kind=F32,
         limit=32,
     )
-    parts = call(
+    (parts,) = call(
         edge_kernel,
-        (LINE, CELLS, CHANS),
-        [(edges, False), (parts, False), (own, True), (other, True)],
-        [
-            pltpu.VMEM((2, 9 * PART, EDGE), BF16),
-            pltpu.VMEM((2, 3, 3, PART, CHANS), BF16),
-            pltpu.SemaphoreType.DMA((2, 3)),
-        ],
+        [((LINE, CELLS, CHANS), BF16)],
+        [(edges, False), (parts, False), (taps, False)],
+        [pltpu.VMEM((2, 9 * PART, EDGE), BF16)],
     )
     parts = along_line(parts)
-    block = call(
+    row = ((FRAMES, COLS, CHANS), BF16)
+    block, far, near = call(
         block_kernel,
-        (FRAMES, ROWS, COLS, CHANS),
+        [((FRAMES, ROWS, COLS, CHANS), BF16), row, row],
         [(parts, False), (latent, False), (bias_first, False), (upper, True)],
     )
-    above, below = row_neighbours(block)
-    inner = call(
+    far, near = swapped(far, 1), swapped(near, 0)
+    (inner,) = call(
         upper_inner_kernel,
-        (COLS, FRAMES * 2 * ROWS, 6 * OUTS),
+        [((COLS, FRAMES * 2 * ROWS, 6 * OUTS), F32)],
         [(block, False), (upper, False)],
-        kind=F32,
-    )
-    out = call(
+    )
+    (out,) = call(
         upper_kernel,
-        (FRAMES * 2 * ROWS, 2 * COLS * OUTS),
-        [(array, False) for array in (above, below, inner, upper, bias_upper)],
+        [((FRAMES * 2 * ROWS, 2 * COLS * OUTS), BF16)],
+        [(array, False) for array in (far, near, inner, upper, bias_upper)],
     )
     return out.reshape(FRAMES, 2 * ROWS, 2 * COLS * OUTS)
 

time: 69.1 us -> 66.8 us (0.967)
  the two profiles are of different devices: /device:TPU:256 before, /device:TPU:198 now
where the time goes in v5:
time: 66.8 us; the launch traced here: 66.3 us
  starting transfers between devices  31.8 us (48%)
  waiting for transfers between devices  14.6 us (22%)
  Pallas kernels  10.5 us (16%)
  blocking collectives  7.3 us (11%)
  other arithmetic  2.02 us (3%)
    all_to_all x2, starting transfers between devices, along_line(): lax.all_to_all(blocks, 'y', 0, 0, tiled=True, axis_index_groups=[list(ORD...  15.6 us
    all_to_all x2, waiting for transfers between devices, along_line(): lax.all_to_all(blocks, 'y', 0, 0, tiled=True, axis_index_groups=[list(ORD...  11.2 us
    pallas_call x7, Pallas kernels, call(): pl.pallas_call(kernel, out_shape=[jax.ShapeDtypeStruct(shape, kind) for s...  10.5 us
    ppermute x2, starting transfers between devices, swapped(): return lax.ppermute(row, axes, pairs)  7.33 us
    ppermute x1, starting transfers between devices, row_beside(): return lax.ppermute(edges, ('y', 'z', 'x'), pairs)  5.41 us
    ppermute x1, starting transfers between devices, local(): other = lax.ppermute(conv_first, 'y', [(i, i ^ 1) for i in range(LINE)])  3.47 us
    all_gather x1, blocking collectives, local(): own = lax.all_gather(conv_first, 'core', axis=1, tiled=True)  2.72 us
    all_gather x1, blocking collectives, local(): other = lax.all_gather(other, 'core', axis=1, tiled=True)  2.51 us
  transfers between devices with their start and end apart: 6, of which 5 were waited for; matrix products, arithmetic and copies ran while one was open for 3% of the time, Pallas kernels for 11%

profile of v5, /device:TPU:198, one launch (start us, length us, event | category | flops | bytes accessed | tf_op | source)
XLA Modules:
  0.0 66.3 jit_solution(17131906347785915030)
XLA Ops:
  0.0 3.5 %collective-permute-start = (bf16[27,24,384]{2,1,0:T(8,128)(2,1)}, bf16[27,24,384]{2,1,0:T(8,128)(2,1)S(1)}, u32[]{:S(2)}, u32[]{:S(2)}) collective-permute-start(bf16[27,24,384]{2,1,0:T(8,128)(2,1)} %param.8), channel_id=1, source_target_pairs={{0,64},{64,0},{128,192},{192,128},{256,320},{320,256},{384,448},{4... | collective-permute-start | bytes 1493000 | tf_op jit(solution)/shard_map/ppermute | solution.py:340
  3.5 2.0 %shard_map.64 = bf16[8,96,128]{2,1,0:T(8,128)(2,1)} custom-call(bf16[2,4,16,384]{3,2,1,0:T(8,128)(2,1)} %lat_ref.3, f32[384]{0:T(512)} %gain_ref.1), custom_call_target="tpu_custom_call" | custom-call | tf_op jit(solution)/shard_map/pallas_call | solution.py:329
  5.5 8.3 %all-to-all-start = ((bf16[8,96,128]{2,1,0:T(8,128)(2,1)}), bf16[8,96,128]{2,1,0:T(8,128)(2,1)S(1)}, u32[]{:S(2)}, u32[]{:S(2)}) async-start(bf16[8,96,128]{2,1,0:T(8,128)(2,1)} %shard_map.64), calls=%async_computation | async-start | bytes 393216 | tf_op jit(solution)/shard_map/all_to_all | solution.py:324
  13.7 2.7 %all_gather.12.own_ref = bf16[27,48,384]{2,1,0:T(8,128)(2,1)S(1)} all-gather(bf16[27,24,384]{2,1,0:T(8,128)(2,1)} %param.8), channel_id=1, replica_groups=mesh['y'=8,'core'=2,'z'=8,'x'=4] {'core'}, dimensions={1}, use_global_device_ids=true | all-gather | bytes 1492992 | tf_op jit(solution)/shard_map/all_gather | solution.py:353
  16.4 0.0 collective-permute-done
  16.4 2.5 %all_gather.13.other_ref = bf16[27,48,384]{2,1,0:T(8,128)(2,1)S(1)} all-gather(bf16[27,24,384]{2,1,0:T(8,128)(2,1)S(1)} %collective-permute-done), channel_id=1, replica_groups=mesh['y'=8,'core'=2,'z'=8,'x'=4] {'core'}, dimensions={1}, use_global_device_ids=true | all-gather | bytes 1492992 | tf_op jit(solution)/shard_map/all_gather | solution.py:354
  19.0 4.4 %all-to-all-done = bf16[8,96,128]{2,1,0:T(8,128)(2,1)S(1)} async-done(((bf16[8,96,128]{2,1,0:T(8,128)(2,1)}), bf16[8,96,128]{2,1,0:T(8,128)(2,1)S(1)}, u32[]{:S(2)}, u32[]{:S(2)}) %all-to-all-start) | async-done | bytes 196640 | tf_op jit(solution)/shard_map/all_to_all | solution.py:324
  23.4 2.1 %all-gather = bf16[16,96,128]{2,1,0:T(8,128)(2,1)S(1)} all-gather(bf16[8,96,128]{2,1,0:T(8,128)(2,1)S(1)} %all-to-all-done), channel_id=2, replica_groups=mesh['y'=8,'core'=2,'z'=8,'x'=4] {'core'}, dimensions={0}, use_global_device_ids=true | all-gather | bytes 589824 | tf_op jit(solution)/shard_map/all_gather | solution.py:359
  25.5 0.3 shard_map.65
  25.7 5.4 %collective-permute-start.1 = (bf16[2,2,96,128]{3,2,1,0:T(8,128)(2,1)S(1)}, bf16[2,2,96,128]{3,2,1,0:T(8,128)(2,1)S(1)}, u32[]{:S(2)}, u32[]{:S(2)}) collective-permute-start(bf16[2,2,96,128]{3,2,1,0:T(8,128)(2,1)S(1)} %shard_map.65), channel_id=1, source_target_pairs={{1,2},{2,1},{3,4},{4,3},{5,6},{6,5},{7,8},{8,7},{9,10},{10,9},{11,... | collective-permute-start | bytes 294920 | tf_op jit(solution)/shard_map/ppermute | solution.py:320
  31.2 3.6 %shard_map.66 = (f32[8,2,2,16,384]{4,3,2,1,0:T(8,128)S(1)}, bf16[2,3,3,48,384]{4,3,2,1,0:T(8,128)(2,1)S(1)}) custom-call(bf16[2,8,96,128]{3,2,1,0:T(8,128)(2,1)S(1)} %bitcast.4, bf16[27,48,384]{2,1,0:T(8,128)(2,1)S(1)} %all_gather.12.own_ref, bf16[27,48,384]{2,1,0:T(8,128)(2,1)S(1)} %all_gather.13.other_ref), custom_call_target="tpu_custom_call" | custom-call | tf_op jit(solution)/shard_map/pallas_call | solution.py:329
  34.8 1.0 %collective-permute-done.1.edge_ref = bf16[2,2,96,128]{3,2,1,0:T(8,128)(2,1)S(1)} collective-permute-done((bf16[2,2,96,128]{3,2,1,0:T(8,128)(2,1)S(1)}, bf16[2,2,96,128]{3,2,1,0:T(8,128)(2,1)S(1)}, u32[]{:S(2)}, u32[]{:S(2)}) %collective-permute-start.1) | collective-permute-done | bytes 98336 | tf_op jit(solution)/shard_map/ppermute | solution.py:320
  35.8 1.7 %shard_map.67 = bf16[8,64,384]{2,1,0:T(8,128)(2,1)} custom-call(bf16[2,2,96,128]{3,2,1,0:T(8,128)(2,1)S(1)} %collective-permute-done.1.edge_ref, f32[8,2,2,16,384]{4,3,2,1,0:T(8,128)S(1)} %get-tuple-element.21.part_ref, bf16[2,3,3,48,384]{4,3,2,1,0:T(8,128)(2,1)S(1)} %get-tuple-element.22.taps_ref), custom_call_target="tpu_custom_call" | custom-call | tf_op jit(solution)/shard_map/pallas_call | solution.py:329
  37.5 0.0 copy-start
  37.5 0.0 copy-start.1
  37.5 7.3 %all-to-all-start.1 = ((bf16[8,64,384]{2,1,0:T(8,128)(2,1)}), bf16[8,64,384]{2,1,0:T(8,128)(2,1)S(1)}, u32[]{:S(2)}, u32[]{:S(2)}) async-start(bf16[8,64,384]{2,1,0:T(8,128)(2,1)} %shard_map.67), calls=%async_computation.1 | async-start | bytes 786432 | tf_op jit(solution)/shard_map/all_to_all | solution.py:324
  44.8 2.0 %pad_maximum_fusion.later_ref.weight_ref = bf16[9,384,384]{2,1,0:T(8,128)(2,1)S(1)} fusion(bf16[9,192,384]{2,1,0:T(8,128)(2,1)} %bitcast.5), kind=kLoop, calls=%fused_computation | loop fusion | flops 5308416 | bytes 3981312 | tf_op jit(solution)/shard_map/concatenate | solution.py:356
  46.8 6.8 %all-to-all-done.1.part_ref = bf16[8,64,384]{2,1,0:T(8,128)(2,1)S(1)} async-done(((bf16[8,64,384]{2,1,0:T(8,128)(2,1)}), bf16[8,64,384]{2,1,0:T(8,128)(2,1)S(1)}, u32[]{:S(2)}, u32[]{:S(2)}) %all-to-all-start.1) | async-done | bytes 393248 | tf_op jit(solution)/shard_map/all_to_all | solution.py:324
  53.6 0.0 copy-done
  53.6 0.0 copy-done.1
  53.6 0.1 shard_map.68
  53.7 0.0 copy-start.2
  53.7 5.4 %collective-permute-start.2 = (bf16[2,16,384]{2,1,0:T(8,128)(2,1)S(1)}, bf16[2,16,384]{2,1,0:T(8,128)(2,1)S(1)}, u32[]{:S(2)}, u32[]{:S(2)}) collective-permute-start(bf16[2,16,384]{2,1,0:T(8,128)(2,1)S(1)} %get-tuple-element.24), channel_id=1, source_target_pairs={{1,2},{2,1},{3,4},{4,3},{5,6},{6,5},{7,8},{8,7},{9,10},{10,9},{11,... | collective-permute-start | bytes 73736 | tf_op jit(solution)/shard_map/ppermute | solution.py:310
  59.1 1.9 %collective-permute-start.3 = (bf16[2,16,384]{2,1,0:T(8,128)(2,1)S(1)}, bf16[2,16,384]{2,1,0:T(8,128)(2,1)S(1)}, u32[]{:S(2)}, u32[]{:S(2)}) collective-permute-start(bf16[2,16,384]{2,1,0:T(8,128)(2,1)S(1)} %get-tuple-element.25), channel_id=1, source_target_pairs={{0,1},{1,0},{2,3},{3,2},{4,5},{5,4},{6,7},{7,6},{8,9},{9,8},{10,11... | collective-permute-start | bytes 73736 | tf_op jit(solution)/shard_map/ppermute | solution.py:310
  61.1 1.4 %shard_map.69.inner_ref = f32[16,16,1152]{2,1,0:T(8,128)S(1)} custom-call(bf16[2,4,16,384]{3,2,1,0:T(8,128)(2,1)S(1)} %get-tuple-element.26.block_ref, bf16[9,384,384]{2,1,0:T(8,128)(2,1)S(1)} %pad_maximum_fusion.later_ref.weight_ref), custom_call_target="tpu_custom_call" | custom-call | tf_op jit(solution)/shard_map/pallas_call | solution.py:329
  62.5 0.2 collective-permute-done.2.far_ref
  62.7 2.1 %collective-permute-done.3.near_ref = bf16[2,16,384]{2,1,0:T(8,128)(2,1)S(1)} collective-permute-done((bf16[2,16,384]{2,1,0:T(8,128)(2,1)S(1)}, bf16[2,16,384]{2,1,0:T(8,128)(2,1)S(1)}, u32[]{:S(2)}, u32[]{:S(2)}) %collective-permute-start.3) | collective-permute-done | bytes 24608 | tf_op jit(solution)/shard_map/ppermute | solution.py:310
  64.8 0.0 copy-done.2
  64.8 1.5 %shard_map.70 = bf16[16,6144]{1,0:T(8,128)(2,1)} custom-call(bf16[2,16,384]{2,1,0:T(8,128)(2,1)S(1)} %collective-permute-done.2.far_ref, bf16[2,16,384]{2,1,0:T(8,128)(2,1)S(1)} %collective-permute-done.3.near_ref, f32[16,16,1152]{2,1,0:T(8,128)S(1)} %shard_map.69.inner_ref, bf16[9,384,384]{2,1,0:T(8,128)(2,1)S(1)} %pad_maximum_fusion.later_ref.weight_ref, ...), custom_call_target="tpu_custom_call" | custom-call | tf_op jit(solution)/shard_map/pallas_call | solution.py:329
Async XLA Ops:
  0.0 16.4 %collective-permute-start = (bf16[27,24,384]{2,1,0:T(8,128)(2,1)}, bf16[27,24,384]{2,1,0:T(8,128)(2,1)S(1)}, u32[]{:S(2)}, u32[]{:S(2)}) collective-permute-start(bf16[27,24,384]{2,1,0:T(8,128)(2,1)} %param.8), channel_id=1, source_target_pairs={{0,64},{64,0},{128,192},{192,128},{256,320},{320,256},{384,448},{4... | collective-permute-start | bytes 1493000 | tf_op jit(solution)/shard_map/ppermute | solution.py:340
  5.5 17.9 %all-to-all-start = ((bf16[8,96,128]{2,1,0:T(8,128)(2,1)}), bf16[8,96,128]{2,1,0:T(8,128)(2,1)S(1)}, u32[]{:S(2)}, u32[]{:S(2)}) async-start(bf16[8,96,128]{2,1,0:T(8,128)(2,1)} %shard_map.64), calls=%async_computation | async-start | bytes 393216 | tf_op jit(solution)/shard_map/all_to_all | solution.py:324
  25.7 10.1 %collective-permute-start.1 = (bf16[2,2,96,128]{3,2,1,0:T(8,128)(2,1)S(1)}, bf16[2,2,96,128]{3,2,1,0:T(8,128)(2,1)S(1)}, u32[]{:S(2)}, u32[]{:S(2)}) collective-permute-start(bf16[2,2,96,128]{3,2,1,0:T(8,128)(2,1)S(1)} %shard_map.65), channel_id=1, source_target_pairs={{1,2},{2,1},{3,4},{4,3},{5,6},{6,5},{7,8},{8,7},{9,10},{10,9},{11,... | collective-permute-start | bytes 294920 | tf_op jit(solution)/shard_map/ppermute | solution.py:320
  37.5 16.1 %copy-start = (bf16[2,4,16,384]{3,2,1,0:T(8,128)(2,1)S(1)}, bf16[2,4,16,384]{3,2,1,0:T(8,128)(2,1)}, u32[]{:S(2)}) copy-start(bf16[2,4,16,384]{3,2,1,0:T(8,128)(2,1)} %lat_ref.3) | copy-start | bytes 294916
  37.5 16.1 %copy-start.1 = (f32[384]{0:T(512)S(1)}, f32[384]{0:T(512)}, u32[]{:S(2)}) copy-start(f32[384]{0:T(512)} %bias_ref.2) | copy-start | bytes 4612
  37.5 16.1 %all-to-all-start.1 = ((bf16[8,64,384]{2,1,0:T(8,128)(2,1)}), bf16[8,64,384]{2,1,0:T(8,128)(2,1)S(1)}, u32[]{:S(2)}, u32[]{:S(2)}) async-start(bf16[8,64,384]{2,1,0:T(8,128)(2,1)} %shard_map.67), calls=%async_computation.1 | async-start | bytes 786432 | tf_op jit(solution)/shard_map/all_to_all | solution.py:324
  53.7 11.2 %copy-start.2 = (f32[192]{0:T(256)S(1)}, f32[192]{0:T(256)}, u32[]{:S(2)}) copy-start(f32[192]{0:T(256)} %bias_ref.3) | copy-start | bytes 2308
  53.7 9.0 %collective-permute-start.2 = (bf16[2,16,384]{2,1,0:T(8,128)(2,1)S(1)}, bf16[2,16,384]{2,1,0:T(8,128)(2,1)S(1)}, u32[]{:S(2)}, u32[]{:S(2)}) collective-permute-start(bf16[2,16,384]{2,1,0:T(8,128)(2,1)S(1)} %get-tuple-element.24), channel_id=1, source_target_pairs={{1,2},{2,1},{3,4},{4,3},{5,6},{6,5},{7,8},{8,7},{9,10},{10,9},{11,... | collective-permute-start | bytes 73736 | tf_op jit(solution)/shard_map/ppermute | solution.py:310
  59.1 5.7 %collective-permute-start.3 = (bf16[2,16,384]{2,1,0:T(8,128)(2,1)S(1)}, bf16[2,16,384]{2,1,0:T(8,128)(2,1)S(1)}, u32[]{:S(2)}, u32[]{:S(2)}) collective-permute-start(bf16[2,16,384]{2,1,0:T(8,128)(2,1)S(1)} %get-tuple-element.25), channel_id=1, source_target_pairs={{0,1},{1,0},{2,3},{3,2},{4,5},{5,4},{6,7},{7,6},{8,9},{9,8},{10,11... | collective-permute-start | bytes 73736 | tf_op jit(solution)/shard_map/ppermute | solution.py:310

commit v6 on v5

v6 whole, which is shorter than its diff:
```python
import jax
import jax.numpy as jnp
from jax import lax
from jax.experimental import pallas as pl
from jax.experimental.pallas import tpu as pltpu
from jax.sharding import Mesh
from jax.sharding import PartitionSpec as P

F32 = jnp.float32
BF16 = jnp.bfloat16
FRAMES, ROWS, COLS, CHANS, OUTS = 2, 4, 16, 384, 192
LINE = 8
PART = CHANS // LINE
PAIRS = LINE // 2
HALF = ROWS // 2
CELLS = FRAMES * HALF * COLS
SENT = FRAMES * ROWS * COLS
ORDER = (4, 5, 6, 7, 0, 1, 2, 3)
SLOT = tuple(ORDER.index(y) for y in range(LINE))
NT_DIMS = (((1,), (1,)), ((), ()))
TN_DIMS = (((0,), (0,)), ((), ()))


def one_hot(wanted, there):
    return jnp.where(wanted == there, 1.0, 0.0).astype(BF16)


def window_picks():
    lane = lax.broadcasted_iota(jnp.int32, (1, 18 * CELLS), 1)
    tap, frame, row, col = lane >> 7, (lane >> 5) & 3, (lane >> 4) & 1, lane & 15
    dy = (tap * 11) >> 5
    col = col + tap - 3 * dy - 1
    wanted = (frame << 6) + ((row + dy) << 4) + col
    wanted = jnp.where((col >= 0) & (col < COLS), wanted, -1)
    return one_hot(wanted, lax.broadcasted_iota(jnp.int32, (2 * SENT, 18 * CELLS), 0))


def row_picks():
    shape = (6 * ROWS * COLS * FRAMES, SENT)
    place = lax.broadcasted_iota(jnp.int32, (shape[0], 1), 0)
    dy, col, frame, i = place >> 8, (place >> 4) & 15, (place >> 3) & 1, place & 7
    row = ((i + dy + 1) >> 1) - 1
    wanted = (frame << 6) + (row << 4) + col
    wanted = jnp.where((row >= 0) & (row < ROWS), wanted, -1)
    return one_hot(wanted, lax.broadcasted_iota(jnp.int32, shape, 1))


def scaled_silu(block, gain):
    values = block.astype(F32)
    mean_square = jnp.mean(values * values, axis=-1, keepdims=True)
    scaled = values * lax.rsqrt(mean_square + 1e-06) * gain
    return scaled / (1.0 + jnp.exp(-scaled))


def own_kernel(lat_ref, gain_ref, out_ref):
    out_ref[...] = scaled_silu(
        lat_ref[...].reshape(SENT, CHANS), gain_ref[...].reshape(1, CHANS)
    )


def act_kernel(far_ref, near_ref, own_ref, gain_ref, out_ref):
    odd = lax.axis_index("x") & 1
    count = FRAMES * COLS
    far = far_ref[...].reshape(count, CHANS).astype(F32)
    near = near_ref[...].reshape(count, CHANS).astype(F32)
    edges = jnp.concatenate(
        [jnp.where(odd == 1, near, far), jnp.where(odd == 1, far, near)], axis=0
    )
    edges = scaled_silu(edges, gain_ref[...].reshape(1, CHANS))
    own = own_ref[...]
    size = (HALF + 1) * COLS
    for half in range(2):
        cells = []
        for f in range(FRAMES):
            start = (f * ROWS + half * (HALF - 1)) * COLS
            beside = (half * FRAMES + f) * COLS
            parts = [edges[beside : beside + COLS], own[start : start + size]]
            cells += parts if half == 0 else parts[::-1]
        flipped = jnp.concatenate(cells, axis=0).T.astype(BF16)
        for pair in range(PAIRS):
            start = pair * 2 * PART
            out_ref[SLOT[2 * pair + half]] = flipped[start : start + 2 * PART]


def weight_dots(blocks, weights, mine):
    total = None
    for i in range(2):
        rows = blocks.shape[1]
        part = lax.dot_general(
            blocks[mine if i == 0 else 1 - mine],
            weights[i][...].reshape(rows, CHANS),
            TN_DIMS,
            preferred_element_type=F32,
        )
        total = part if total is None else total + part
    return total


def inner_kernel(act_ref, own_ref, other_ref, out_ref, here, before, windows):
    core, mine = lax.axis_index("core"), lax.axis_index("y") & 1
    for y in range(LINE):
        where = (y // 2, slice(None), slice((y % 2) * SENT, (y % 2 + 1) * SENT))
        here[where] = act_ref[core, SLOT[y]]

        @pl.when(core == 1)
        def _():
            before[where] = act_ref[0, SLOT[y]]

        @pl.when(core == 0)
        def _():
            before[where] = act_ref[1, SLOT[y - 1]] if y else jnp.zeros_like(act_ref[1, 0])

    now = here[...].reshape(PAIRS * 2 * PART, 2 * SENT)
    prior = before[...].reshape(PAIRS * 2 * PART, 2 * SENT)
    picks = window_picks()
    earliest = jnp.dot(prior, picks, preferred_element_type=F32)
    latest = jnp.dot(now, picks, preferred_element_type=F32)
    lanes = 2 * CELLS
    step = lanes // 4
    frame = (lax.broadcasted_iota(jnp.int32, (PAIRS * 2 * PART, lanes), 1) >> 5) & 1
    for tap in range(9):
        first = earliest[:, tap * lanes : (tap + 1) * lanes]
        last = latest[:, tap * lanes : (tap + 1) * lanes]
        middle = jnp.where(
            frame == 0, pltpu.roll(first, lanes - step, 1), pltpu.roll(last, step, 1)
        )
        for dt, taken in enumerate((first, middle, last)):
            taken = taken.astype(BF16)
            for pair in range(PAIRS):
                for part in range(2):
                    row = (2 * pair + part) * PART
                    windows[
                        part,
                        (9 * dt + tap) * PART : (9 * dt + tap + 1) * PART,
                        pair * lanes : (pair + 1) * lanes,
                    ] = taken[row : row + PART]
    sums = weight_dots(windows, (own_ref, other_ref), mine).astype(BF16)
    for y in range(LINE):
        out_ref[SLOT[y]] = sums[y * CELLS : (y + 1) * CELLS]


def block_kernel(part_ref, lat_ref, bias_ref, later_ref, out_ref, far_ref, near_ref):
    del later_ref
    bias = bias_ref[...].reshape(1, CHANS)
    odd = lax.axis_index("x") & 1
    for half in range(2):
        total = part_ref[SLOT[half]].astype(F32)
        for y in range(half + 2, LINE, 2):
            total = total + part_ref[SLOT[y]].astype(F32)
        total = total + bias
        for f in range(FRAMES):
            for inside in range(HALF):
                row = half * HALF + inside
                start = (f * HALF + inside) * COLS
                value = lat_ref[f, row].astype(F32) + total[start : start + COLS]
                out_ref[f, row] = value.astype(BF16)

    @pl.when(odd == 1)
    def _():
        far_ref[...] = out_ref[:, ROWS - 1]
        near_ref[...] = out_ref[:, 0]

    @pl.when(odd == 0)
    def _():
        far_ref[...] = out_ref[:, 0]
        near_ref[...] = out_ref[:, ROWS - 1]


def upper_inner_kernel(block_ref, weight_ref, out_ref):
    rows = jnp.dot(
        row_picks(), block_ref[...].reshape(SENT, CHANS), preferred_element_type=F32
    ).astype(BF16)
    cells = COLS * FRAMES * 2 * ROWS
    total = None
    for dy in range(3):
        part = lax.dot_general(
            rows[dy * cells : (dy + 1) * cells],
            weight_ref[3 * dy : 3 * dy + 3].reshape(6 * OUTS, CHANS),
            NT_DIMS,
            preferred_element_type=F32,
        )
        total = part if total is None else total + part
    out_ref[...] = total.reshape(out_ref.shape)


def upper_kernel(far_ref, near_ref, inner_ref, weight_ref, bias_ref, out_ref):
    wide = 2 * OUTS
    lines = FRAMES * 2 * ROWS

    far = far_ref[...].reshape(FRAMES * COLS, CHANS).astype(F32)
    near = near_ref[...].reshape(FRAMES * COLS, CHANS).astype(F32)
    odd = lax.axis_index("x") & 1

    def taps(row, dy):
        return lax.dot_general(
            row.astype(BF16),
            weight_ref[3 * dy : 3 * dy + 3].reshape(3 * wide, CHANS),
            NT_DIMS,
            preferred_element_type=F32,
        )

    above = taps(jnp.where(odd == 1, near, far), 0)
    below = taps(jnp.where(odd == 1, far, near), 2)
    line = lax.broadcasted_iota(jnp.int32, (lines, 3 * wide), 0)
    totals = []
    for c in range(COLS):
        total = inner_ref[c]
        for f in range(FRAMES):
            row = f * COLS + c
            top, bottom = f * 2 * ROWS, (f + 1) * 2 * ROWS - 1
            total = total + jnp.where(line == top, above[row : row + 1], 0.0)
            total = total + jnp.where(line == bottom, below[row : row + 1], 0.0)
        totals.append(total)
    bias = bias_ref[...].reshape(1, OUTS)
    bias = jnp.concatenate([bias, bias], axis=1)
    left = lax.broadcasted_iota(jnp.int32, (lines, wide), 1) < OUTS
    zero = jnp.zeros((lines, wide), F32)
    for c in range(COLS):
        first_before = totals[c - 1][:, :wide] if c else zero
        last_after = totals[c + 1][:, 2 * wide :] if c < COLS - 1 else zero
        value = (
            jnp.where(left, first_before, totals[c][:, :wide])
            + totals[c][:, wide : 2 * wide]
            + jnp.where(left, totals[c][:, 2 * wide :], last_after)
            + bias
        )
        out_ref[:, c * wide : (c + 1) * wide] = value.astype(BF16)


def swapped(row, first):
    axes = ("z", "x")
    pairs = []
    for i in range(first, lax.axis_size(axes) - 1, 2):
        pairs += [(i, i + 1), (i + 1, i)]
    return lax.ppermute(row, axes, pairs)


def along_line(blocks):
    return lax.all_to_all(blocks, "y", 0, 0, tiled=True, axis_index_groups=[list(ORDER)])


def call(kernel, outs, inputs, scratch=(), limit=16):
    spaces = [pltpu.HBM if far else pltpu.VMEM for _, far in inputs]
    return pl.pallas_call(
        kernel,
        out_shape=[jax.ShapeDtypeStruct(shape, kind) for shape, kind in outs],
        in_specs=[pl.BlockSpec(memory_space=space) for space in spaces],
        out_specs=[pl.BlockSpec(memory_space=pltpu.VMEM) for _ in outs],
        scratch_shapes=list(scratch),
        compiler_params=pltpu.CompilerParams(vmem_limit_bytes=limit * 1024 * 1024),
    )(*[array for array, _ in inputs])


def local(latent, gain_first, conv_first, bias_first, conv_upper, bias_upper):
    odd = (lax.axis_index("x") & 1) == 1
    first, last = latent[:, 0], latent[:, ROWS - 1]
    far, near = jnp.where(odd, last, first), jnp.where(odd, first, last)
    far, near, conv_first = lax.optimization_barrier((far, near, conv_first))
    far, near = swapped(far, 1), swapped(near, 0)
    other = lax.ppermute(conv_first, "y", [(i, i ^ 1) for i in range(LINE)])
    (own_acts,) = call(
        own_kernel, [((SENT, CHANS), F32)], [(latent, False), (gain_first, False)]
    )
    (acts,) = call(
        act_kernel,
        [((LINE, 2 * PART, SENT), BF16)],
        [(array, False) for array in (far, near, own_acts, gain_first)],
    )
    acts, conv_first, conv_upper = lax.optimization_barrier((acts, conv_first, conv_upper))
    own = lax.all_gather(conv_first, "core", axis=1, tiled=True)
    other = lax.all_gather(other, "core", axis=1, tiled=True)
    upper = jnp.swapaxes(conv_upper, 1, 2)
    upper = jnp.concatenate([upper, upper], axis=1)
    acts = along_line(acts)
    acts, own, other = lax.optimization_barrier((acts, own, other))
    acts = lax.all_gather(acts, "core", axis=0, tiled=False)
    (parts,) = call(
        inner_kernel,
        [((LINE, CELLS, CHANS), BF16)],
        [(acts, False), (own, False), (other, False)],
        [
            pltpu.VMEM((PAIRS, 2 * PART, 2 * SENT), BF16),
            pltpu.VMEM((PAIRS, 2 * PART, 2 * SENT), BF16),
            pltpu.VMEM((2, 27 * PART, LINE * CELLS), BF16),
        ],
        limit=24,
    )
    parts = along_line(parts)
    row = ((FRAMES, COLS, CHANS), BF16)
    block, far, near = call(
        block_kernel,
        [((FRAMES, ROWS, COLS, CHANS), BF16), row, row],
        [(parts, False), (latent, False), (bias_first, False), (upper, True)],
    )
    far, near = swapped(far, 1), swapped(near, 0)
    (inner,) = call(
        upper_inner_kernel,
        [((COLS, FRAMES * 2 * ROWS, 6 * OUTS), F32)],
        [(block, False), (upper, False)],
    )
    (out,) = call(
        upper_kernel,
        [((FRAMES * 2 * ROWS, 2 * COLS * OUTS), BF16)],
        [(array, False) for array in (far, near, inner, upper, bias_upper)],
    )
    return out.reshape(FRAMES, 2 * ROWS, 2 * COLS * OUTS)


def solution(mesh):
    fine = Mesh(mesh.devices.reshape(8, 2, 8, 4), ("y", "core", "z", "x"))
    tm, rows = ("y", "core"), ("z", "x")
    in_specs = (P(tm, rows, None, None), P(), P(None, tm, None), P(), P(), P())
    return jax.shard_map(
        local, mesh=fine, in_specs=in_specs, out_specs=P(tm, rows, None), check_vma=False
    )
```

time: 66.8 us -> 65.3 us (0.978)
  Pallas kernels: 10.5 us -> 7.89 us
  waiting for transfers between devices: 14.6 us -> 12.3 us
  local copies, waits for them, and re-layouts: 0.01 us -> 1.58 us
  starting transfers between devices: 31.8 us -> 32.8 us
  other arithmetic: 2.02 us -> 2.78 us
    ppermute x2 -> x4, starting transfers between devices: 7.33 us -> 13 us  [swapped(): return lax.ppermute(row, axes, pairs)]
    ppermute x1 -> x0, starting transfers between devices: 5.41 us -> none  [row_beside(): return lax.ppermute(edges, ('y', 'z', 'x'), pairs)]
    all_to_all x2, waiting for transfers between devices: 11.2 us -> 7.87 us  [along_line(): lax.all_to_all(blocks, 'y', 0, 0, tiled=True, axis_index_groups=[list(ORD...]
    pallas_call x7 -> x6, Pallas kernels: 10.5 us -> 7.89 us  [call(): pl.pallas_call(kernel, out_shape=[jax.ShapeDtypeStruct(shape, kind) for s...]
    ppermute x2 -> x4, waiting for transfers between devices: 2.34 us -> 4.38 us  [swapped(): return lax.ppermute(row, axes, pairs)]
    unnamed x6 -> x10, local copies, waits for them, and re-layouts: 0.01 us -> 1.58 us
    ppermute x1 -> x0, waiting for transfers between devices: 1.05 us -> none  [row_beside(): return lax.ppermute(edges, ('y', 'z', 'x'), pairs)]
    select_n x0 -> x1, other arithmetic: none -> 0.77 us  [local(): far, near = (jnp.where(odd, last, first), jnp.where(odd, first, last))]
  transfers between devices with their start and end apart: 6 -> 7, of which waited for: 5 -> 4; matrix products, arithmetic and copies ran while one was open for 3% -> 3% of each run, Pallas kernels for 11% -> 4%
where the time goes in v6:
time: 65.3 us; the launch traced here: 64.7 us
  starting transfers between devices  32.8 us (50%)
  waiting for transfers between devices  12.3 us (19%)
  Pallas kernels  7.89 us (12%)
  blocking collectives  7.3 us (11%)
  other arithmetic  2.78 us (4%)
  local copies, waits for them, and re-layouts  1.58 us (2%)
    all_to_all x2, starting transfers between devices, along_line(): lax.all_to_all(blocks, 'y', 0, 0, tiled=True, axis_index_groups=[list(ORD...  16.3 us
    ppermute x4, starting transfers between devices, swapped(): return lax.ppermute(row, axes, pairs)  13 us
    pallas_call x6, Pallas kernels, call(): pl.pallas_call(kernel, out_shape=[jax.ShapeDtypeStruct(shape, kind) for s...  7.89 us
    all_to_all x2, waiting for transfers between devices, along_line(): lax.all_to_all(blocks, 'y', 0, 0, tiled=True, axis_index_groups=[list(ORD...  7.87 us
    ppermute x4, waiting for transfers between devices, swapped(): return lax.ppermute(row, axes, pairs)  4.38 us
    ppermute x1, starting transfers between devices, local(): other = lax.ppermute(conv_first, 'y', [(i, i ^ 1) for i in range(LINE)])  3.49 us
    all_gather x1, blocking collectives, local(): own = lax.all_gather(conv_first, 'core', axis=1, tiled=True)  2.72 us
    all_gather x1, blocking collectives, local(): other = lax.all_gather(other, 'core', axis=1, tiled=True)  2.51 us
  transfers between devices with their start and end apart: 7, of which 4 were waited for; matrix products, arithmetic and copies ran while one was open for 3% of the time, Pallas kernels for 4%

profile of v6, /device:TPU:198, one launch (start us, length us, event | category | flops | bytes accessed | tf_op | source)
XLA Modules:
  0.0 64.7 jit_solution(5442197155069227552)
XLA Ops:
  0.0 0.8 %fusion.1 = (bf16[2,16,384]{2,1,0:T(8,128)(2,1)S(1)}, bf16[2,16,384]{2,1,0:T(8,128)(2,1)S(1)}) fusion(pred[]{:T(512)S(6)} %eq.3, bf16[2,4,16,384]{3,2,1,0:T(8,128)(2,1)} %lat_ref.3), kind=kLoop, calls=%fused_computation.4 | loop fusion | flops 24576 | bytes 98305 | tf_op jit(solution)/shard_map/jit(_where)/select_n | solution.py:257
  0.8 3.5 %collective-permute-start.2 = (bf16[27,24,384]{2,1,0:T(8,128)(2,1)}, bf16[27,24,384]{2,1,0:T(8,128)(2,1)S(1)}, u32[]{:S(2)}, u32[]{:S(2)}) collective-permute-start(bf16[27,24,384]{2,1,0:T(8,128)(2,1)} %param.8), channel_id=1, source_target_pairs={{0,64},{64,0},{128,192},{192,128},{256,320},{320,256},{384,448},{4... | collective-permute-start | bytes 1493000 | tf_op jit(solution)/shard_map/ppermute | solution.py:260
  4.3 5.4 %collective-permute-start = (bf16[2,16,384]{2,1,0:T(8,128)(2,1)S(1)}, bf16[2,16,384]{2,1,0:T(8,128)(2,1)S(1)}, u32[]{:S(2)}, u32[]{:S(2)}) collective-permute-start(bf16[2,16,384]{2,1,0:T(8,128)(2,1)S(1)} %get-tuple-element.17), channel_id=1, source_target_pairs={{1,2},{2,1},{3,4},{4,3},{5,6},{6,5},{7,8},{8,7},{9,10},{10,9},{11,... | collective-permute-start | bytes 73736 | tf_op jit(solution)/shard_map/ppermute | solution.py:235
  9.7 1.9 %collective-permute-start.1 = (bf16[2,16,384]{2,1,0:T(8,128)(2,1)S(1)}, bf16[2,16,384]{2,1,0:T(8,128)(2,1)S(1)}, u32[]{:S(2)}, u32[]{:S(2)}) collective-permute-start(bf16[2,16,384]{2,1,0:T(8,128)(2,1)S(1)} %get-tuple-element.18), channel_id=1, source_target_pairs={{0,1},{1,0},{2,3},{3,2},{4,5},{5,4},{6,7},{7,6},{8,9},{9,8},{10,11... | collective-permute-start | bytes 73736 | tf_op jit(solution)/shard_map/ppermute | solution.py:235
  11.6 0.0 copy-start
  11.6 0.9 %copy-done = bf16[2,4,16,384]{3,2,1,0:T(8,128)(2,1)S(1)} copy-done((bf16[2,4,16,384]{3,2,1,0:T(8,128)(2,1)S(1)}, bf16[2,4,16,384]{3,2,1,0:T(8,128)(2,1)}, u32[]{:S(2)}) %copy-start) | copy-done | bytes 98328
  12.5 0.7 %copy-done.2 = f32[384]{0:T(512)S(1)} copy-done((f32[384]{0:T(512)S(1)}, f32[384]{0:T(512)}, u32[]{:S(2)}) %copy-start.2) | copy-done | bytes 1560
  13.2 0.2 shard_map.64.own_ref
  13.3 0.0 collective-permute-done.far_ref
  13.4 2.0 %collective-permute-done.1.near_ref = bf16[2,16,384]{2,1,0:T(8,128)(2,1)S(1)} collective-permute-done((bf16[2,16,384]{2,1,0:T(8,128)(2,1)S(1)}, bf16[2,16,384]{2,1,0:T(8,128)(2,1)S(1)}, u32[]{:S(2)}, u32[]{:S(2)}) %collective-permute-start.1) | collective-permute-done | bytes 24608 | tf_op jit(solution)/shard_map/ppermute | solution.py:235
  15.4 0.9 %shard_map.65 = bf16[8,96,128]{2,1,0:T(8,128)(2,1)} custom-call(bf16[2,16,384]{2,1,0:T(8,128)(2,1)S(1)} %collective-permute-done.far_ref, bf16[2,16,384]{2,1,0:T(8,128)(2,1)S(1)} %collective-permute-done.1.near_ref, f32[128,384]{1,0:T(8,128)S(1)} %shard_map.64.own_ref, f32[384]{0:T(512)S(1)} %copy-done.2), custom_call_target="tpu_custom_call" | custom-call | tf_op jit(solution)/shard_map/pallas_call | solution.py:244
  16.3 8.2 %all-to-all-start = ((bf16[8,96,128]{2,1,0:T(8,128)(2,1)}), bf16[8,96,128]{2,1,0:T(8,128)(2,1)S(1)}, u32[]{:S(2)}, u32[]{:S(2)}) async-start(bf16[8,96,128]{2,1,0:T(8,128)(2,1)} %shard_map.65), calls=%async_computation | async-start | bytes 393216 | tf_op jit(solution)/shard_map/all_to_all | solution.py:239
  24.6 2.7 %all_gather.12.own_ref = bf16[27,48,384]{2,1,0:T(8,128)(2,1)S(1)} all-gather(bf16[27,24,384]{2,1,0:T(8,128)(2,1)} %param.8), channel_id=1, replica_groups=mesh['y'=8,'core'=2,'z'=8,'x'=4] {'core'}, dimensions={1}, use_global_device_ids=true | all-gather | bytes 1492992 | tf_op jit(solution)/shard_map/all_gather | solution.py:270
  27.3 0.0 collective-permute-done.2
  27.3 2.5 %all_gather.13.other_ref = bf16[27,48,384]{2,1,0:T(8,128)(2,1)S(1)} all-gather(bf16[27,24,384]{2,1,0:T(8,128)(2,1)S(1)} %collective-permute-done.2), channel_id=1, replica_groups=mesh['y'=8,'core'=2,'z'=8,'x'=4] {'core'}, dimensions={1}, use_global_device_ids=true | all-gather | bytes 1492992 | tf_op jit(solution)/shard_map/all_gather | solution.py:271
  29.8 0.0 all-to-all-done
  29.8 2.1 %all-gather = bf16[16,96,128]{2,1,0:T(8,128)(2,1)S(1)} all-gather(bf16[8,96,128]{2,1,0:T(8,128)(2,1)S(1)} %all-to-all-done), channel_id=2, replica_groups=mesh['y'=8,'core'=2,'z'=8,'x'=4] {'core'}, dimensions={0}, use_global_device_ids=true | all-gather | bytes 589824 | tf_op jit(solution)/shard_map/all_gather | solution.py:276
  31.9 3.8 %shard_map.66 = bf16[8,64,384]{2,1,0:T(8,128)(2,1)} custom-call(bf16[2,8,96,128]{3,2,1,0:T(8,128)(2,1)S(1)} %bitcast.17, bf16[27,48,384]{2,1,0:T(8,128)(2,1)S(1)} %all_gather.12.own_ref, bf16[27,48,384]{2,1,0:T(8,128)(2,1)S(1)} %all_gather.13.other_ref), custom_call_target="tpu_custom_call" | custom-call | tf_op jit(solution)/shard_map/pallas_call | solution.py:244
  35.7 8.1 %all-to-all-start.1 = ((bf16[8,64,384]{2,1,0:T(8,128)(2,1)}), bf16[8,64,384]{2,1,0:T(8,128)(2,1)S(1)}, u32[]{:S(2)}, u32[]{:S(2)}) async-start(bf16[8,64,384]{2,1,0:T(8,128)(2,1)} %shard_map.66), calls=%async_computation.1 | async-start | bytes 786432 | tf_op jit(solution)/shard_map/all_to_all | solution.py:239
  43.8 2.0 %pad_maximum_fusion.later_ref.weight_ref = bf16[9,384,384]{2,1,0:T(8,128)(2,1)S(1)} fusion(bf16[9,192,384]{2,1,0:T(8,128)(2,1)} %bitcast.18), kind=kLoop, calls=%fused_computation | loop fusion | flops 5308416 | bytes 3981312 | tf_op jit(solution)/shard_map/concatenate | solution.py:273
  45.8 7.9 %all-to-all-done.1.part_ref = bf16[8,64,384]{2,1,0:T(8,128)(2,1)S(1)} async-done(((bf16[8,64,384]{2,1,0:T(8,128)(2,1)}), bf16[8,64,384]{2,1,0:T(8,128)(2,1)S(1)}, u32[]{:S(2)}, u32[]{:S(2)}) %all-to-all-start.1) | async-done | bytes 393248 | tf_op jit(solution)/shard_map/all_to_all | solution.py:239
  53.6 0.0 copy-done.1
  53.7 0.0 copy-done.3
  53.7 0.1 shard_map.67
  53.7 0.0 copy-start.4
  53.8 3.8 %collective-permute-start.3 = (bf16[2,16,384]{2,1,0:T(8,128)(2,1)S(1)}, bf16[2,16,384]{2,1,0:T(8,128)(2,1)S(1)}, u32[]{:S(2)}, u32[]{:S(2)}) collective-permute-start(bf16[2,16,384]{2,1,0:T(8,128)(2,1)S(1)} %get-tuple-element.26), channel_id=1, source_target_pairs={{1,2},{2,1},{3,4},{4,3},{5,6},{6,5},{7,8},{8,7},{9,10},{10,9},{11,... | collective-permute-start | bytes 73736 | tf_op jit(solution)/shard_map/ppermute | solution.py:235
  57.5 1.9 %collective-permute-start.4 = (bf16[2,16,384]{2,1,0:T(8,128)(2,1)S(1)}, bf16[2,16,384]{2,1,0:T(8,128)(2,1)S(1)}, u32[]{:S(2)}, u32[]{:S(2)}) collective-permute-start(bf16[2,16,384]{2,1,0:T(8,128)(2,1)S(1)} %get-tuple-element.27), channel_id=1, source_target_pairs={{0,1},{1,0},{2,3},{3,2},{4,5},{5,4},{6,7},{7,6},{8,9},{9,8},{10,11... | collective-permute-start | bytes 73736 | tf_op jit(solution)/shard_map/ppermute | solution.py:235
  59.5 1.4 %shard_map.68.inner_ref = f32[16,16,1152]{2,1,0:T(8,128)S(1)} custom-call(bf16[2,4,16,384]{3,2,1,0:T(8,128)(2,1)S(1)} %get-tuple-element.28.block_ref, bf16[9,384,384]{2,1,0:T(8,128)(2,1)S(1)} %pad_maximum_fusion.later_ref.weight_ref), custom_call_target="tpu_custom_call" | custom-call | tf_op jit(solution)/shard_map/pallas_call | solution.py:244
  60.9 1.9 %collective-permute-done.3.far_ref = bf16[2,16,384]{2,1,0:T(8,128)(2,1)S(1)} collective-permute-done((bf16[2,16,384]{2,1,0:T(8,128)(2,1)S(1)}, bf16[2,16,384]{2,1,0:T(8,128)(2,1)S(1)}, u32[]{:S(2)}, u32[]{:S(2)}) %collective-permute-start.3) | collective-permute-done | bytes 24608 | tf_op jit(solution)/shard_map/ppermute | solution.py:235
  62.8 0.4 collective-permute-done.4.near_ref
  63.2 0.0 copy-done.4
  63.2 1.5 %shard_map.69 = bf16[16,6144]{1,0:T(8,128)(2,1)} custom-call(bf16[2,16,384]{2,1,0:T(8,128)(2,1)S(1)} %collective-permute-done.3.far_ref, bf16[2,16,384]{2,1,0:T(8,128)(2,1)S(1)} %collective-permute-done.4.near_ref, f32[16,16,1152]{2,1,0:T(8,128)S(1)} %shard_map.68.inner_ref, bf16[9,384,384]{2,1,0:T(8,128)(2,1)S(1)} %pad_maximum_fusion.later_ref.weight_ref, ...), custom_call_target="tpu_custom_call" | custom-call | tf_op jit(solution)/shard_map/pallas_call | solution.py:244
  (3 shorter events, 0.0 us)
Async XLA Ops:
  0.8 26.5 %collective-permute-start.2 = (bf16[27,24,384]{2,1,0:T(8,128)(2,1)}, bf16[27,24,384]{2,1,0:T(8,128)(2,1)S(1)}, u32[]{:S(2)}, u32[]{:S(2)}) collective-permute-start(bf16[27,24,384]{2,1,0:T(8,128)(2,1)} %param.8), channel_id=1, source_target_pairs={{0,64},{64,0},{128,192},{192,128},{256,320},{320,256},{384,448},{4... | collective-permute-start | bytes 1493000 | tf_op jit(solution)/shard_map/ppermute | solution.py:260
  4.3 9.1 %collective-permute-start = (bf16[2,16,384]{2,1,0:T(8,128)(2,1)S(1)}, bf16[2,16,384]{2,1,0:T(8,128)(2,1)S(1)}, u32[]{:S(2)}, u32[]{:S(2)}) collective-permute-start(bf16[2,16,384]{2,1,0:T(8,128)(2,1)S(1)} %get-tuple-element.17), channel_id=1, source_target_pairs={{1,2},{2,1},{3,4},{4,3},{5,6},{6,5},{7,8},{8,7},{9,10},{10,9},{11,... | collective-permute-start | bytes 73736 | tf_op jit(solution)/shard_map/ppermute | solution.py:235
  9.7 5.7 %collective-permute-start.1 = (bf16[2,16,384]{2,1,0:T(8,128)(2,1)S(1)}, bf16[2,16,384]{2,1,0:T(8,128)(2,1)S(1)}, u32[]{:S(2)}, u32[]{:S(2)}) collective-permute-start(bf16[2,16,384]{2,1,0:T(8,128)(2,1)S(1)} %get-tuple-element.18), channel_id=1, source_target_pairs={{0,1},{1,0},{2,3},{3,2},{4,5},{5,4},{6,7},{7,6},{8,9},{9,8},{10,11... | collective-permute-start | bytes 73736 | tf_op jit(solution)/shard_map/ppermute | solution.py:235
  11.6 0.9 %copy-start = (bf16[2,4,16,384]{3,2,1,0:T(8,128)(2,1)S(1)}, bf16[2,4,16,384]{3,2,1,0:T(8,128)(2,1)}, u32[]{:S(2)}) copy-start(bf16[2,4,16,384]{3,2,1,0:T(8,128)(2,1)} %lat_ref.3) | copy-start | bytes 294916
  12.5 0.7 %copy-start.2 = (f32[384]{0:T(512)S(1)}, f32[384]{0:T(512)}, u32[]{:S(2)}) copy-start(f32[384]{0:T(512)} %gain_ref.3) | copy-start | bytes 4612
  16.3 13.5 %all-to-all-start = ((bf16[8,96,128]{2,1,0:T(8,128)(2,1)}), bf16[8,96,128]{2,1,0:T(8,128)(2,1)S(1)}, u32[]{:S(2)}, u32[]{:S(2)}) async-start(bf16[8,96,128]{2,1,0:T(8,128)(2,1)} %shard_map.65), calls=%async_computation | async-start | bytes 393216 | tf_op jit(solution)/shard_map/all_to_all | solution.py:239
  35.7 18.0 %copy-start.1 = (bf16[2,4,16,384]{3,2,1,0:T(8,128)(2,1)S(1)}, bf16[2,4,16,384]{3,2,1,0:T(8,128)(2,1)}, u32[]{:S(2)}) copy-start(bf16[2,4,16,384]{3,2,1,0:T(8,128)(2,1)} %lat_ref.3) | copy-start | bytes 294916
  35.7 18.0 %copy-start.3 = (f32[384]{0:T(512)S(1)}, f32[384]{0:T(512)}, u32[]{:S(2)}) copy-start(f32[384]{0:T(512)} %bias_ref.2) | copy-start | bytes 4612
  35.7 18.0 %all-to-all-start.1 = ((bf16[8,64,384]{2,1,0:T(8,128)(2,1)}), bf16[8,64,384]{2,1,0:T(8,128)(2,1)S(1)}, u32[]{:S(2)}, u32[]{:S(2)}) async-start(bf16[8,64,384]{2,1,0:T(8,128)(2,1)} %shard_map.66), calls=%async_computation.1 | async-start | bytes 786432 | tf_op jit(solution)/shard_map/all_to_all | solution.py:239
  53.7 9.5 %copy-start.4 = (f32[192]{0:T(256)S(1)}, f32[192]{0:T(256)}, u32[]{:S(2)}) copy-start(f32[192]{0:T(256)} %bias_ref.3) | copy-start | bytes 2308
  53.8 9.0 %collective-permute-start.3 = (bf16[2,16,384]{2,1,0:T(8,128)(2,1)S(1)}, bf16[2,16,384]{2,1,0:T(8,128)(2,1)S(1)}, u32[]{:S(2)}, u32[]{:S(2)}) collective-permute-start(bf16[2,16,384]{2,1,0:T(8,128)(2,1)S(1)} %get-tuple-element.26), channel_id=1, source_target_pairs={{1,2},{2,1},{3,4},{4,3},{5,6},{6,5},{7,8},{8,7},{9,10},{10,9},{11,... | collective-permute-start | bytes 73736 | tf_op jit(solution)/shard_map/ppermute | solution.py:235
  57.5 5.7 %collective-permute-start.4 = (bf16[2,16,384]{2,1,0:T(8,128)(2,1)S(1)}, bf16[2,16,384]{2,1,0:T(8,128)(2,1)S(1)}, u32[]{:S(2)}, u32[]{:S(2)}) collective-permute-start(bf16[2,16,384]{2,1,0:T(8,128)(2,1)S(1)} %get-tuple-element.27), channel_id=1, source_target_pairs={{0,1},{1,0},{2,3},{3,2},{4,5},{5,4},{6,7},{7,6},{8,9},{9,8},{10,11... | collective-permute-start | bytes 73736 | tf_op jit(solution)/shard_map/ppermute | solution.py:235

commit v7 on v6

--- a/solution.py
+++ b/solution.py
@@ -15,7 +15,7 @@
 HALF = ROWS // 2
 CELLS = FRAMES * HALF * COLS
 SENT = FRAMES * ROWS * COLS
-ORDER = (4, 5, 6, 7, 0, 1, 2, 3)
+ORDER = (4, 6, 0, 2, 5, 7, 1, 3)
 SLOT = tuple(ORDER.index(y) for y in range(LINE))
 NT_DIMS = (((1,), (1,)), ((), ()))
 TN_DIMS = (((0,), (0,)), ((), ()))

time: 65.3 us -> 64.3 us (0.985)
  the two profiles are of different devices: /device:TPU:198 before, /device:TPU:256 now
where the time goes in v7:
time: 64.3 us; the launch traced here: 63.7 us
  starting transfers between devices  33.2 us (52%)
  waiting for transfers between devices  10.9 us (17%)
  Pallas kernels  7.89 us (12%)
  blocking collectives  7.3 us (11%)
  other arithmetic  2.78 us (4%)
  local copies, waits for them, and re-layouts  1.58 us (2%)
    all_to_all x2, starting transfers between devices, along_line(): lax.all_to_all(blocks, 'y', 0, 0, tiled=True, axis_index_groups=[list(ORD...  15.6 us
    ppermute x4, starting transfers between devices, swapped(): return lax.ppermute(row, axes, pairs)  14.1 us
    pallas_call x6, Pallas kernels, call(): pl.pallas_call(kernel, out_shape=[jax.ShapeDtypeStruct(shape, kind) for s...  7.89 us
    all_to_all x2, waiting for transfers between devices, along_line(): lax.all_to_all(blocks, 'y', 0, 0, tiled=True, axis_index_groups=[list(ORD...  7.61 us
    ppermute x1, starting transfers between devices, local(): other = lax.ppermute(conv_first, 'y', [(i, i ^ 1) for i in range(LINE)])  3.49 us
    ppermute x4, waiting for transfers between devices, swapped(): return lax.ppermute(row, axes, pairs)  3.26 us
    all_gather x1, blocking collectives, local(): own = lax.all_gather(conv_first, 'core', axis=1, tiled=True)  2.72 us
    all_gather x1, blocking collectives, local(): other = lax.all_gather(other, 'core', axis=1, tiled=True)  2.51 us
  transfers between devices with their start and end apart: 7, of which 5 were waited for; matrix products, arithmetic and copies ran while one was open for 3% of the time, Pallas kernels for 4%

profile of v7, /device:TPU:256, one launch (start us, length us, event | category | flops | bytes accessed | tf_op | source)
XLA Modules:
  0.0 63.7 jit_solution(6786323252246865172)
XLA Ops:
  0.0 0.8 %fusion.1 = (bf16[2,16,384]{2,1,0:T(8,128)(2,1)S(1)}, bf16[2,16,384]{2,1,0:T(8,128)(2,1)S(1)}) fusion(pred[]{:T(512)S(6)} %eq.3, bf16[2,4,16,384]{3,2,1,0:T(8,128)(2,1)} %lat_ref.3), kind=kLoop, calls=%fused_computation.4 | loop fusion | flops 24576 | bytes 98305 | tf_op jit(solution)/shard_map/jit(_where)/select_n | solution.py:257
  0.8 3.5 %collective-permute-start.2 = (bf16[27,24,384]{2,1,0:T(8,128)(2,1)}, bf16[27,24,384]{2,1,0:T(8,128)(2,1)S(1)}, u32[]{:S(2)}, u32[]{:S(2)}) collective-permute-start(bf16[27,24,384]{2,1,0:T(8,128)(2,1)} %param.8), channel_id=1, source_target_pairs={{0,64},{64,0},{128,192},{192,128},{256,320},{320,256},{384,448},{4... | collective-permute-start | bytes 1493000 | tf_op jit(solution)/shard_map/ppermute | solution.py:260
  4.3 3.8 %collective-permute-start = (bf16[2,16,384]{2,1,0:T(8,128)(2,1)S(1)}, bf16[2,16,384]{2,1,0:T(8,128)(2,1)S(1)}, u32[]{:S(2)}, u32[]{:S(2)}) collective-permute-start(bf16[2,16,384]{2,1,0:T(8,128)(2,1)S(1)} %get-tuple-element.17), channel_id=1, source_target_pairs={{1,2},{2,1},{3,4},{4,3},{5,6},{6,5},{7,8},{8,7},{9,10},{10,9},{11,... | collective-permute-start | bytes 73736 | tf_op jit(solution)/shard_map/ppermute | solution.py:235
  8.0 3.0 %collective-permute-start.1 = (bf16[2,16,384]{2,1,0:T(8,128)(2,1)S(1)}, bf16[2,16,384]{2,1,0:T(8,128)(2,1)S(1)}, u32[]{:S(2)}, u32[]{:S(2)}) collective-permute-start(bf16[2,16,384]{2,1,0:T(8,128)(2,1)S(1)} %get-tuple-element.18), channel_id=1, source_target_pairs={{0,1},{1,0},{2,3},{3,2},{4,5},{5,4},{6,7},{7,6},{8,9},{9,8},{10,11... | collective-permute-start | bytes 73736 | tf_op jit(solution)/shard_map/ppermute | solution.py:235
  11.1 0.0 copy-start
  11.1 0.9 %copy-done = bf16[2,4,16,384]{3,2,1,0:T(8,128)(2,1)S(1)} copy-done((bf16[2,4,16,384]{3,2,1,0:T(8,128)(2,1)S(1)}, bf16[2,4,16,384]{3,2,1,0:T(8,128)(2,1)}, u32[]{:S(2)}) %copy-start) | copy-done | bytes 98328
  12.0 0.7 %copy-done.2 = f32[384]{0:T(512)S(1)} copy-done((f32[384]{0:T(512)S(1)}, f32[384]{0:T(512)}, u32[]{:S(2)}) %copy-start.2) | copy-done | bytes 1560
  12.7 0.2 shard_map.64.own_ref
  12.8 0.5 collective-permute-done.far_ref
  13.3 0.4 collective-permute-done.1.near_ref
  13.7 0.9 %shard_map.65 = bf16[8,96,128]{2,1,0:T(8,128)(2,1)} custom-call(bf16[2,16,384]{2,1,0:T(8,128)(2,1)S(1)} %collective-permute-done.far_ref, bf16[2,16,384]{2,1,0:T(8,128)(2,1)S(1)} %collective-permute-done.1.near_ref, f32[128,384]{1,0:T(8,128)S(1)} %shard_map.64.own_ref, f32[384]{0:T(512)S(1)} %copy-done.2), custom_call_target="tpu_custom_call" | custom-call | tf_op jit(solution)/shard_map/pallas_call | solution.py:244
  14.7 8.2 %all-to-all-start = ((bf16[8,96,128]{2,1,0:T(8,128)(2,1)}), bf16[8,96,128]{2,1,0:T(8,128)(2,1)S(1)}, u32[]{:S(2)}, u32[]{:S(2)}) async-start(bf16[8,96,128]{2,1,0:T(8,128)(2,1)} %shard_map.65), calls=%async_computation | async-start | bytes 393216 | tf_op jit(solution)/shard_map/all_to_all | solution.py:239
  22.9 2.7 %all_gather.12.own_ref = bf16[27,48,384]{2,1,0:T(8,128)(2,1)S(1)} all-gather(bf16[27,24,384]{2,1,0:T(8,128)(2,1)} %param.8), channel_id=1, replica_groups=mesh['y'=8,'core'=2,'z'=8,'x'=4] {'core'}, dimensions={1}, use_global_device_ids=true | all-gather | bytes 1492992 | tf_op jit(solution)/shard_map/all_gather | solution.py:270
  25.6 0.0 collective-permute-done.2
  25.6 2.5 %all_gather.13.other_ref = bf16[27,48,384]{2,1,0:T(8,128)(2,1)S(1)} all-gather(bf16[27,24,384]{2,1,0:T(8,128)(2,1)S(1)} %collective-permute-done.2), channel_id=1, replica_groups=mesh['y'=8,'core'=2,'z'=8,'x'=4] {'core'}, dimensions={1}, use_global_device_ids=true | all-gather | bytes 1492992 | tf_op jit(solution)/shard_map/all_gather | solution.py:271
  28.1 0.0 all-to-all-done
  28.1 2.1 %all-gather = bf16[16,96,128]{2,1,0:T(8,128)(2,1)S(1)} all-gather(bf16[8,96,128]{2,1,0:T(8,128)(2,1)S(1)} %all-to-all-done), channel_id=2, replica_groups=mesh['y'=8,'core'=2,'z'=8,'x'=4] {'core'}, dimensions={0}, use_global_device_ids=true | all-gather | bytes 589824 | tf_op jit(solution)/shard_map/all_gather | solution.py:276
  30.2 3.8 %shard_map.66 = bf16[8,64,384]{2,1,0:T(8,128)(2,1)} custom-call(bf16[2,8,96,128]{3,2,1,0:T(8,128)(2,1)S(1)} %bitcast.17, bf16[27,48,384]{2,1,0:T(8,128)(2,1)S(1)} %all_gather.12.own_ref, bf16[27,48,384]{2,1,0:T(8,128)(2,1)S(1)} %all_gather.13.other_ref), custom_call_target="tpu_custom_call" | custom-call | tf_op jit(solution)/shard_map/pallas_call | solution.py:244
  34.0 7.3 %all-to-all-start.1 = ((bf16[8,64,384]{2,1,0:T(8,128)(2,1)}), bf16[8,64,384]{2,1,0:T(8,128)(2,1)S(1)}, u32[]{:S(2)}, u32[]{:S(2)}) async-start(bf16[8,64,384]{2,1,0:T(8,128)(2,1)} %shard_map.66), calls=%async_computation.1 | async-start | bytes 786432 | tf_op jit(solution)/shard_map/all_to_all | solution.py:239
  41.4 2.0 %pad_maximum_fusion.later_ref.weight_ref = bf16[9,384,384]{2,1,0:T(8,128)(2,1)S(1)} fusion(bf16[9,192,384]{2,1,0:T(8,128)(2,1)} %bitcast.18), kind=kLoop, calls=%fused_computation | loop fusion | flops 5308416 | bytes 3981312 | tf_op jit(solution)/shard_map/concatenate | solution.py:273
  43.4 7.6 %all-to-all-done.1.part_ref = bf16[8,64,384]{2,1,0:T(8,128)(2,1)S(1)} async-done(((bf16[8,64,384]{2,1,0:T(8,128)(2,1)}), bf16[8,64,384]{2,1,0:T(8,128)(2,1)S(1)}, u32[]{:S(2)}, u32[]{:S(2)}) %all-to-all-start.1) | async-done | bytes 393248 | tf_op jit(solution)/shard_map/all_to_all | solution.py:239
  51.0 0.0 copy-done.1
  51.0 0.0 copy-done.3
  51.0 0.1 shard_map.67
  51.1 0.0 copy-start.4
  51.1 5.4 %collective-permute-start.3 = (bf16[2,16,384]{2,1,0:T(8,128)(2,1)S(1)}, bf16[2,16,384]{2,1,0:T(8,128)(2,1)S(1)}, u32[]{:S(2)}, u32[]{:S(2)}) collective-permute-start(bf16[2,16,384]{2,1,0:T(8,128)(2,1)S(1)} %get-tuple-element.26), channel_id=1, source_target_pairs={{1,2},{2,1},{3,4},{4,3},{5,6},{6,5},{7,8},{8,7},{9,10},{10,9},{11,... | collective-permute-start | bytes 73736 | tf_op jit(solution)/shard_map/ppermute | solution.py:235
  56.5 1.9 %collective-permute-start.4 = (bf16[2,16,384]{2,1,0:T(8,128)(2,1)S(1)}, bf16[2,16,384]{2,1,0:T(8,128)(2,1)S(1)}, u32[]{:S(2)}, u32[]{:S(2)}) collective-permute-start(bf16[2,16,384]{2,1,0:T(8,128)(2,1)S(1)} %get-tuple-element.27), channel_id=1, source_target_pairs={{0,1},{1,0},{2,3},{3,2},{4,5},{5,4},{6,7},{7,6},{8,9},{9,8},{10,11... | collective-permute-start | bytes 73736 | tf_op jit(solution)/shard_map/ppermute | solution.py:235
  58.5 1.4 %shard_map.68.inner_ref = f32[16,16,1152]{2,1,0:T(8,128)S(1)} custom-call(bf16[2,4,16,384]{3,2,1,0:T(8,128)(2,1)S(1)} %get-tuple-element.28.block_ref, bf16[9,384,384]{2,1,0:T(8,128)(2,1)S(1)} %pad_maximum_fusion.later_ref.weight_ref), custom_call_target="tpu_custom_call" | custom-call | tf_op jit(solution)/shard_map/pallas_call | solution.py:244
  59.9 0.2 collective-permute-done.3.far_ref
  60.1 2.1 %collective-permute-done.4.near_ref = bf16[2,16,384]{2,1,0:T(8,128)(2,1)S(1)} collective-permute-done((bf16[2,16,384]{2,1,0:T(8,128)(2,1)S(1)}, bf16[2,16,384]{2,1,0:T(8,128)(2,1)S(1)}, u32[]{:S(2)}, u32[]{:S(2)}) %collective-permute-start.4) | collective-permute-done | bytes 24608 | tf_op jit(solution)/shard_map/ppermute | solution.py:235
  62.3 0.0 copy-done.4
  62.3 1.5 %shard_map.69 = bf16[16,6144]{1,0:T(8,128)(2,1)} custom-call(bf16[2,16,384]{2,1,0:T(8,128)(2,1)S(1)} %collective-permute-done.3.far_ref, bf16[2,16,384]{2,1,0:T(8,128)(2,1)S(1)} %collective-permute-done.4.near_ref, f32[16,16,1152]{2,1,0:T(8,128)S(1)} %shard_map.68.inner_ref, bf16[9,384,384]{2,1,0:T(8,128)(2,1)S(1)} %pad_maximum_fusion.later_ref.weight_ref, ...), custom_call_target="tpu_custom_call" | custom-call | tf_op jit(solution)/shard_map/pallas_call | solution.py:244
  (3 shorter events, 0.0 us)
Async XLA Ops:
  0.8 24.9 %collective-permute-start.2 = (bf16[27,24,384]{2,1,0:T(8,128)(2,1)}, bf16[27,24,384]{2,1,0:T(8,128)(2,1)S(1)}, u32[]{:S(2)}, u32[]{:S(2)}) collective-permute-start(bf16[27,24,384]{2,1,0:T(8,128)(2,1)} %param.8), channel_id=1, source_target_pairs={{0,64},{64,0},{128,192},{192,128},{256,320},{320,256},{384,448},{4... | collective-permute-start | bytes 1493000 | tf_op jit(solution)/shard_map/ppermute | solution.py:260
  4.3 9.0 %collective-permute-start = (bf16[2,16,384]{2,1,0:T(8,128)(2,1)S(1)}, bf16[2,16,384]{2,1,0:T(8,128)(2,1)S(1)}, u32[]{:S(2)}, u32[]{:S(2)}) collective-permute-start(bf16[2,16,384]{2,1,0:T(8,128)(2,1)S(1)} %get-tuple-element.17), channel_id=1, source_target_pairs={{1,2},{2,1},{3,4},{4,3},{5,6},{6,5},{7,8},{8,7},{9,10},{10,9},{11,... | collective-permute-start | bytes 73736 | tf_op jit(solution)/shard_map/ppermute | solution.py:235
  8.0 5.7 %collective-permute-start.1 = (bf16[2,16,384]{2,1,0:T(8,128)(2,1)S(1)}, bf16[2,16,384]{2,1,0:T(8,128)(2,1)S(1)}, u32[]{:S(2)}, u32[]{:S(2)}) collective-permute-start(bf16[2,16,384]{2,1,0:T(8,128)(2,1)S(1)} %get-tuple-element.18), channel_id=1, source_target_pairs={{0,1},{1,0},{2,3},{3,2},{4,5},{5,4},{6,7},{7,6},{8,9},{9,8},{10,11... | collective-permute-start | bytes 73736 | tf_op jit(solution)/shard_map/ppermute | solution.py:235
  11.1 0.9 %copy-start = (bf16[2,4,16,384]{3,2,1,0:T(8,128)(2,1)S(1)}, bf16[2,4,16,384]{3,2,1,0:T(8,128)(2,1)}, u32[]{:S(2)}) copy-start(bf16[2,4,16,384]{3,2,1,0:T(8,128)(2,1)} %lat_ref.3) | copy-start | bytes 294916
  12.0 0.7 %copy-start.2 = (f32[384]{0:T(512)S(1)}, f32[384]{0:T(512)}, u32[]{:S(2)}) copy-start(f32[384]{0:T(512)} %gain_ref.3) | copy-start | bytes 4612
  14.7 13.5 %all-to-all-start = ((bf16[8,96,128]{2,1,0:T(8,128)(2,1)}), bf16[8,96,128]{2,1,0:T(8,128)(2,1)S(1)}, u32[]{:S(2)}, u32[]{:S(2)}) async-start(bf16[8,96,128]{2,1,0:T(8,128)(2,1)} %shard_map.65), calls=%async_computation | async-start | bytes 393216 | tf_op jit(solution)/shard_map/all_to_all | solution.py:239
  34.0 17.0 %copy-start.1 = (bf16[2,4,16,384]{3,2,1,0:T(8,128)(2,1)S(1)}, bf16[2,4,16,384]{3,2,1,0:T(8,128)(2,1)}, u32[]{:S(2)}) copy-start(bf16[2,4,16,384]{3,2,1,0:T(8,128)(2,1)} %lat_ref.3) | copy-start | bytes 294916
  34.0 17.0 %copy-start.3 = (f32[384]{0:T(512)S(1)}, f32[384]{0:T(512)}, u32[]{:S(2)}) copy-start(f32[384]{0:T(512)} %bias_ref.2) | copy-start | bytes 4612
  34.0 17.0 %all-to-all-start.1 = ((bf16[8,64,384]{2,1,0:T(8,128)(2,1)}), bf16[8,64,384]{2,1,0:T(8,128)(2,1)S(1)}, u32[]{:S(2)}, u32[]{:S(2)}) async-start(bf16[8,64,384]{2,1,0:T(8,128)(2,1)} %shard_map.66), calls=%async_computation.1 | async-start | bytes 786432 | tf_op jit(solution)/shard_map/all_to_all | solution.py:239
  51.1 11.2 %copy-start.4 = (f32[192]{0:T(256)S(1)}, f32[192]{0:T(256)}, u32[]{:S(2)}) copy-start(f32[192]{0:T(256)} %bias_ref.3) | copy-start | bytes 2308
  51.1 9.0 %collective-permute-start.3 = (bf16[2,16,384]{2,1,0:T(8,128)(2,1)S(1)}, bf16[2,16,384]{2,1,0:T(8,128)(2,1)S(1)}, u32[]{:S(2)}, u32[]{:S(2)}) collective-permute-start(bf16[2,16,384]{2,1,0:T(8,128)(2,1)S(1)} %get-tuple-element.26), channel_id=1, source_target_pairs={{1,2},{2,1},{3,4},{4,3},{5,6},{6,5},{7,8},{8,7},{9,10},{10,9},{11,... | collective-permute-start | bytes 73736 | tf_op jit(solution)/shard_map/ppermute | solution.py:235
  56.5 5.7 %collective-permute-start.4 = (bf16[2,16,384]{2,1,0:T(8,128)(2,1)S(1)}, bf16[2,16,384]{2,1,0:T(8,128)(2,1)S(1)}, u32[]{:S(2)}, u32[]{:S(2)}) collective-permute-start(bf16[2,16,384]{2,1,0:T(8,128)(2,1)S(1)} %get-tuple-element.27), channel_id=1, source_target_pairs={{0,1},{1,0},{2,3},{3,2},{4,5},{5,4},{6,7},{7,6},{8,9},{9,8},{10,11... | collective-permute-start | bytes 73736 | tf_op jit(solution)/shard_map/ppermute | solution.py:235

commit v8 on v7

--- a/solution.py
+++ b/solution.py
@@ -166,7 +166,7 @@
         near_ref[...] = out_ref[:, ROWS - 1]
 
 
-def upper_inner_kernel(block_ref, weight_ref, out_ref):
+def upper_inner_kernel(block_ref, weight_ref, bias_ref, out_ref):
     rows = jnp.dot(
         row_picks(), block_ref[...].reshape(SENT, CHANS), preferred_element_type=F32
     ).astype(BF16)
@@ -180,10 +180,13 @@
             preferred_element_type=F32,
         )
         total = part if total is None else total + part
+    bias = bias_ref[...].reshape(1, OUTS)
+    zero = jnp.zeros((1, 2 * OUTS), F32)
+    total = total + jnp.concatenate([zero, bias, bias, zero], axis=1)
     out_ref[...] = total.reshape(out_ref.shape)
 
 
-def upper_kernel(far_ref, near_ref, inner_ref, weight_ref, bias_ref, out_ref):
+def upper_kernel(far_ref, near_ref, inner_ref, weight_ref, out_ref):
     wide = 2 * OUTS
     lines = FRAMES * 2 * ROWS
 
@@ -204,15 +207,13 @@
     line = lax.broadcasted_iota(jnp.int32, (lines, 3 * wide), 0)
     totals = []
     for c in range(COLS):
-        total = inner_ref[c]
+        beside = 0.0
         for f in range(FRAMES):
             row = f * COLS + c
             top, bottom = f * 2 * ROWS, (f + 1) * 2 * ROWS - 1
-            total = total + jnp.where(line == top, above[row : row + 1], 0.0)
-            total = total + jnp.where(line == bottom, below[row : row + 1], 0.0)
-        totals.append(total)
-    bias = bias_ref[...].reshape(1, OUTS)
-    bias = jnp.concatenate([bias, bias], axis=1)
+            beside = jnp.where(line == top, above[row : row + 1], beside)
+            beside = jnp.where(line == bottom, below[row : row + 1], beside)
+        totals.append(inner_ref[c] + beside)
     left = lax.broadcasted_iota(jnp.int32, (lines, wide), 1) < OUTS
     zero = jnp.zeros((lines, wide), F32)
     for c in range(COLS):
@@ -222,7 +223,6 @@
             jnp.where(left, first_before, totals[c][:, :wide])
             + totals[c][:, wide : 2 * wide]
             + jnp.where(left, totals[c][:, 2 * wide :], last_after)
-            + bias
         )
         out_ref[:, c * wide : (c + 1) * wide] = value.astype(BF16)
 
@@ -296,12 +296,12 @@
     (inner,) = call(
         upper_inner_kernel,
         [((COLS, FRAMES * 2 * ROWS, 6 * OUTS), F32)],
-        [(block, False), (upper, False)],
+        [(block, False), (upper, False), (bias_upper, False)],
     )
     (out,) = call(
         upper_kernel,
         [((FRAMES * 2 * ROWS, 2 * COLS * OUTS), BF16)],
-        [(array, False) for array in (far, near, inner, upper, bias_upper)],
+        [(array, False) for array in (far, near, inner, upper)],
     )
     return out.reshape(FRAMES, 2 * ROWS, 2 * COLS * OUTS)
 

time: 64.3 us -> 64.3 us (level)
  no operation moved by 1% of the time
where the time goes in v8:
time: 64.3 us; the launch traced here: 63.7 us
  starting transfers between devices  33.2 us (52%)
  waiting for transfers between devices  10.9 us (17%)
  Pallas kernels  7.87 us (12%)
  blocking collectives  7.3 us (11%)
  other arithmetic  2.78 us (4%)
  local copies, waits for them, and re-layouts  1.58 us (2%)
    all_to_all x2, starting transfers between devices, along_line(): lax.all_to_all(blocks, 'y', 0, 0, tiled=True, axis_index_groups=[list(ORD...  15.6 us
    ppermute x4, starting transfers between devices, swapped(): return lax.ppermute(row, axes, pairs)  14.1 us
    pallas_call x6, Pallas kernels, call(): pl.pallas_call(kernel, out_shape=[jax.ShapeDtypeStruct(shape, kind) for s...  7.87 us
    all_to_all x2, waiting for transfers between devices, along_line(): lax.all_to_all(blocks, 'y', 0, 0, tiled=True, axis_index_groups=[list(ORD...  7.61 us
    ppermute x1, starting transfers between devices, local(): other = lax.ppermute(conv_first, 'y', [(i, i ^ 1) for i in range(LINE)])  3.49 us
    ppermute x4, waiting for transfers between devices, swapped(): return lax.ppermute(row, axes, pairs)  3.26 us
    all_gather x1, blocking collectives, local(): own = lax.all_gather(conv_first, 'core', axis=1, tiled=True)  2.72 us
    all_gather x1, blocking collectives, local(): other = lax.all_gather(other, 'core', axis=1, tiled=True)  2.51 us
  transfers between devices with their start and end apart: 7, of which 5 were waited for; matrix products, arithmetic and copies ran while one was open for 3% of the time, Pallas kernels for 4%

profile of v8, /device:TPU:256, one launch (start us, length us, event | category | flops | bytes accessed | tf_op | source)
XLA Modules:
  0.0 63.7 jit_solution(17061486488973455459)
XLA Ops:
  0.0 0.8 %fusion.1 = (bf16[2,16,384]{2,1,0:T(8,128)(2,1)S(1)}, bf16[2,16,384]{2,1,0:T(8,128)(2,1)S(1)}) fusion(pred[]{:T(512)S(6)} %eq.3, bf16[2,4,16,384]{3,2,1,0:T(8,128)(2,1)} %lat_ref.3), kind=kLoop, calls=%fused_computation.4 | loop fusion | flops 24576 | bytes 98305 | tf_op jit(solution)/shard_map/jit(_where)/select_n | solution.py:257
  0.8 3.5 %collective-permute-start.2 = (bf16[27,24,384]{2,1,0:T(8,128)(2,1)}, bf16[27,24,384]{2,1,0:T(8,128)(2,1)S(1)}, u32[]{:S(2)}, u32[]{:S(2)}) collective-permute-start(bf16[27,24,384]{2,1,0:T(8,128)(2,1)} %param.8), channel_id=1, source_target_pairs={{0,64},{64,0},{128,192},{192,128},{256,320},{320,256},{384,448},{4... | collective-permute-start | bytes 1493000 | tf_op jit(solution)/shard_map/ppermute | solution.py:260
  4.3 3.8 %collective-permute-start = (bf16[2,16,384]{2,1,0:T(8,128)(2,1)S(1)}, bf16[2,16,384]{2,1,0:T(8,128)(2,1)S(1)}, u32[]{:S(2)}, u32[]{:S(2)}) collective-permute-start(bf16[2,16,384]{2,1,0:T(8,128)(2,1)S(1)} %get-tuple-element.17), channel_id=1, source_target_pairs={{1,2},{2,1},{3,4},{4,3},{5,6},{6,5},{7,8},{8,7},{9,10},{10,9},{11,... | collective-permute-start | bytes 73736 | tf_op jit(solution)/shard_map/ppermute | solution.py:235
  8.0 3.0 %collective-permute-start.1 = (bf16[2,16,384]{2,1,0:T(8,128)(2,1)S(1)}, bf16[2,16,384]{2,1,0:T(8,128)(2,1)S(1)}, u32[]{:S(2)}, u32[]{:S(2)}) collective-permute-start(bf16[2,16,384]{2,1,0:T(8,128)(2,1)S(1)} %get-tuple-element.18), channel_id=1, source_target_pairs={{0,1},{1,0},{2,3},{3,2},{4,5},{5,4},{6,7},{7,6},{8,9},{9,8},{10,11... | collective-permute-start | bytes 73736 | tf_op jit(solution)/shard_map/ppermute | solution.py:235
  11.1 0.0 copy-start
  11.1 0.9 %copy-done = bf16[2,4,16,384]{3,2,1,0:T(8,128)(2,1)S(1)} copy-done((bf16[2,4,16,384]{3,2,1,0:T(8,128)(2,1)S(1)}, bf16[2,4,16,384]{3,2,1,0:T(8,128)(2,1)}, u32[]{:S(2)}) %copy-start) | copy-done | bytes 98328
  12.0 0.0 copy-start.2
  12.0 0.7 %copy-done.2 = f32[384]{0:T(512)S(1)} copy-done((f32[384]{0:T(512)S(1)}, f32[384]{0:T(512)}, u32[]{:S(2)}) %copy-start.2) | copy-done | bytes 1560
  12.7 0.2 shard_map.64.own_ref
  12.8 0.5 collective-permute-done.far_ref
  13.3 0.4 collective-permute-done.1.near_ref
  13.7 0.9 %shard_map.65 = bf16[8,96,128]{2,1,0:T(8,128)(2,1)} custom-call(bf16[2,16,384]{2,1,0:T(8,128)(2,1)S(1)} %collective-permute-done.far_ref, bf16[2,16,384]{2,1,0:T(8,128)(2,1)S(1)} %collective-permute-done.1.near_ref, f32[128,384]{1,0:T(8,128)S(1)} %shard_map.64.own_ref, f32[384]{0:T(512)S(1)} %copy-done.2), custom_call_target="tpu_custom_call" | custom-call | tf_op jit(solution)/shard_map/pallas_call | solution.py:244
  14.7 8.2 %all-to-all-start = ((bf16[8,96,128]{2,1,0:T(8,128)(2,1)}), bf16[8,96,128]{2,1,0:T(8,128)(2,1)S(1)}, u32[]{:S(2)}, u32[]{:S(2)}) async-start(bf16[8,96,128]{2,1,0:T(8,128)(2,1)} %shard_map.65), calls=%async_computation | async-start | bytes 393216 | tf_op jit(solution)/shard_map/all_to_all | solution.py:239
  22.9 2.7 %all_gather.12.own_ref = bf16[27,48,384]{2,1,0:T(8,128)(2,1)S(1)} all-gather(bf16[27,24,384]{2,1,0:T(8,128)(2,1)} %param.8), channel_id=1, replica_groups=mesh['y'=8,'core'=2,'z'=8,'x'=4] {'core'}, dimensions={1}, use_global_device_ids=true | all-gather | bytes 1492992 | tf_op jit(solution)/shard_map/all_gather | solution.py:270
  25.6 0.0 collective-permute-done.2
  25.6 2.5 %all_gather.13.other_ref = bf16[27,48,384]{2,1,0:T(8,128)(2,1)S(1)} all-gather(bf16[27,24,384]{2,1,0:T(8,128)(2,1)S(1)} %collective-permute-done.2), channel_id=1, replica_groups=mesh['y'=8,'core'=2,'z'=8,'x'=4] {'core'}, dimensions={1}, use_global_device_ids=true | all-gather | bytes 1492992 | tf_op jit(solution)/shard_map/all_gather | solution.py:271
  28.1 0.0 all-to-all-done
  28.1 2.1 %all-gather = bf16[16,96,128]{2,1,0:T(8,128)(2,1)S(1)} all-gather(bf16[8,96,128]{2,1,0:T(8,128)(2,1)S(1)} %all-to-all-done), channel_id=2, replica_groups=mesh['y'=8,'core'=2,'z'=8,'x'=4] {'core'}, dimensions={0}, use_global_device_ids=true | all-gather | bytes 589824 | tf_op jit(solution)/shard_map/all_gather | solution.py:276
  30.2 3.8 %shard_map.66 = bf16[8,64,384]{2,1,0:T(8,128)(2,1)} custom-call(bf16[2,8,96,128]{3,2,1,0:T(8,128)(2,1)S(1)} %bitcast.17, bf16[27,48,384]{2,1,0:T(8,128)(2,1)S(1)} %all_gather.12.own_ref, bf16[27,48,384]{2,1,0:T(8,128)(2,1)S(1)} %all_gather.13.other_ref), custom_call_target="tpu_custom_call" | custom-call | tf_op jit(solution)/shard_map/pallas_call | solution.py:244
  34.0 7.3 %all-to-all-start.1 = ((bf16[8,64,384]{2,1,0:T(8,128)(2,1)}), bf16[8,64,384]{2,1,0:T(8,128)(2,1)S(1)}, u32[]{:S(2)}, u32[]{:S(2)}) async-start(bf16[8,64,384]{2,1,0:T(8,128)(2,1)} %shard_map.66), calls=%async_computation.1 | async-start | bytes 786432 | tf_op jit(solution)/shard_map/all_to_all | solution.py:239
  41.4 2.0 %pad_maximum_fusion.later_ref.weight_ref = bf16[9,384,384]{2,1,0:T(8,128)(2,1)S(1)} fusion(bf16[9,192,384]{2,1,0:T(8,128)(2,1)} %bitcast.18), kind=kLoop, calls=%fused_computation | loop fusion | flops 5308416 | bytes 3981312 | tf_op jit(solution)/shard_map/concatenate | solution.py:273
  43.4 7.6 %all-to-all-done.1.part_ref = bf16[8,64,384]{2,1,0:T(8,128)(2,1)S(1)} async-done(((bf16[8,64,384]{2,1,0:T(8,128)(2,1)}), bf16[8,64,384]{2,1,0:T(8,128)(2,1)S(1)}, u32[]{:S(2)}, u32[]{:S(2)}) %all-to-all-start.1) | async-done | bytes 393248 | tf_op jit(solution)/shard_map/all_to_all | solution.py:239
  51.0 0.0 copy-done.1
  51.0 0.0 copy-done.3
  51.0 0.1 shard_map.67
  51.1 5.4 %collective-permute-start.3 = (bf16[2,16,384]{2,1,0:T(8,128)(2,1)S(1)}, bf16[2,16,384]{2,1,0:T(8,128)(2,1)S(1)}, u32[]{:S(2)}, u32[]{:S(2)}) collective-permute-start(bf16[2,16,384]{2,1,0:T(8,128)(2,1)S(1)} %get-tuple-element.26), channel_id=1, source_target_pairs={{1,2},{2,1},{3,4},{4,3},{5,6},{6,5},{7,8},{8,7},{9,10},{10,9},{11,... | collective-permute-start | bytes 73736 | tf_op jit(solution)/shard_map/ppermute | solution.py:235
  56.5 1.9 %collective-permute-start.4 = (bf16[2,16,384]{2,1,0:T(8,128)(2,1)S(1)}, bf16[2,16,384]{2,1,0:T(8,128)(2,1)S(1)}, u32[]{:S(2)}, u32[]{:S(2)}) collective-permute-start(bf16[2,16,384]{2,1,0:T(8,128)(2,1)S(1)} %get-tuple-element.27), channel_id=1, source_target_pairs={{0,1},{1,0},{2,3},{3,2},{4,5},{5,4},{6,7},{7,6},{8,9},{9,8},{10,11... | collective-permute-start | bytes 73736 | tf_op jit(solution)/shard_map/ppermute | solution.py:235
  58.4 0.0 copy-done.4
  58.5 1.4 %shard_map.68.inner_ref = f32[16,16,1152]{2,1,0:T(8,128)S(1)} custom-call(bf16[2,4,16,384]{3,2,1,0:T(8,128)(2,1)S(1)} %get-tuple-element.28.block_ref, bf16[9,384,384]{2,1,0:T(8,128)(2,1)S(1)} %pad_maximum_fusion.later_ref.weight_ref, f32[192]{0:T(256)S(1)} %copy-done.4), custom_call_target="tpu_custom_call" | custom-call | tf_op jit(solution)/shard_map/pallas_call | solution.py:244
  59.9 0.2 collective-permute-done.3.far_ref
  60.1 2.1 %collective-permute-done.4.near_ref = bf16[2,16,384]{2,1,0:T(8,128)(2,1)S(1)} collective-permute-done((bf16[2,16,384]{2,1,0:T(8,128)(2,1)S(1)}, bf16[2,16,384]{2,1,0:T(8,128)(2,1)S(1)}, u32[]{:S(2)}, u32[]{:S(2)}) %collective-permute-start.4) | collective-permute-done | bytes 24608 | tf_op jit(solution)/shard_map/ppermute | solution.py:235
  62.2 1.4 %shard_map.69 = bf16[16,6144]{1,0:T(8,128)(2,1)} custom-call(bf16[2,16,384]{2,1,0:T(8,128)(2,1)S(1)} %collective-permute-done.3.far_ref, bf16[2,16,384]{2,1,0:T(8,128)(2,1)S(1)} %collective-permute-done.4.near_ref, f32[16,16,1152]{2,1,0:T(8,128)S(1)} %shard_map.68.inner_ref, bf16[9,384,384]{2,1,0:T(8,128)(2,1)S(1)} %pad_maximum_fusion.later_ref.weight_ref), custom_call_target="tpu_custom_call" | custom-call | tf_op jit(solution)/shard_map/pallas_call | solution.py:244
  (3 shorter events, 0.0 us)
Async XLA Ops:
  0.8 24.9 %collective-permute-start.2 = (bf16[27,24,384]{2,1,0:T(8,128)(2,1)}, bf16[27,24,384]{2,1,0:T(8,128)(2,1)S(1)}, u32[]{:S(2)}, u32[]{:S(2)}) collective-permute-start(bf16[27,24,384]{2,1,0:T(8,128)(2,1)} %param.8), channel_id=1, source_target_pairs={{0,64},{64,0},{128,192},{192,128},{256,320},{320,256},{384,448},{4... | collective-permute-start | bytes 1493000 | tf_op jit(solution)/shard_map/ppermute | solution.py:260
  4.3 9.0 %collective-permute-start = (bf16[2,16,384]{2,1,0:T(8,128)(2,1)S(1)}, bf16[2,16,384]{2,1,0:T(8,128)(2,1)S(1)}, u32[]{:S(2)}, u32[]{:S(2)}) collective-permute-start(bf16[2,16,384]{2,1,0:T(8,128)(2,1)S(1)} %get-tuple-element.17), channel_id=1, source_target_pairs={{1,2},{2,1},{3,4},{4,3},{5,6},{6,5},{7,8},{8,7},{9,10},{10,9},{11,... | collective-permute-start | bytes 73736 | tf_op jit(solution)/shard_map/ppermute | solution.py:235
  8.0 5.7 %collective-permute-start.1 = (bf16[2,16,384]{2,1,0:T(8,128)(2,1)S(1)}, bf16[2,16,384]{2,1,0:T(8,128)(2,1)S(1)}, u32[]{:S(2)}, u32[]{:S(2)}) collective-permute-start(bf16[2,16,384]{2,1,0:T(8,128)(2,1)S(1)} %get-tuple-element.18), channel_id=1, source_target_pairs={{0,1},{1,0},{2,3},{3,2},{4,5},{5,4},{6,7},{7,6},{8,9},{9,8},{10,11... | collective-permute-start | bytes 73736 | tf_op jit(solution)/shard_map/ppermute | solution.py:235
  11.1 0.9 %copy-start = (bf16[2,4,16,384]{3,2,1,0:T(8,128)(2,1)S(1)}, bf16[2,4,16,384]{3,2,1,0:T(8,128)(2,1)}, u32[]{:S(2)}) copy-start(bf16[2,4,16,384]{3,2,1,0:T(8,128)(2,1)} %lat_ref.3) | copy-start | bytes 294916
  12.0 0.7 %copy-start.2 = (f32[384]{0:T(512)S(1)}, f32[384]{0:T(512)}, u32[]{:S(2)}) copy-start(f32[384]{0:T(512)} %gain_ref.3) | copy-start | bytes 4612
  14.7 13.5 %all-to-all-start = ((bf16[8,96,128]{2,1,0:T(8,128)(2,1)}), bf16[8,96,128]{2,1,0:T(8,128)(2,1)S(1)}, u32[]{:S(2)}, u32[]{:S(2)}) async-start(bf16[8,96,128]{2,1,0:T(8,128)(2,1)} %shard_map.65), calls=%async_computation | async-start | bytes 393216 | tf_op jit(solution)/shard_map/all_to_all | solution.py:239
  34.0 17.0 %copy-start.1 = (bf16[2,4,16,384]{3,2,1,0:T(8,128)(2,1)S(1)}, bf16[2,4,16,384]{3,2,1,0:T(8,128)(2,1)}, u32[]{:S(2)}) copy-start(bf16[2,4,16,384]{3,2,1,0:T(8,128)(2,1)} %lat_ref.3) | copy-start | bytes 294916
  34.0 17.0 %copy-start.3 = (f32[384]{0:T(512)S(1)}, f32[384]{0:T(512)}, u32[]{:S(2)}) copy-start(f32[384]{0:T(512)} %bias_ref.2) | copy-start | bytes 4612
  34.0 17.0 %all-to-all-start.1 = ((bf16[8,64,384]{2,1,0:T(8,128)(2,1)}), bf16[8,64,384]{2,1,0:T(8,128)(2,1)S(1)}, u32[]{:S(2)}, u32[]{:S(2)}) async-start(bf16[8,64,384]{2,1,0:T(8,128)(2,1)} %shard_map.66), calls=%async_computation.1 | async-start | bytes 786432 | tf_op jit(solution)/shard_map/all_to_all | solution.py:239
  41.4 17.1 %copy-start.4 = (f32[192]{0:T(256)S(1)}, f32[192]{0:T(256)}, u32[]{:S(2)}) copy-start(f32[192]{0:T(256)} %bias_ref.3) | copy-start | bytes 2308
  51.1 9.0 %collective-permute-start.3 = (bf16[2,16,384]{2,1,0:T(8,128)(2,1)S(1)}, bf16[2,16,384]{2,1,0:T(8,128)(2,1)S(1)}, u32[]{:S(2)}, u32[]{:S(2)}) collective-permute-start(bf16[2,16,384]{2,1,0:T(8,128)(2,1)S(1)} %get-tuple-element.26), channel_id=1, source_target_pairs={{1,2},{2,1},{3,4},{4,3},{5,6},{6,5},{7,8},{8,7},{9,10},{10,9},{11,... | collective-permute-start | bytes 73736 | tf_op jit(solution)/shard_map/ppermute | solution.py:235
  56.5 5.7 %collective-permute-start.4 = (bf16[2,16,384]{2,1,0:T(8,128)(2,1)S(1)}, bf16[2,16,384]{2,1,0:T(8,128)(2,1)S(1)}, u32[]{:S(2)}, u32[]{:S(2)}) collective-permute-start(bf16[2,16,384]{2,1,0:T(8,128)(2,1)S(1)} %get-tuple-element.27), channel_id=1, source_target_pairs={{0,1},{1,0},{2,3},{3,2},{4,5},{5,4},{6,7},{7,6},{8,9},{9,8},{10,11... | collective-permute-start | bytes 73736 | tf_op jit(solution)/shard_map/ppermute | solution.py:235
